TPU v7x, 512 devices: a whole 4x4x16 slice. The times are simulated.
512 devices in a mesh: dp: 16 (over z_lo, core), context: 8 (over z_hi, y), tensor: 4 (over x).
Axes of the slice: x: 4, y: 4, z: 16 (z_hi: 2, z_lo: 8; z = z_hi * 8 + z_lo), core: 2. Of those that a mesh axis runs over, the one named last changes fastest.
Arguments:
- latent: bfloat16 [16, 1024, 512], P('dp', 'context'), may hold values from -6 to 6
- key_rope: bfloat16 [16, 1024, 1024], P('dp', 'context', 'tensor'), may hold values from -6 to 6
- query: bfloat16 [16, 1024, 4096], P('dp', 'context', 'tensor'), may hold values from -600 to 600
- out_grad: bfloat16 [16, 1024, 4096], P('dp', 'context', 'tensor'), may hold values from -6 to 6
- positions: int32 [16, 1024], P('dp', 'context'), may hold values from 0 to 1023, as said below
- freq_index: int32 [32, 16], P('tensor'), may hold values from 0 to 63, all different within a row
- up_key: bfloat16 [512, 3072], P(('dp', 'context'), 'tensor'), may hold values from -0.25 to 0.25
- up_value: bfloat16 [512, 4096], P(('dp', 'context'), 'tensor'), may hold values from -0.25 to 0.25
Outputs:
- query_grad: bfloat16 [16, 1024, 4096], P('dp', 'context', 'tensor')
- key_rope_grad: bfloat16 [16, 1024, 1024], P('dp', 'context', 'tensor')
- latent_grad: bfloat16 [16, 1024, 512], P('dp', 'context')
- up_key_grad: bfloat16 [512, 3072], P(('dp', 'context'), 'tensor')
- up_value_grad: bfloat16 [512, 4096], P(('dp', 'context'), 'tensor')
Inputs may be any that keep to these rules, and one draw needn't show every extreme that they name: In each sequence every position 0 to 1023 appears once, in 16 runs of 64 consecutive increasing positions that start at multiples of 64; each device along context holds two runs, in any order. `freq_index`: each row names 16 different frequency pairs.
All inputs are finite; a program needn't handle non-finite values.
Results may differ from a plain program's by a relative error of at most 0.018.
Values may be sent and summed in bfloat16 or wider, within the bound.
No kernel may reach another device: no remote copies, remote signals or barrier semaphores. Data moves between devices by JAX's collectives and lax.ppermute only.
A program may use at most 64 MiB of HBM per device.

v0:
```python
import jax
import jax.numpy as jnp
from jax import lax
from jax.sharding import PartitionSpec as P

rope_base = 500000.0
neg_large = -1e30


def rope_tables(places, freq_index, head_dim):
    inverse = rope_base ** (-2.0 * freq_index.astype(jnp.float32) / head_dim)
    angles = places.astype(jnp.float32)[:, None, None] * inverse[None]
    return (jnp.cos(angles), jnp.sin(angles))


def rotate(values, cosine, sine_table):
    width = cosine.shape[-1]
    first = values[..., :width]
    second = values[..., width:]
    return jnp.concatenate(
        [first * cosine - second * sine_table, second * cosine + first * sine_table], -1
    )


def unrotate(values, cosine, sine_table):
    width = cosine.shape[-1]
    first = values[..., :width]
    second = values[..., width:]
    return jnp.concatenate(
        [first * cosine + second * sine_table, second * cosine - first * sine_table], -1
    )


def score_block(query_heads, key_heads, score_scale):
    return score_scale * jnp.einsum(
        "ihd,jhd->hij", query_heads, key_heads, preferred_element_type=jnp.float32
    )


def forward_block(carried, query_heads, query_places, key_heads, values, key_places, score_scale):
    running_max, denominator, accumulated = carried
    scores = score_block(query_heads, key_heads, score_scale)
    visible = key_places[None, :] <= query_places[:, None]
    masked = jnp.where(visible[None], scores, neg_large)
    new_max = jnp.maximum(running_max, jnp.max(masked, -1))
    weights = jnp.where(visible[None], jnp.exp(masked - new_max[..., None]), 0.0)
    factor = jnp.exp(running_max - new_max)
    denominator = jnp.sum(weights, -1)
    update = jnp.einsum(
        "hij,jhv->ihv", weights, values.astype(jnp.float32), precision=lax.Precision.HIGHEST
    )
    accumulated = accumulated * factor.T[:, :, None] + update
    return (new_max, denominator, accumulated)


def grads_block(
    query_heads,
    grad_out,
    log_total,
    row_delta,
    query_places,
    key_heads,
    values,
    key_places,
    score_scale,
):
    scores = score_block(query_heads, key_heads, score_scale)
    visible = key_places[None, :] <= query_places[:, None]
    shifted = jnp.where(visible[None], scores - log_total.T[:, :, None], neg_large)
    probs = jnp.exp(shifted).astype(jnp.bfloat16)
    dprob = jnp.einsum("ihv,jhv->hij", grad_out, values, preferred_element_type=jnp.float32)
    score_grad = (
        score_scale * probs.astype(jnp.float32) * (dprob - row_delta.T[:, :, None])
    ).astype(jnp.bfloat16)
    return (probs, score_grad)


def body(latent, key_rope, query, out_grad, positions, freq_index, up_key, up_value):
    tok_rows = latent.shape[1]
    head_count, pair_count = freq_index.shape
    rope_dims = 2 * pair_count
    head_dim = query.shape[2] // head_count
    nope_dims = head_dim - rope_dims
    value_dims = out_grad.shape[2] // head_count
    score_scale = head_dim ** (-0.5)
    latent_rows = latent[0]
    places = positions[0]
    w_key, w_value = (
        lax.all_gather(up_key, ("dp", "context"), axis=0, tiled=True),
        lax.all_gather(up_value, ("dp", "context"), axis=0, tiled=True),
    )
    all_places = lax.all_gather(places, "context", axis=0, tiled=True)
    cosine, sine_table = rope_tables(places, freq_index, head_dim)
    own_rot = rotate(
        key_rope[0].reshape(tok_rows, head_count, rope_dims).astype(jnp.float32), cosine, sine_table
    ).astype(jnp.bfloat16)
    query_split = query[0].reshape(tok_rows, head_count, head_dim)
    query_rot = rotate(query_split[..., :rope_dims].astype(jnp.float32), cosine, sine_table).astype(
        jnp.bfloat16
    )
    query_heads = jnp.concatenate([query_rot, query_split[..., rope_dims:]], -1)
    grad_out = out_grad[0].reshape(tok_rows, head_count, value_dims)
    own_nope_flat = jnp.dot(latent_rows, w_key, preferred_element_type=jnp.float32).astype(
        jnp.bfloat16
    )
    own_value_flat = jnp.dot(latent_rows, w_value, preferred_element_type=jnp.float32).astype(
        jnp.bfloat16
    )
    own_keys = jnp.concatenate(
        [own_rot, own_nope_flat.reshape(tok_rows, head_count, nope_dims)], -1
    )
    own_values = own_value_flat.reshape(tok_rows, head_count, value_dims)
    own_rot_flat = own_rot.reshape(tok_rows, head_count * rope_dims)

    def keys_from_latent(pieces):
        piece_latent, piece_rot = pieces
        piece_rows = piece_latent.shape[0]
        key_nope = jnp.dot(piece_latent, w_key, preferred_element_type=jnp.float32).astype(
            jnp.bfloat16
        )
        values = jnp.dot(piece_latent, w_value, preferred_element_type=jnp.float32).astype(
            jnp.bfloat16
        )
        key_heads = jnp.concatenate(
            [
                piece_rot.reshape(piece_rows, head_count, rope_dims),
                key_nope.reshape(piece_rows, head_count, nope_dims),
            ],
            -1,
        )
        return (key_heads, values.reshape(piece_rows, head_count, value_dims))

    start_state = (
        jnp.full((head_count, tok_rows), neg_large, jnp.float32),
        jnp.zeros((head_count, tok_rows), jnp.float32),
        jnp.zeros((tok_rows, head_count, value_dims), jnp.float32),
    )
    pieces = (
        lax.all_gather(latent_rows, "context", axis=0, tiled=True),
        lax.all_gather(own_rot_flat, "context", axis=0, tiled=True),
    )
    key_places = all_places
    key_heads, values = keys_from_latent(pieces)
    running_max, denominator, accumulated = forward_block(
        start_state, query_heads, places, key_heads, values, key_places, score_scale
    )
    log_total = (running_max + jnp.log(denominator)).T
    attn = accumulated / denominator.T[:, :, None]
    row_delta = jnp.sum(grad_out.astype(jnp.float32) * attn, -1)
    pieces = (
        lax.all_gather(latent_rows, "context", axis=0, tiled=True),
        lax.all_gather(own_rot_flat, "context", axis=0, tiled=True),
    )
    key_places = all_places
    key_heads, values = keys_from_latent(pieces)
    probs, score_grad = grads_block(
        query_heads,
        grad_out,
        log_total,
        row_delta,
        places,
        key_heads,
        values,
        key_places,
        score_scale,
    )
    grad_query_heads = jnp.einsum(
        "hij,jhd->ihd", score_grad, key_heads, preferred_element_type=jnp.float32
    )
    query_grad = jnp.concatenate(
        [
            unrotate(grad_query_heads[..., :rope_dims], cosine, sine_table),
            grad_query_heads[..., rope_dims:],
        ],
        -1,
    )
    query_grad = query_grad.astype(jnp.bfloat16).reshape(1, tok_rows, head_count * head_dim)
    all_totals, all_deltas = (
        lax.all_gather(log_total, "context", axis=0, tiled=True),
        lax.all_gather(row_delta, "context", axis=0, tiled=True),
    )
    query_joined = query_heads.reshape(tok_rows, head_count * head_dim)
    piece_query = lax.all_gather(query_joined, "context", axis=0, tiled=True)
    piece_grad = lax.all_gather(out_grad[0], "context", axis=0, tiled=True)
    piece_rows = piece_query.shape[0]
    piece_heads = piece_query.reshape(piece_rows, head_count, head_dim)
    piece_out = piece_grad.reshape(piece_rows, head_count, value_dims)
    probs, score_grad = grads_block(
        piece_heads,
        piece_out,
        all_totals,
        all_deltas,
        all_places,
        own_keys,
        own_values,
        places,
        score_scale,
    )
    key_part = jnp.einsum(
        "hij,ihd->jhd", score_grad, piece_heads, preferred_element_type=jnp.float32
    )
    carried_values = jnp.einsum(
        "hij,ihv->jhv", probs, piece_out, preferred_element_type=jnp.float32
    )
    key_rope_grad = (
        unrotate(key_part[..., :rope_dims], cosine, sine_table)
        .astype(jnp.bfloat16)
        .reshape(1, tok_rows, head_count * rope_dims)
    )
    key_nope_grad = (
        key_part[..., rope_dims:].astype(jnp.bfloat16).reshape(tok_rows, head_count * nope_dims)
    )
    values_grad = carried_values.astype(jnp.bfloat16).reshape(tok_rows, head_count * value_dims)
    partial_latent = jnp.dot(key_nope_grad, w_key.T, preferred_element_type=jnp.float32) + jnp.dot(
        values_grad, w_value.T, preferred_element_type=jnp.float32
    )
    latent_grad = lax.psum(partial_latent.astype(jnp.bfloat16), "tensor")[None]
    joined_grads = jnp.concatenate([key_nope_grad, values_grad], 1)
    summed = lax.psum_scatter(
        jnp.einsum("tr,tc->rc", latent_rows, joined_grads, preferred_element_type=jnp.float32),
        ("dp", "context"),
        scatter_dimension=0,
        tiled=True,
    )
    boundary = head_count * nope_dims
    up_key_grad = summed[:, :boundary].astype(jnp.bfloat16)
    up_value_grad = summed[:, boundary:].astype(jnp.bfloat16)
    return (query_grad, key_rope_grad, latent_grad, up_key_grad, up_value_grad)


def solution(mesh):
    placed = (
        P("dp", "context", None),
        P("dp", "context", "tensor"),
        P("dp", "context", "tensor"),
        P("dp", "context", "tensor"),
        P("dp", "context"),
        P("tensor", None),
        P(("dp", "context"), "tensor"),
        P(("dp", "context"), "tensor"),
    )
    return jax.shard_map(
        body,
        mesh=mesh,
        in_specs=placed,
        out_specs=(
            P("dp", "context", "tensor"),
            P("dp", "context", "tensor"),
            P("dp", "context", None),
            P(("dp", "context"), "tensor"),
            P(("dp", "context"), "tensor"),
        ),
        check_vma=False,
    )
```

profile of v0, /device:TPU:422, one launch (start us, length us, event | category | flops | bytes accessed | tf_op | source)
XLA Modules:
  0.0 1977.4 jit_solution(10392566731190841365)
XLA Ops:
  7.2 0.0 all-gather.12.cloned.1.call-start
  7.3 0.7 all-gather.12.cloned.1.call-update
  7.9 0.0 all-gather.16.cloned.1.call-start
  8.0 0.7 all-gather.16.cloned.1.call-update
  8.7 0.0 all-gather.10.cloned.1.call-start
  8.7 1.1 copy.152
  9.9 0.2 copy.183
  10.1 0.7 bitcast_convert_fusion
  10.7 0.7 multiply_power_fusion
  11.4 0.3 fusion.56
  11.8 0.2 copy.155
  12.0 0.2 copy.154
  12.1 0.3 pad_maximum_fusion.3
  12.4 0.8 copy.161
  13.3 0.0 all-gather.10.cloned.1.call-update
  13.3 0.0 all-gather.14.cloned.1.call-start
  13.3 0.8 copy.156
  14.2 0.0 all-gather.14.cloned.1.call-update
  14.2 0.0 all-reduce.4.cloned.1.call-start
  14.3 37.5 %all-gather.1 = s32[1,1024]{1,0:T(1,128)S(1)} all-gather(s32[1,128]{1,0:T(1,128)S(1)} %copy-done.14), channel_id=3, replica_groups=mesh['dp'=16,'context'=8,'tensor'=4] {'context'}, dimensions={1}, use_global_device_ids=true | all-gather | bytes 4608 | tf_op jit(solution)/shard_map/all_gather | solution.py:92
  51.8 0.1 broadcast_compare_fusion.1
  52.0 0.9 broadcast_compare_fusion
  52.8 537.7 %all-gather.3 = bf16[128,4,768]{2,1,0:T(4,128)(2,1)S(1)} all-gather(bf16[1,4,768]{2,1,0:T(4,128)(2,1)S(1)} %bitcast.131), channel_id=1, replica_groups=mesh['dp'=16,'context'=8,'tensor'=4] {'dp','context'}, dimensions={0}, use_global_device_ids=true | all-gather | bytes 792576 | tf_op jit(solution)/shard_map/all_gather | solution.py:89
  590.5 0.2 reshape.165
  590.7 0.1 copy.149
  590.9 0.3 fusion.53
  591.2 0.8 copy.163
  592.1 103.5 %all_gather.29 = bf16[1024,256]{0,1:T(8,128)(2,1)} all-gather(bf16[128,256]{0,1:T(8,128)(2,1)S(1)} %bitcast.122), channel_id=1, replica_groups=mesh['dp'=16,'context'=8,'tensor'=4] {'context'}, dimensions={0}, use_global_device_ids=true | all-gather | bytes 589824 | tf_op jit(solution)/shard_map/all_gather | solution.py:152
  695.6 1.9 copy.150
  697.5 0.9 convolution_convert_fusion.4
  698.5 1.7 copy.162
  700.2 1.8 copy.164
  702.0 1.3 dynamic-slice
  703.9 0.0 all-gather.12.cloned.1.call-done
  703.9 3.4 convolution_convert_fusion.1
  707.4 3.7 copy.151
  711.1 3.6 select_reduce_fusion
  714.7 1.9 copy-done
  716.6 1.3 fusion.3
  718.0 64.2 %all_gather.35 = f32[1024,8]{0,1:T(8,128)} all-gather(f32[128,8]{0,1:T(8,128)S(1)} %get-tuple-element.45), channel_id=1, replica_groups=mesh['dp'=16,'context'=8,'tensor'=4] {'context'}, dimensions={0}, use_global_device_ids=true | all-gather | bytes 36864 | tf_op jit(solution)/shard_map/all_gather | solution.py:179
  782.1 0.0 all-gather.16.cloned.1.call-done
  782.2 1.3 reshape.167
  783.6 2.7 convolution_convert_fusion
  786.3 3.2 fusion.22
  789.5 7.9 fusion.11
  797.5 1.7 slice.100
  799.2 64.6 %all_gather.37 = f32[1024,8]{0,1:T(8,128)} all-gather(f32[128,8]{0,1:T(8,128)S(1)} %fusion.22), channel_id=1, replica_groups=mesh['dp'=16,'context'=8,'tensor'=4] {'context'}, dimensions={0}, use_global_device_ids=true | all-gather | bytes 36864 | tf_op jit(solution)/shard_map/all_gather | solution.py:180
  863.8 1.0 fusion.15
  864.8 4.9 exponential_convert_fusion
  869.7 3.1 convolution_convert_fusion.2
  872.7 5.0 fusion.12
  877.7 1.3 fusion.64
  879.1 1.0 slice.99
  880.1 0.5 fusion.79
  880.6 2.4 convolution_bitcast_fusion
  883.0 1.1 fusion.17
  884.1 0.0 all-reduce.4.cloned.1.call-update
  884.1 1081.8 %all-reduce.5 = bf16[512,1792]{0,1:T(8,128)(2,1)S(1)} all-reduce(f32[512,1792]{0,1:T(8,128)} %convolution_bitcast_fusion), channel_id=5, replica_groups=mesh['dp'=16,'context'=8,'tensor'=4] {'dp','context'}, use_global_device_ids=true, to_apply=%region_4.5.clone | all-reduce | flops 917504 | bytes 5505024
  1965.9 0.2 dynamic-slice_convert_fusion
  1966.2 0.9 copy.170
  1967.1 0.7 copy.171
  1967.8 0.7 copy.172
  1968.5 0.7 copy.173
  1969.3 1.6 copy.193
  (45 shorter events, 0.2 us)
Async XLA Ops:
  7.2 7.1 copy-start.14
  7.2 6.2 copy-start.10
  7.2 45.6 %copy-start.13 = (bf16[4,768]{1,0:T(4,128)(2,1)S(1)}, bf16[4,768]{1,0:T(4,128)(2,1)}, u32[]{:S(2)}) copy-start(bf16[4,768]{1,0:T(4,128)(2,1)} %param.14) | copy-start | bytes 18436
  7.2 583.5 %copy-start.12 = (bf16[1,128,256]{2,1,0:T(8,128)(2,1)S(1)}, bf16[1,128,256]{2,1,0:T(8,128)(2,1)}, u32[]{:S(2)}) copy-start(bf16[1,128,256]{2,1,0:T(8,128)(2,1)} %param.9) | copy-start | bytes 196612
  7.2 696.7 %all-gather.12.cloned.1.call-start = ((), (), s32[]{:S(2)}) async-start(), calls=%async_computation.2 | async-start | bytes 1179648 | tf_op jit(solution)/shard_map/all_gather | solution.py:151
  7.9 774.2 %all-gather.16.cloned.1.call-start = ((), (), s32[]{:S(2)}) async-start(), calls=%async_computation.4 | async-start | bytes 1056768 | tf_op jit(solution)/shard_map/all_gather | solution.py:90
  8.7 856.1 %all-gather.10.cloned.1.call-start = ((), (), s32[]{:S(2)}) async-start(), calls=%async_computation | async-start | bytes 2359296 | tf_op jit(solution)/shard_map/all_gather | solution.py:183
  12.4 685.1 %copy-start.5 = (bf16[1,128,512]{2,1,0:T(8,128)(2,1)S(1)}, bf16[1,128,512]{2,1,0:T(8,128)(2,1)}, u32[]{:S(2)}) copy-start(bf16[1,128,512]{2,1,0:T(8,128)(2,1)} %param.8) | copy-start | bytes 393220
  13.3 856.4 %all-gather.14.cloned.1.call-start = ((), (), s32[]{:S(2)}) async-start(), calls=%async_computation.3 | async-start | bytes 2359296 | tf_op jit(solution)/shard_map/all_gather | solution.py:184
  14.2 1955.1 %all-reduce.4.cloned.1.call-start = ((), (), s32[]{:S(2)}) async-start(), calls=%async_computation.1 | async-start | bytes 262144 | tf_op jit(solution)/shard_map/psum | solution.py:217
  51.9 662.8 %copy-start.6 = (pred[128,1024]{1,0:T(8,128)(4,1)}, pred[128,1024]{1,0:T(8,128)(4,1)S(1)}, u32[]{:S(2)}) copy-start(pred[128,1024]{1,0:T(8,128)(4,1)S(1)} %broadcast_compare_fusion.1) | copy-start | bytes 393220
  590.7 116.6 %copy-start.2 = (bf16[512,768]{1,0:T(8,128)(2,1)}, bf16[512,768]{1,0:T(8,128)(2,1)S(1)}, u32[]{:S(2)}) copy-start(bf16[512,768]{1,0:T(8,128)(2,1)S(1)} %reshape.165) | copy-start | bytes 2359300
  714.7 1.9 copy-start
  783.5 2.7 copy-start.1
  783.5 2.7 copy-start.7
  783.5 2.7 copy-start.8
  786.2 3.3 copy-start.15
  789.5 75.3 %copy-start.11 = (pred[1024,128]{1,0:T(8,128)(4,1)S(1)}, pred[1024,128]{1,0:T(8,128)(4,1)}, u32[]{:S(2)}) copy-start(pred[1024,128]{1,0:T(8,128)(4,1)} %broadcast_compare_fusion) | copy-start | bytes 393220
  869.7 3.1 copy-start.4
  877.7 5.3 copy-start.3
  883.0 1083.1 %copy-start.9 = (bf16[128,8,96]{0,2,1:T(8,128)(2,1)S(1)}, bf16[128,8,96]{0,2,1:T(8,128)(2,1)}, u32[]{:S(2)}) copy-start(bf16[128,8,96]{0,2,1:T(8,128)(2,1)} %slice.100) | copy-start | bytes 589828
Sparse Core Ops, SparseCore 0:
  11.3 84.8 all-gather.11
  98.3 363.0 all-gather.15
  464.4 115.3 all-gather.9
  583.3 129.5 all-gather.13
  884.2 52.5 all-reduce.3
where the time goes:
time: 1980 us
  blocking collectives  1890 us (95%)
  matrix products  39.7 us (2%)
  local copies, waits for them, and re-layouts  25.8 us (1%)
    unnamed x1, blocking collectives  1080 us
    all_gather x1, blocking collectives, body(): lax.all_gather(up_key, ('dp', 'context'), axis=0, tiled=True)  538 us
    all_gather x1, blocking collectives, body(): lax.all_gather(own_rot_flat, 'context', axis=0, tiled=True)  104 us
    all_gather x1, blocking collectives, body(): lax.all_gather(row_delta, 'context', axis=0, tiled=True)  64.6 us
    all_gather x1, blocking collectives, body(): lax.all_gather(log_total, 'context', axis=0, tiled=True)  64.2 us
  transfers between devices with their start and end apart: 5, of which 0 were waited for; matrix products, arithmetic and copies ran while one was open for 3% of the time, Pallas kernels for 0%

commit v1 on v0

v1 whole, which is shorter than its diff:
```python
import jax
import jax.numpy as jnp
from jax import lax
from jax.experimental import pallas as pl
from jax.experimental.pallas import tpu as pltpu
from jax.sharding import Mesh, PartitionSpec as P

rope_base = 500000.0
neg_large = -1e30
log2_e = 1.4426950408889634

CTX = 8
TOK = 128
SEQ = CTX * TOK
HD = 128
RD = 32
HALF_RD = 16
NOPE = 96
RANK = 512
ROWS = 4
ZL = 8
CORE = 2
TEN = 4
Q0, G0, K0, W0, MSG = 0, 128, 256, 288, 304
BLK = 256

f32 = jnp.float32
bf16 = jnp.bfloat16


def dot(a, b, dims=((1,), (0,))):
    return lax.dot_general(a, b, (dims, ((), ())), preferred_element_type=f32)


def pack_kernel(q_ref, g_ref, kr_ref, wk_ref, wv_ref, pos_ref, out_ref):
    rope_t = kr_ref[...].astype(f32).T.astype(bf16)
    pos = pos_ref[...]
    high = (pos >> 6).astype(f32)
    low = (pos & 63).astype(f32)
    wk = wk_ref[...].astype(f32)
    wv = wv_ref[...].astype(f32)
    for h in range(CTX):
        out_ref[h, Q0:Q0 + TOK, :] = q_ref[:, h * HD:(h + 1) * HD]
        out_ref[h, G0:G0 + TOK, :] = g_ref[:, h * HD:(h + 1) * HD]
        out_ref[h, K0:K0 + RD, :] = rope_t[h * RD:(h + 1) * RD, :]
        wk_h = jnp.concatenate([jnp.zeros((ROWS, RD), f32), wk[:, h * NOPE:(h + 1) * NOPE]], 1)
        tail = jnp.concatenate(
            [wv[:, h * HD:(h + 1) * HD], wk_h, high, low, jnp.zeros((6, TOK), f32)], 0
        )
        out_ref[h, W0:MSG, :] = tail.astype(bf16)


def pack(query, out_grad, key_rope, up_key, up_value, positions):
    return pl.pallas_call(
        pack_kernel,
        out_shape=jax.ShapeDtypeStruct((CTX, MSG, HD), bf16),
        name="pack",
    )(query, out_grad, key_rope, up_key, up_value, positions)


def main_kernel(
    zh_ref, inv_ref, msg_ref, lat_ref, w_ref,
    dq_ref, dkr_ref, dlat_ref, dw_ref,
    lat_s, w_s, k_s, kt_s, q_s, qt_s, v_s, gt_s, pos_s, cos_s, sin_s, dkv_s, dqt_s,
):
    zh = zh_ref[0]
    for z in range(2):
        for y in range(4):
            c = z * 4 + y
            lat_s[c * TOK:(c + 1) * TOK, :] = lat_ref[y, z ^ zh]
    for z in range(ZL):
        for c in range(CORE):
            r = (z * CORE + c) * 32
            w_s[r:r + 32, HD:2 * HD] = w_ref[c, z, 0:32, :]
            w_s[r:r + 32, 0:HD] = w_ref[c, z, 32:64, :]
    for c in range(CTX):
        tail = msg_ref[c, W0:MSG, :].astype(f32)
        pos_s[0:1, c * TOK:(c + 1) * TOK] = tail[8:9] * 64.0 + tail[9:10]
    pos_row = pos_s[0:1, :]
    angles = inv_ref[...] * pos_row
    cos_s[...] = jnp.cos(angles)
    sin_s[...] = jnp.sin(angles)
    cos = cos_s[...]
    sin = sin_s[...]

    def rot(x):
        a, b = x[:HALF_RD], x[HALF_RD:RD]
        return jnp.concatenate([a * cos - b * sin, b * cos + a * sin], 0)

    kr = jnp.concatenate([msg_ref[c, K0:K0 + RD, :] for c in range(CTX)], 1).astype(f32)
    kr_pad = jnp.concatenate([rot(kr), jnp.zeros((HD - RD, SEQ), f32)], 0)
    kv = dot(lat_s[...], w_s[...])
    k = (kv[:, :HD] + kr_pad.T).astype(bf16)
    k_s[...] = k
    kt_s[...] = k.astype(f32).T.astype(bf16)
    v_s[...] = kv[:, HD:].astype(bf16)
    for c in range(CTX):
        qt_s[:, c * TOK:(c + 1) * TOK] = msg_ref[c, Q0:Q0 + TOK, :].astype(f32).T
        gt_s[:, c * TOK:(c + 1) * TOK] = msg_ref[c, G0:G0 + TOK, :].astype(f32).T.astype(bf16)
    qt_s[0:RD, :] = rot(qt_s[0:RD, :])
    qt = qt_s[...]
    q_s[...] = qt.T.astype(bf16)
    pos_col = jnp.broadcast_to(pos_row, (8, SEQ)).T[:, 0:1]
    scale = HD ** -0.5
    dkv_s[...] = jnp.zeros_like(dkv_s)

    for b in range(SEQ // BLK):
        cols = slice(b * BLK, (b + 1) * BLK)
        st = dot(k_s[...], qt[:, cols].astype(bf16))
        visible = pos_col <= pos_row[:, cols]
        st = jnp.where(visible, st * (scale * log2_e), neg_large)
        top = jnp.max(st, 0, keepdims=True)
        e = jnp.exp2(st - top)
        dp = dot(v_s[...], gt_s[:, cols])
        total = jnp.sum(e, 0, keepdims=True)
        weighted = jnp.sum(e * dp, 0, keepdims=True)
        inv_total = 1.0 / total
        delta = weighted * inv_total
        probs = (e * inv_total).astype(bf16)
        ds = (scale * probs.astype(f32) * (dp - delta)).astype(bf16)
        dqt_s[:, cols] = dot(kt_s[...], ds)
        dkv_s[:, 0:HD] += dot(ds, q_s[cols, :])
        grad = jnp.concatenate(
            [msg_ref[c, G0:G0 + TOK, :] for c in range(b * BLK // TOK, (b + 1) * BLK // TOK)], 0
        )
        dkv_s[:, HD:] += dot(probs, grad)

    def unrot(x):
        a, b = x[:HALF_RD], x[HALF_RD:RD]
        return jnp.concatenate([a * cos + b * sin, b * cos - a * sin], 0)

    dqt_s[0:RD, :] = unrot(dqt_s[0:RD, :])
    dq = dqt_s[...].T.astype(bf16)
    dkr = unrot(dkv_s[:, 0:HD].T[0:RD, :]).astype(bf16)
    for c in range(CTX):
        dq_ref[c] = dq[c * TOK:(c + 1) * TOK, :]
        dkr_ref[c] = dkr[:, c * TOK:(c + 1) * TOK]
    dkv = dkv_s[...].astype(bf16)
    dlat = dot(dkv, w_s[...], ((1,), (1,))).astype(bf16)
    for t in range(TEN):
        dlat_ref[t] = dlat[:, t * HD:(t + 1) * HD]
    dw = dot(lat_s[...], dkv, ((0,), (0,))).astype(bf16)
    for z in range(ZL):
        for c in range(CORE):
            r = (z * CORE + c) * 32
            dw_ref[c, z] = dw[r:r + 32, :]


def attention(zh, inverse, msg, lat, w):
    smem = pl.BlockSpec(memory_space=pltpu.SMEM)
    vmem = pl.BlockSpec(memory_space=pltpu.VMEM)
    return pl.pallas_call(
        main_kernel,
        in_specs=[smem, vmem, vmem, vmem, vmem],
        out_specs=[vmem] * 4,
        out_shape=[
            jax.ShapeDtypeStruct((CTX, TOK, HD), bf16),
            jax.ShapeDtypeStruct((CTX, RD, TOK), bf16),
            jax.ShapeDtypeStruct((TEN, SEQ, HD), bf16),
            jax.ShapeDtypeStruct((CORE, ZL, 32, 2 * HD), bf16),
        ],
        scratch_shapes=[
            pltpu.VMEM((SEQ, RANK), bf16),
            pltpu.VMEM((RANK, 2 * HD), bf16),
            pltpu.VMEM((SEQ, HD), bf16),
            pltpu.VMEM((HD, SEQ), bf16),
            pltpu.VMEM((SEQ, HD), bf16),
            pltpu.VMEM((HD, SEQ), f32),
            pltpu.VMEM((SEQ, HD), bf16),
            pltpu.VMEM((HD, SEQ), bf16),
            pltpu.VMEM((8, SEQ), f32),
            pltpu.VMEM((HALF_RD, SEQ), f32),
            pltpu.VMEM((HALF_RD, SEQ), f32),
            pltpu.VMEM((SEQ, 2 * HD), f32),
            pltpu.VMEM((HD, SEQ), f32),
        ],
        compiler_params=pltpu.CompilerParams(vmem_limit_bytes=56 * 1024 * 1024),
        name="attention_backward",
    )(zh, inverse, msg, lat, w)


def combine_kernel(dq_ref, dkr_ref, lat_ref, dw_ref, out_ref):
    dw = jnp.sum(dw_ref[...].astype(f32), 0)
    for c in range(CTX):
        out_ref[c, 0:TOK, :] = dq_ref[c]
        out_ref[c, K0:K0 + RD, :] = dkr_ref[c]
        rows = slice(c * TOK, (c + 1) * TOK)
        out_ref[c, G0:G0 + TOK, :] = jnp.sum(lat_ref[:, rows, :].astype(f32), 0).astype(bf16)
        part = dw[c * ROWS:(c + 1) * ROWS, :]
        tail = jnp.concatenate([part[:, HD:], part[:, :HD], jnp.zeros((8, HD), f32)], 0)
        out_ref[c, W0:MSG, :] = tail.astype(bf16)


def combine(dq, dkr, lat, dw):
    return pl.pallas_call(
        combine_kernel,
        out_shape=jax.ShapeDtypeStruct((CTX, MSG, HD), bf16),
        name="combine",
    )(dq, dkr, lat, dw)


def unpack_kernel(msg_ref, q_ref, kr_ref, lat_ref, wk_ref, wv_ref):
    ropes = []
    wk = []
    wv = []
    lat = jnp.zeros((TOK, HD), f32)
    for h in range(CTX):
        q_ref[:, h * HD:(h + 1) * HD] = msg_ref[h, 0:TOK, :]
        ropes.append(msg_ref[h, K0:K0 + RD, :].astype(f32))
        lat = lat + msg_ref[h, G0:G0 + TOK, :].astype(f32)
        tail = msg_ref[h, W0:MSG, :].astype(f32)
        wv.append(tail[0:ROWS])
        wk.append(tail[ROWS:2 * ROWS, RD:])
    kr_ref[...] = jnp.concatenate(ropes, 0).T.astype(bf16)
    lat_ref[...] = lat.astype(bf16)
    wk_ref[...] = jnp.concatenate(wk, 1).astype(bf16)
    wv_ref[...] = jnp.concatenate(wv, 1).astype(bf16)


def unpack(msg):
    return pl.pallas_call(
        unpack_kernel,
        out_shape=[
            jax.ShapeDtypeStruct((TOK, CTX * HD), bf16),
            jax.ShapeDtypeStruct((TOK, CTX * RD), bf16),
            jax.ShapeDtypeStruct((TOK, HD), bf16),
            jax.ShapeDtypeStruct((ROWS, CTX * NOPE), bf16),
            jax.ShapeDtypeStruct((ROWS, CTX * HD), bf16),
        ],
        name="unpack",
    )(msg)


def body(latent, key_rope, query, out_grad, positions, freq_index, up_key, up_value):
    ctx = ("zh", "y")
    zh = lax.axis_index("zh")
    head = lax.axis_index(ctx)
    own_freq = lax.dynamic_index_in_dim(freq_index, head, 0, keepdims=False)
    inverse = rope_base ** (-2.0 * own_freq.astype(f32) / HD)

    other = lax.ppermute(latent[0], "zh", [(0, 1), (1, 0)])
    lat = lax.all_gather(jnp.stack([latent[0], other]), "y", axis=0)

    msg = pack(query[0], out_grad[0], key_rope[0], up_key, up_value, positions)
    msg = lax.all_to_all(msg, ctx, 0, 0)

    own_w = msg[:, W0:W0 + 2 * ROWS, :].reshape(CTX, 2, ROWS, HD).transpose(1, 0, 2, 3)
    own_w = own_w.reshape(1, 2 * 32, HD)
    w = lax.all_to_all(jnp.broadcast_to(own_w, (ZL, 2 * 32, HD)), "zl", 0, 0)
    w = lax.all_gather(w, "core", axis=0)

    dq, dkr, dlat, dw = attention(
        zh.reshape(1).astype(jnp.int32), inverse.reshape(HALF_RD, 1), msg, lat, w
    )

    dw = lax.all_to_all(dw, "core", 0, 0)
    dw = (dw[0].astype(f32) + dw[1].astype(f32)).astype(bf16)
    dw = lax.all_to_all(dw, "zl", 0, 0)
    dlat = lax.all_to_all(dlat, "x", 0, 0)
    back = lax.all_to_all(combine(dq, dkr, dlat, dw), ctx, 0, 0)
    query_grad, key_rope_grad, quarter, up_key_grad, up_value_grad = unpack(back)
    latent_grad = lax.all_gather(quarter, "x", axis=1, tiled=True)
    return (query_grad[None], key_rope_grad[None], latent_grad[None], up_key_grad, up_value_grad)


def solution(mesh):
    split = Mesh(mesh.devices.reshape(ZL, CORE, 2, 4, TEN), ("zl", "core", "zh", "y", "x"))
    dp, context, tensor = ("zl", "core"), ("zh", "y"), "x"
    return jax.shard_map(
        body,
        mesh=split,
        in_specs=(
            P(dp, context, None),
            P(dp, context, tensor),
            P(dp, context, tensor),
            P(dp, context, tensor),
            P(dp, context),
            P(tensor, None),
            P(dp + context, tensor),
            P(dp + context, tensor),
        ),
        out_specs=(
            P(dp, context, tensor),
            P(dp, context, tensor),
            P(dp, context, None),
            P(dp + context, tensor),
            P(dp + context, tensor),
        ),
        check_vma=False,
    )
```

time: 1980 us -> 218 us (0.11)
  the two profiles are of different devices: /device:TPU:422 before, /device:TPU:8 now
where the time goes in v1:
time: 218 us; the launch traced here: 217 us
  blocking collectives  98.2 us (45%)
  starting transfers between devices  57.7 us (26%)
  waiting for transfers between devices  29.1 us (13%)
  Pallas kernels  14.6 us (7%)
  between operations  14.1 us (6%)
    all_to_all x1, blocking collectives, body(): back = lax.all_to_all(combine(dq, dkr, dlat, dw), ctx, 0, 0)  40.2 us
    all_to_all x1, starting transfers between devices, body(): w = lax.all_to_all(jnp.broadcast_to(own_w, (ZL, 2 * 32, HD)), 'zl', 0, 0)  27.3 us
    all_to_all x1, blocking collectives, body(): dw = lax.all_to_all(dw, 'zl', 0, 0)  22.5 us
    all_to_all x1, starting transfers between devices, body(): msg = lax.all_to_all(msg, ctx, 0, 0)  18.3 us
    all_to_all x1, blocking collectives, body(): dlat = lax.all_to_all(dlat, 'x', 0, 0)  17.4 us
    ppermute x1, waiting for transfers between devices, body(): other = lax.ppermute(latent[0], 'zh', [(0, 1), (1, 0)])  13.6 us
    ppermute x1, starting transfers between devices, body(): other = lax.ppermute(latent[0], 'zh', [(0, 1), (1, 0)])  12.1 us
    all_gather x1, blocking collectives, body(): latent_grad = lax.all_gather(quarter, 'x', axis=1, tiled=True)  10.9 us
  transfers between devices with their start and end apart: 4, of which 3 were waited for; matrix products, arithmetic and copies ran while one was open for 1% of the time, Pallas kernels for 0%

profile of v1, /device:TPU:8, one launch (start us, length us, event | category | flops | bytes accessed | tf_op | source)
XLA Modules:
  0.0 217.2 jit_solution(7743996614152904133)
XLA Ops:
  7.2 2.0 pack.1
  9.2 0.0 copy-start.2
  9.2 18.3 %all-to-all-start = ((bf16[8,304,128]{2,1,0:T(8,128)(2,1)}), bf16[8,304,128]{2,1,0:T(8,128)(2,1)S(1)}, u32[]{:S(2)}, u32[]{:S(2)}) async-start(bf16[8,304,128]{2,1,0:T(8,128)(2,1)} %pack.1), calls=%async_computation | async-start | bytes 1245184 | tf_op jit(solution)/shard_map/all_to_all | solution.py:245
  27.5 0.0 all-gather.4.cloned.1.call-start
  27.5 0.0 copy-done.2
  27.5 12.1 %collective-permute-start = (bf16[128,512]{1,0:T(8,128)(2,1)S(1)}, bf16[128,512]{1,0:T(8,128)(2,1)S(1)}, u32[]{:S(2)}, u32[]{:S(2)}) collective-permute-start(bf16[128,512]{1,0:T(8,128)(2,1)S(1)} %bitcast.24), channel_id=1, source_target_pairs={{0,16},{16,0},{1,17},{17,1},{2,18},{18,2},{3,19},{19,3},{4,20},{20... | collective-permute-start | bytes 393224 | tf_op jit(solution)/shard_map/ppermute | solution.py:241
  39.6 13.6 %collective-permute-done = bf16[128,512]{1,0:T(8,128)(2,1)S(1)} collective-permute-done((bf16[128,512]{1,0:T(8,128)(2,1)S(1)}, bf16[128,512]{1,0:T(8,128)(2,1)S(1)}, u32[]{:S(2)}, u32[]{:S(2)}) %collective-permute-start) | collective-permute-done | bytes 131104 | tf_op jit(solution)/shard_map/ppermute | solution.py:241
  53.2 0.7 pad_maximum_fusion
  54.0 0.0 all-gather.4.cloned.1.call-update
  54.0 0.0 all-to-all-done.msg_ref
  54.0 0.0 copy-start
  54.0 0.8 broadcast_in_dim.17
  54.8 27.3 %all-to-all-start.1 = ((bf16[8,64,128]{2,1,0:T(8,128)(2,1)}), bf16[8,64,128]{2,1,0:T(8,128)(2,1)S(1)}, u32[]{:S(2)}, u32[]{:S(2)}) async-start(bf16[8,64,128]{2,1,0:T(8,128)(2,1)} %broadcast_in_dim.17), calls=%async_computation.1 | async-start | bytes 262144 | tf_op jit(solution)/shard_map/all_to_all | solution.py:249
  82.1 0.7 power_bitcast_fusion
  82.8 0.7 copy.17.inv_ref
  83.5 10.0 %all-to-all-done.1 = bf16[8,64,128]{2,1,0:T(8,128)(2,1)S(1)} async-done(((bf16[8,64,128]{2,1,0:T(8,128)(2,1)}), bf16[8,64,128]{2,1,0:T(8,128)(2,1)S(1)}, u32[]{:S(2)}, u32[]{:S(2)}) %all-to-all-start.1) | async-done | bytes 131104 | tf_op jit(solution)/shard_map/all_to_all | solution.py:249
  93.5 2.1 all-gather.1
  95.6 5.4 %all-gather.4.cloned.1.call-done = bf16[8,128,512]{2,1,0:T(8,128)(2,1)} async-done(((bf16[2,128,512]{2,1,0:T(8,128)(2,1)}), bf16[8,128,512]{2,1,0:T(8,128)(2,1)}) %all-gather.4.cloned.1.call-update) | async-done | bytes 1048592 | tf_op jit(solution)/shard_map/all_gather | solution.py:242
  101.0 0.0 copy-done
  101.0 8.3 %attention_backward.1 = (bf16[8,128,128]{2,1,0:T(8,128)(2,1)}, bf16[8,32,128]{2,1,0:T(8,128)(2,1)}, bf16[4,1024,128]{2,1,0:T(8,128)(2,1)}, bf16[2,8,32,256]{3,2,1,0:T(8,128)(2,1)}) custom-call(s32[1]{0:T(128)} %bitcast.zh_ref, f32[16,1]{1,0:T(8,128)} %copy.17.inv_ref, bf16[8,304,128]{2,1,0:T(8,128)(2,1)} %copy-done, bf16[4,2,128,512]{3,2,1,0:T(8,128)(2,1)} %bitcast.20, ...), custom_call_target="tpu_custom_call" | custom-call | tf_op jit(solution)/shard_map/attention_backward/pallas_call | solution.py:152
  109.4 0.0 copy-start.1
  109.4 5.1 %all_to_all.30 = bf16[2,8,32,256]{3,2,1,0:T(8,128)(2,1)S(1)} all-to-all(bf16[2,8,32,256]{3,2,1,0:T(8,128)(2,1)} %get-tuple-element.17), channel_id=1, replica_groups=mesh['zl'=8,'core'=2,'zh'=2,'y'=4,'x'=4] {'core'}, dimensions={0} | all-to-all | bytes 524288 | tf_op jit(solution)/shard_map/all_to_all | solution.py:256
  114.5 22.5 %all_to_all.31.dw_ref = bf16[8,32,256]{2,1,0:T(8,128)(2,1)} all-to-all(bf16[8,32,256]{2,1,0:T(8,128)(2,1)S(1)} %fusion), channel_id=1, replica_groups=mesh['zl'=8,'core'=2,'zh'=2,'y'=4,'x'=4] {'zl'}, dimensions={0} | all-to-all | bytes 262144 | tf_op jit(solution)/shard_map/all_to_all | solution.py:258
  137.0 0.0 copy-done.1
  137.0 17.4 %all_to_all.32.lat_ref = bf16[4,1024,128]{2,1,0:T(8,128)(2,1)} all-to-all(bf16[4,1024,128]{2,1,0:T(8,128)(2,1)S(1)} %copy-done.1), channel_id=1, replica_groups=mesh['zl'=8,'core'=2,'zh'=2,'y'=4,'x'=4] {'x'}, dimensions={0} | all-to-all | bytes 2097152 | tf_op jit(solution)/shard_map/all_to_all | solution.py:259
  154.4 2.4 %combine.1 = bf16[8,304,128]{2,1,0:T(8,128)(2,1)} custom-call(bf16[8,128,128]{2,1,0:T(8,128)(2,1)} %get-tuple-element.14.dq_ref, bf16[8,32,128]{2,1,0:T(8,128)(2,1)} %get-tuple-element.15.dkr_ref, bf16[4,1024,128]{2,1,0:T(8,128)(2,1)} %all_to_all.32.lat_ref, bf16[8,32,256]{2,1,0:T(8,128)(2,1)} %all_to_all.31.dw_ref), custom_call_target="tpu_custom_call" | custom-call | tf_op jit(solution)/shard_map/combine/pallas_call | solution.py:195
  156.7 40.2 %all_to_all.33.msg_ref = bf16[8,304,128]{2,1,0:T(8,128)(2,1)} all-to-all(bf16[8,304,128]{2,1,0:T(8,128)(2,1)} %combine.1), channel_id=1, replica_groups=mesh['zl'=8,'core'=2,'zh'=2,'y'=4,'x'=4] {'zh','y'}, dimensions={0} | all-to-all | bytes 1245184 | tf_op jit(solution)/shard_map/all_to_all | solution.py:260
  196.9 1.9 unpack.1
  198.8 10.9 %all_gather.19 = bf16[128,512]{1,0:T(8,128)(2,1)S(1)} all-gather(bf16[128,128]{1,0:T(8,128)(2,1)} %get-tuple-element.20), channel_id=1, replica_groups=mesh['zl'=8,'core'=2,'zh'=2,'y'=4,'x'=4] {'x'}, dimensions={1}, use_global_device_ids=true | all-gather | bytes 163840 | tf_op jit(solution)/shard_map/all_gather | solution.py:262
  209.7 0.7 copy.19
  (3 shorter events, 0.0 us)
Async XLA Ops:
  9.2 18.3 %copy-start.2 = (bf16[1,128,512]{2,1,0:T(8,128)(2,1)S(1)}, bf16[1,128,512]{2,1,0:T(8,128)(2,1)}, u32[]{:S(2)}) copy-start(bf16[1,128,512]{2,1,0:T(8,128)(2,1)} %param.8) | copy-start | bytes 393220
  9.2 44.8 %all-to-all-start = ((bf16[8,304,128]{2,1,0:T(8,128)(2,1)}), bf16[8,304,128]{2,1,0:T(8,128)(2,1)S(1)}, u32[]{:S(2)}, u32[]{:S(2)}) async-start(bf16[8,304,128]{2,1,0:T(8,128)(2,1)} %pack.1), calls=%async_computation | async-start | bytes 1245184 | tf_op jit(solution)/shard_map/all_to_all | solution.py:245
  27.5 73.5 %all-gather.4.cloned.1.call-start = ((), (), s32[]{:S(2)}) async-start(), calls=%async_computation.6 | async-start | bytes 1310720 | tf_op jit(solution)/shard_map/all_gather | solution.py:242
  27.5 25.7 %collective-permute-start = (bf16[128,512]{1,0:T(8,128)(2,1)S(1)}, bf16[128,512]{1,0:T(8,128)(2,1)S(1)}, u32[]{:S(2)}, u32[]{:S(2)}) collective-permute-start(bf16[128,512]{1,0:T(8,128)(2,1)S(1)} %bitcast.24), channel_id=1, source_target_pairs={{0,16},{16,0},{1,17},{17,1},{2,18},{18,2},{3,19},{19,3},{4,20},{20... | collective-permute-start | bytes 393224 | tf_op jit(solution)/shard_map/ppermute | solution.py:241
  54.0 47.0 %copy-start = (bf16[8,304,128]{2,1,0:T(8,128)(2,1)}, bf16[8,304,128]{2,1,0:T(8,128)(2,1)S(1)}, u32[]{:S(2)}) copy-start(bf16[8,304,128]{2,1,0:T(8,128)(2,1)S(1)} %all-to-all-done.msg_ref) | copy-start | bytes 1867780
  54.8 38.7 %all-to-all-start.1 = ((bf16[8,64,128]{2,1,0:T(8,128)(2,1)}), bf16[8,64,128]{2,1,0:T(8,128)(2,1)S(1)}, u32[]{:S(2)}, u32[]{:S(2)}) async-start(bf16[8,64,128]{2,1,0:T(8,128)(2,1)} %broadcast_in_dim.17), calls=%async_computation.1 | async-start | bytes 262144 | tf_op jit(solution)/shard_map/all_to_all | solution.py:249
  109.4 27.6 %copy-start.1 = (bf16[4,1024,128]{2,1,0:T(8,128)(2,1)S(1)}, bf16[4,1024,128]{2,1,0:T(8,128)(2,1)}, u32[]{:S(2)}) copy-start(bf16[4,1024,128]{2,1,0:T(8,128)(2,1)} %get-tuple-element.16) | copy-start | bytes 3145732
Sparse Core Ops, SparseCore 0:
  54.1 46.8 all-gather.3

commit v2 on v1

v2 whole, which is shorter than its diff:
```python
import jax
import jax.numpy as jnp
from jax import lax
from jax.experimental import pallas as pl
from jax.experimental.pallas import tpu as pltpu
from jax.sharding import Mesh, PartitionSpec as P

rope_base = 500000.0
neg_large = -1e30
log2_e = 1.4426950408889634

NY = 4
GRP = 2
TOK = 128
HALF = NY * TOK
SEQ = 2 * HALF
HD = 128
RD = 32
HALF_RD = 16
NOPE = 96
RANK = 512
ROWS = 4
ZL = 8
CORE = 2
NZ = 2 * ZL
TEN = 4
Q0, G0, K0, S0, W0, MSG = 0, 256, 512, 576, 592, 608
BL0, BK0, BW0, BACK = 256, 512, 576, 592
BLK = 256

f32 = jnp.float32
bf16 = jnp.bfloat16


def dot(a, b, dims=((1,), (0,))):
    return lax.dot_general(a, b, (dims, ((), ())), preferred_element_type=f32)


def pack_kernel(q_ref, g_ref, kr_ref, wk_ref, wv_ref, pos_ref, out_ref):
    rope_t = kr_ref[...].astype(f32).T.astype(bf16)
    pos = pos_ref[...]
    places = jnp.concatenate(
        [(pos >> 6).astype(f32), (pos & 63).astype(f32), jnp.zeros((14, TOK), f32)], 0
    ).astype(bf16)
    wk = wk_ref[...].astype(f32)
    wv = wv_ref[...].astype(f32)
    for y in range(NY):
        parts_k = []
        parts_v = []
        for g in range(GRP):
            h = y * GRP + g
            cols = slice(h * HD, (h + 1) * HD)
            out_ref[y, Q0 + g * TOK:Q0 + (g + 1) * TOK, :] = q_ref[:, cols]
            out_ref[y, G0 + g * TOK:G0 + (g + 1) * TOK, :] = g_ref[:, cols]
            parts_v.append(wv[:, cols])
            parts_k.append(
                jnp.concatenate([jnp.zeros((ROWS, RD), f32), wk[:, h * NOPE:(h + 1) * NOPE]], 1)
            )
        out_ref[y, K0:S0, :] = rope_t[y * GRP * RD:(y + 1) * GRP * RD, :]
        out_ref[y, S0:W0, :] = places
        out_ref[y, W0:MSG, :] = jnp.concatenate(parts_k + parts_v, 0).astype(bf16)


def pack(query, out_grad, key_rope, up_key, up_value, positions):
    return pl.pallas_call(
        pack_kernel,
        out_shape=jax.ShapeDtypeStruct((NY, MSG, HD), bf16),
        name="pack",
    )(query, out_grad, key_rope, up_key, up_value, positions)


def main_kernel(
    where_ref, inv_ref, msg_ref, other_ref, lat_ref, w_ref,
    dq_ref, dkr_own_ref, dkr_other_ref, dl0_ref, dl1_ref, dl2_ref, dl3_ref, dw_own_ref, dw_other_ref,
    lat_s, w_s, k_s, kt_s, q_s, qt_s, v_s, gt_s, pos_s, cos_s, sin_s, dkv_s, dqt_s, dw_s,
):
    core = where_ref[0]
    x = where_ref[1]
    for z in range(2):
        for y in range(NY):
            c = z * NY + y
            lat_s[c * TOK:(c + 1) * TOK, :] = lat_ref[y, z]
    for z in range(NZ):
        for c in range(CORE):
            r = ((z // 2) * CORE + c) * 32 + (z % 2) * 16
            for kind in range(2 * GRP):
                w_s[r:r + 16, kind * HD:(kind + 1) * HD] = w_ref[c, z, kind * 16:(kind + 1) * 16, :]
    ropes = []
    for z in range(2):
        for y in range(NY):
            c = z * NY + y
            if z == 0:
                tail = msg_ref[y, S0:W0, :].astype(f32)
                ropes.append(msg_ref[y, K0:S0, :])
            else:
                tail = other_ref[y, GRP * RD:GRP * RD + 16, :].astype(f32)
                ropes.append(other_ref[y, 0:GRP * RD, :])
            pos_s[0:1, c * TOK:(c + 1) * TOK] = tail[0:1] * 64.0 + tail[1:2]
    rope_t = jnp.concatenate(ropes, 1).astype(f32)
    pos_row = pos_s[0:1, :]
    angles = inv_ref[...] * pos_row
    cos_s[...] = jnp.cos(angles)
    sin_s[...] = jnp.sin(angles)
    pos_col = jnp.broadcast_to(pos_row, (8, SEQ)).T[:, 0:1]
    scale = HD ** -0.5
    kv = dot(lat_s[...], w_s[...])
    dkv_s[...] = jnp.zeros_like(dkv_s)

    for g in range(GRP):
        cos = cos_s[g * HALF_RD:(g + 1) * HALF_RD, :]
        sin = sin_s[g * HALF_RD:(g + 1) * HALF_RD, :]

        def rot(a, width):
            a, b = a[:HALF_RD], a[HALF_RD:RD]
            c, s = cos[:, :width], sin[:, :width]
            return jnp.concatenate([a * c - b * s, b * c + a * s], 0)

        def unrot(a, width):
            a, b = a[:HALF_RD], a[HALF_RD:RD]
            c, s = cos[:, :width], sin[:, :width]
            return jnp.concatenate([a * c + b * s, b * c - a * s], 0)

        kr = rot(rope_t[g * RD:(g + 1) * RD, :], SEQ)
        kr_pad = jnp.concatenate([kr, jnp.zeros((HD - RD, SEQ), f32)], 0)
        k = kv[:, g * HD:(g + 1) * HD] + kr_pad.T
        k_s[...] = k.astype(bf16)
        kt_s[...] = k.T.astype(bf16)
        v_s[...] = kv[:, (GRP + g) * HD:(GRP + g + 1) * HD].astype(bf16)
        for c in range(NY):
            cols = slice(c * TOK, (c + 1) * TOK)
            qt_s[:, cols] = msg_ref[c, Q0 + g * TOK:Q0 + (g + 1) * TOK, :].astype(f32).T
            gt_s[:, cols] = msg_ref[c, G0 + g * TOK:G0 + (g + 1) * TOK, :].astype(f32).T.astype(bf16)
        qt_s[0:RD, :] = rot(qt_s[0:RD, :], HALF)
        qt = qt_s[...]
        q_s[...] = qt.T.astype(bf16)

        for b in range(HALF // BLK):
            cols = slice(b * BLK, (b + 1) * BLK)
            st = dot(k_s[...], qt[:, cols].astype(bf16))
            visible = pos_col <= pos_row[:, cols]
            st = jnp.where(visible, st * (scale * log2_e), neg_large)
            top = jnp.max(st, 0, keepdims=True)
            e = jnp.exp2(st - top)
            dp = dot(v_s[...], gt_s[:, cols])
            total = jnp.sum(e, 0, keepdims=True)
            weighted = jnp.sum(e * dp, 0, keepdims=True)
            inv_total = 1.0 / total
            delta = weighted * inv_total
            probs = (e * inv_total).astype(bf16)
            ds = (scale * probs.astype(f32) * (dp - delta)).astype(bf16)
            dqt_s[:, cols] = dot(kt_s[...], ds)
            dkv_s[:, g * HD:(g + 1) * HD] += dot(ds, q_s[cols, :])
            grad = jnp.concatenate(
                [
                    msg_ref[c, G0 + g * TOK:G0 + (g + 1) * TOK, :]
                    for c in range(b * BLK // TOK, (b + 1) * BLK // TOK)
                ],
                0,
            )
            dkv_s[:, (GRP + g) * HD:(GRP + g + 1) * HD] += dot(probs, grad)

        dqt_s[0:RD, :] = unrot(dqt_s[0:RD, :], HALF)
        dq = dqt_s[...].T.astype(bf16)
        dkr = unrot(dkv_s[:, g * HD:(g + 1) * HD].T[0:RD, :], SEQ).astype(bf16)
        for c in range(NY):
            cols = slice(c * TOK, (c + 1) * TOK)
            dq_ref[c, g * TOK:(g + 1) * TOK, :] = dq[cols, :]
            dkr_own_ref[c, g * RD:(g + 1) * RD, :] = dkr[:, cols]
            dkr_other_ref[c, g * RD:(g + 1) * RD, :] = dkr[:, HALF + c * TOK:HALF + (c + 1) * TOK]

    dkv = dkv_s[...].astype(bf16)
    for t, ref in enumerate((dl0_ref, dl1_ref, dl2_ref, dl3_ref)):
        rows = pl.ds(pl.multiple_of((x ^ t) * HD, HD), HD)
        ref[...] = dot(dkv, w_s[rows, :], ((1,), (1,))).astype(bf16)
    dw_s[...] = dot(lat_s[...], dkv, ((0,), (0,)))
    for z in range(NZ):
        base = (z // 2) * CORE * 32 + (z % 2) * 16
        dw_own_ref[z] = dw_s[pl.ds(pl.multiple_of(base + core * 32, 16), 16), :].astype(bf16)
        dw_other_ref[z] = dw_s[pl.ds(pl.multiple_of(base + (1 - core) * 32, 16), 16), :].astype(bf16)


def attention(place, inverse, msg, other, lat, w):
    smem = pl.BlockSpec(memory_space=pltpu.SMEM)
    vmem = pl.BlockSpec(memory_space=pltpu.VMEM)
    rope = jax.ShapeDtypeStruct((NY, GRP * RD, TOK), bf16)
    quarter = jax.ShapeDtypeStruct((SEQ, HD), bf16)
    weight = jax.ShapeDtypeStruct((NZ, 16, 2 * GRP * HD), bf16)
    return pl.pallas_call(
        main_kernel,
        in_specs=[smem] + [vmem] * 5,
        out_specs=[vmem] * 9,
        out_shape=[jax.ShapeDtypeStruct((NY, GRP * TOK, HD), bf16), rope, rope]
        + [quarter] * 4
        + [weight, weight],
        scratch_shapes=[
            pltpu.VMEM((SEQ, RANK), bf16),
            pltpu.VMEM((RANK, 2 * GRP * HD), bf16),
            pltpu.VMEM((SEQ, HD), bf16),
            pltpu.VMEM((HD, SEQ), bf16),
            pltpu.VMEM((HALF, HD), bf16),
            pltpu.VMEM((HD, HALF), f32),
            pltpu.VMEM((SEQ, HD), bf16),
            pltpu.VMEM((HD, HALF), bf16),
            pltpu.VMEM((8, SEQ), f32),
            pltpu.VMEM((GRP * HALF_RD, SEQ), f32),
            pltpu.VMEM((GRP * HALF_RD, SEQ), f32),
            pltpu.VMEM((SEQ, 2 * GRP * HD), f32),
            pltpu.VMEM((HD, HALF), f32),
            pltpu.VMEM((RANK, 2 * GRP * HD), f32),
        ],
        compiler_params=pltpu.CompilerParams(vmem_limit_bytes=56 * 1024 * 1024),
        name="attention_backward",
    )(place, inverse, msg, other, lat, w)


def combine_kernel(dq_ref, kr0_ref, kr1_ref, l0_ref, l1_ref, l2_ref, l3_ref, dw_ref, out_ref):
    dw = jnp.sum(dw_ref[...].astype(f32), 0)
    for y in range(NY):
        out_ref[y, 0:BL0, :] = dq_ref[y]
        out_ref[y, BK0:BW0, :] = (kr0_ref[y].astype(f32) + kr1_ref[y].astype(f32)).astype(bf16)
        for z in range(2):
            rows = slice((z * NY + y) * TOK, (z * NY + y + 1) * TOK)
            lat = (l0_ref[rows, :].astype(f32) + l1_ref[rows, :].astype(f32)) + (
                l2_ref[rows, :].astype(f32) + l3_ref[rows, :].astype(f32)
            )
            out_ref[y, BL0 + z * TOK:BL0 + (z + 1) * TOK, :] = lat.astype(bf16)
        part = dw[y * ROWS:(y + 1) * ROWS, :]
        out_ref[y, BW0:BACK, :] = jnp.concatenate(
            [part[:, c * HD:(c + 1) * HD] for c in range(2 * GRP)], 0
        ).astype(bf16)


def combine(*parts):
    return pl.pallas_call(
        combine_kernel,
        out_shape=jax.ShapeDtypeStruct((NY, BACK, HD), bf16),
        name="combine",
    )(*parts)


def unpack_kernel(where_ref, msg_ref, q_ref, kr_ref, lat_ref, wk_ref, wv_ref):
    half = where_ref[0]
    ropes = []
    wk = []
    wv = []
    for y in range(NY):
        for g in range(GRP):
            h = y * GRP + g
            q_ref[:, h * HD:(h + 1) * HD] = msg_ref[y, g * TOK:(g + 1) * TOK, :]
        ropes.append(msg_ref[y, BK0:BW0, :].astype(f32))
        tail = msg_ref[y, BW0:BACK, :].astype(f32)
        for g in range(GRP):
            wk.append(tail[g * ROWS:(g + 1) * ROWS, RD:])
            wv.append(tail[(GRP + g) * ROWS:(GRP + g + 1) * ROWS])
    for z in range(2):
        lat = sum(
            msg_ref[y, BL0 + z * TOK:BL0 + (z + 1) * TOK, :].astype(f32) for y in range(NY)
        ).astype(bf16)
        for t in range(TEN):
            lat_ref[z ^ half, t] = lat
    kr_ref[...] = jnp.concatenate(ropes, 0).T.astype(bf16)
    wk_ref[...] = jnp.concatenate(wk, 1).astype(bf16)
    wv_ref[...] = jnp.concatenate(wv, 1).astype(bf16)


def unpack(half, msg):
    return pl.pallas_call(
        unpack_kernel,
        in_specs=[
            pl.BlockSpec(memory_space=pltpu.SMEM),
            pl.BlockSpec(memory_space=pltpu.VMEM),
        ],
        out_shape=[
            jax.ShapeDtypeStruct((TOK, NY * GRP * HD), bf16),
            jax.ShapeDtypeStruct((TOK, NY * GRP * RD), bf16),
            jax.ShapeDtypeStruct((2, TEN, TOK, HD), bf16),
            jax.ShapeDtypeStruct((ROWS, NY * GRP * NOPE), bf16),
            jax.ShapeDtypeStruct((ROWS, NY * GRP * HD), bf16),
        ],
        name="unpack",
    )(half, msg)


def swap(array, axis, size, flip):
    return lax.ppermute(array, axis, [(i, i ^ flip) for i in range(size)])


def body(latent, key_rope, query, out_grad, positions, freq_index, up_key, up_value):
    i32 = jnp.int32
    zh = lax.axis_index("zh").astype(i32)
    y = lax.axis_index("y")
    place = jnp.stack([lax.axis_index("core").astype(i32), lax.axis_index("x").astype(i32)])
    own_freq = lax.dynamic_slice_in_dim(freq_index, y * GRP, GRP, 0)
    inverse = rope_base ** (-2.0 * own_freq.astype(f32) / HD)

    other_lat = swap(latent[0], "zh", 2, 1)
    lat = lax.all_gather(jnp.stack([latent[0], other_lat]), "y", axis=0)

    msg = pack(query[0], out_grad[0], key_rope[0], up_key, up_value, positions)
    msg = lax.all_to_all(msg, "y", 0, 0)
    other = swap(msg[:, K0:W0, :], "zh", 2, 1)

    own_w = msg[:, W0:MSG, :].reshape(NY, 2 * GRP, ROWS, HD).transpose(1, 0, 2, 3)
    own_w = own_w.reshape(1, 2 * GRP * NY * ROWS, HD)
    w = lax.all_to_all(jnp.broadcast_to(own_w, (NZ,) + own_w.shape[1:]), ("zl", "zh"), 0, 0)
    w = lax.all_gather(w, "core", axis=0)

    dq, kr_own, kr_other, l0, l1, l2, l3, dw_own, dw_other = attention(
        place, inverse.reshape(GRP * HALF_RD, 1), msg, other, lat, w
    )

    dw = dw_own.astype(f32) + swap(dw_other, "core", 2, 1).astype(f32)
    dw = lax.all_to_all(dw.astype(bf16), ("zl", "zh"), 0, 0)
    l1 = swap(l1, "x", TEN, 1)
    l2 = swap(l2, "x", TEN, 2)
    l3 = swap(l3, "x", TEN, 3)
    kr_other = swap(kr_other, "zh", 2, 1)
    back = lax.all_to_all(combine(dq, kr_own, kr_other, l0, l1, l2, l3, dw), "y", 0, 0)
    query_grad, key_rope_grad, quarters, up_key_grad, up_value_grad = unpack(zh.reshape(1), back)
    quarters = lax.all_to_all(quarters.reshape(2 * TEN, TOK, HD), ("zh", "x"), 0, 0)
    halves = quarters.reshape(2, TEN, TOK, HD).astype(f32)
    latent_grad = (halves[0] + halves[1]).astype(bf16).transpose(1, 0, 2).reshape(1, TOK, RANK)
    return (query_grad[None], key_rope_grad[None], latent_grad, up_key_grad, up_value_grad)


def solution(mesh):
    split = Mesh(mesh.devices.reshape(ZL, CORE, 2, NY, TEN), ("zl", "core", "zh", "y", "x"))
    dp, context, tensor = ("zl", "core"), ("zh", "y"), "x"
    return jax.shard_map(
        body,
        mesh=split,
        in_specs=(
            P(dp, context, None),
            P(dp, context, tensor),
            P(dp, context, tensor),
            P(dp, context, tensor),
            P(dp, context),
            P(tensor, None),
            P(dp + context, tensor),
            P(dp + context, tensor),
        ),
        out_specs=(
            P(dp, context, tensor),
            P(dp, context, tensor),
            P(dp, context, None),
            P(dp + context, tensor),
            P(dp + context, tensor),
        ),
        check_vma=False,
    )
```

time: 218 us -> 185 us (0.85)
  the two profiles are of different devices: /device:TPU:8 before, /device:TPU:32 now
where the time goes in v2:
time: 185 us; the launch traced here: 184 us
  starting transfers between devices  72.4 us (39%)
  blocking collectives  36.7 us (20%)
  waiting for transfers between devices  36.1 us (20%)
  Pallas kernels  16.3 us (9%)
  between operations  14.2 us (8%)
  local copies, waits for them, and re-layouts  4.72 us (3%)
  other arithmetic  3.86 us (2%)
    ppermute x7, starting transfers between devices, swap(): return lax.ppermute(array, axis, [(i, i ^ flip) for i in range(size)])  49.6 us
    all_to_all x1, blocking collectives, body(): lax.all_to_all(quarters.reshape(2 * TEN, TOK, HD), ('zh', 'x'), 0, 0)  34.4 us
    all_to_all x1, waiting for transfers between devices, body(): lax.all_to_all(jnp.broadcast_to(own_w, (NZ,) + own_w.shape[1:]), ('zl', '...  12.3 us
    ppermute x7, waiting for transfers between devices, swap(): return lax.ppermute(array, axis, [(i, i ^ flip) for i in range(size)])  11.4 us
    pallas_call x1, Pallas kernels, attention(): pl.pallas_call(main_kernel, in_specs=[smem] + [vmem] * 5, out_specs=[vmem...  9.98 us
    all_to_all x1, waiting for transfers between devices, body(): lax.all_to_all(combine(dq, kr_own, kr_other, l0, l1, l2, l3, dw), 'y', 0, 0)  8.52 us
    all_to_all x1, starting transfers between devices, body(): lax.all_to_all(jnp.broadcast_to(own_w, (NZ,) + own_w.shape[1:]), ('zl', '...  8.31 us
    all_to_all x1, starting transfers between devices, body(): dw = lax.all_to_all(dw.astype(bf16), ('zl', 'zh'), 0, 0)  5.41 us
  transfers between devices with their start and end apart: 12, of which 6 were waited for; matrix products, arithmetic and copies ran while one was open for 2% of the time, Pallas kernels for 1%

profile of v2, /device:TPU:32, one launch (start us, length us, event | category | flops | bytes accessed | tf_op | source)
XLA Modules:
  0.0 184.4 jit_solution(7684563768961677556)
XLA Ops:
  7.2 14.8 %collective-permute-start.1 = (bf16[128,512]{1,0:T(8,128)(2,1)}, bf16[128,512]{1,0:T(8,128)(2,1)S(1)}, u32[]{:S(2)}, u32[]{:S(2)}) collective-permute-start(bf16[128,512]{1,0:T(8,128)(2,1)} %bitcast.24), channel_id=1, source_target_pairs={{0,16},{16,0},{1,17},{17,1},{2,18},{18,2},{3,19},{19,3},{4,20},{20... | collective-permute-start | bytes 393224 | tf_op jit(solution)/shard_map/ppermute | solution.py:285
  22.0 2.0 %pack.1 = bf16[4,608,128]{2,1,0:T(8,128)(2,1)} custom-call(bf16[128,1024]{1,0:T(8,128)(2,1)} %bitcast.22, bf16[128,1024]{1,0:T(8,128)(2,1)} %bitcast.23, bf16[128,256]{1,0:T(8,128)(2,1)} %bitcast.26, bf16[4,768]{1,0:T(4,128)(2,1)} %wk_ref.1, bf16[4,1024]{1,0:T(4,128)(2,1)} %wv_ref.1, s32[1,128]{1,0:T(1,128)} %pos_ref.1), custom_call_target="tpu_custom_call" | custom-call | tf_op jit(solution)/shard_map/pack/pallas_call | solution.py:65
  24.0 0.0 copy-start.6
  24.0 4.6 %all-to-all-start = ((bf16[4,608,128]{2,1,0:T(8,128)(2,1)}), bf16[4,608,128]{2,1,0:T(8,128)(2,1)S(1)}, u32[]{:S(2)}, u32[]{:S(2)}) async-start(bf16[4,608,128]{2,1,0:T(8,128)(2,1)} %pack.1), calls=%async_computation | async-start | bytes 1245184 | tf_op jit(solution)/shard_map/all_to_all | solution.py:300
  28.6 0.0 all-gather.4.cloned.1.call-start
  28.6 5.7 %collective-permute-done.1 = bf16[128,512]{1,0:T(8,128)(2,1)S(1)} collective-permute-done((bf16[128,512]{1,0:T(8,128)(2,1)}, bf16[128,512]{1,0:T(8,128)(2,1)S(1)}, u32[]{:S(2)}, u32[]{:S(2)}) %collective-permute-start.1) | collective-permute-done | bytes 131104 | tf_op jit(solution)/shard_map/ppermute | solution.py:285
  34.3 0.0 copy-done.6
  34.3 0.7 pad_maximum_fusion
  35.0 0.0 all-gather.4.cloned.1.call-update
  35.0 3.8 %all-to-all-done.msg_ref = bf16[4,608,128]{2,1,0:T(8,128)(2,1)S(1)} async-done(((bf16[4,608,128]{2,1,0:T(8,128)(2,1)}), bf16[4,608,128]{2,1,0:T(8,128)(2,1)S(1)}, u32[]{:S(2)}, u32[]{:S(2)}) %all-to-all-start) | async-done | bytes 622624 | tf_op jit(solution)/shard_map/all_to_all | solution.py:300
  38.9 0.0 copy-start
  38.9 0.8 broadcast_in_dim.14
  39.7 8.3 %all-to-all-start.1 = ((bf16[16,64,128]{2,1,0:T(8,128)(2,1)}), bf16[16,64,128]{2,1,0:T(8,128)(2,1)S(1)}, u32[]{:S(2)}, u32[]{:S(2)}) async-start(bf16[16,64,128]{2,1,0:T(8,128)(2,1)} %broadcast_in_dim.14), calls=%async_computation.1 | async-start | bytes 524288 | tf_op jit(solution)/shard_map/all_to_all | solution.py:305
  48.0 0.7 multiply_power_fusion
  48.7 0.7 reshape.43.inv_ref
  49.4 0.6 pad_add_fusion.where_ref
  50.0 11.2 %collective-permute-start = (bf16[4,80,128]{2,1,0:T(8,128)(2,1)S(1)}, bf16[4,80,128]{2,1,0:T(8,128)(2,1)S(1)}, u32[]{:S(2)}, u32[]{:S(2)}) collective-permute-start(bf16[4,80,128]{2,1,0:T(8,128)(2,1)S(1)} %slice.18), channel_id=1, source_target_pairs={{0,16},{16,0},{1,17},{17,1},{2,18},{18,2},{3,19},{19,3},{4,20},{20... | collective-permute-start | bytes 245768 | tf_op jit(solution)/shard_map/ppermute | solution.py:285
  61.2 12.3 %all-to-all-done.1 = bf16[16,64,128]{2,1,0:T(8,128)(2,1)S(1)} async-done(((bf16[16,64,128]{2,1,0:T(8,128)(2,1)}), bf16[16,64,128]{2,1,0:T(8,128)(2,1)S(1)}, u32[]{:S(2)}, u32[]{:S(2)}) %all-to-all-start.1) | async-done | bytes 262176 | tf_op jit(solution)/shard_map/all_to_all | solution.py:305
  73.5 2.3 %all-gather.1 = bf16[32,64,128]{2,1,0:T(8,128)(2,1)} all-gather(bf16[16,64,128]{2,1,0:T(8,128)(2,1)S(1)} %all-to-all-done.1), channel_id=3, replica_groups=mesh['zl'=8,'core'=2,'zh'=2,'y'=4,'x'=4] {'core'}, dimensions={0}, use_global_device_ids=true | all-gather | bytes 786432 | tf_op jit(solution)/shard_map/all_gather | solution.py:306
  75.8 0.0 copy-done
  75.8 0.0 collective-permute-done.other_ref
  75.8 0.0 copy-start.7
  75.8 0.0 all-gather.4.cloned.1.call-done
  75.8 0.6 copy-done.7
  76.4 10.0 %attention_backward.1 = (bf16[4,256,128]{2,1,0:T(8,128)(2,1)}, bf16[4,64,128]{2,1,0:T(8,128)(2,1)}, bf16[4,64,128]{2,1,0:T(8,128)(2,1)}, bf16[1024,128]{1,0:T(8,...) custom-call(s32[2]{0:T(128)} %pad_add_fusion.where_ref, ...), custom_call_target="tpu_custom_call" | custom-call | tf_op jit(solution)/shard_map/attention_backward/pallas_call | solution.py:188
  86.4 2.0 %collective-permute-start.6 = (bf16[16,16,512]{2,1,0:T(8,128)(2,1)}, bf16[16,16,512]{2,1,0:T(8,128)(2,1)S(1)}, u32[]{:S(2)}, u32[]{:S(2)}) collective-permute-start(bf16[16,16,512]{2,1,0:T(8,128)(2,1)} %get-tuple-element.27), channel_id=1, source_target_pairs={{0,32},{32,0},{1,33},{33,1},{2,34},{34,2},{3,35},{35,3},{4,36},{36... | collective-permute-start | bytes 786440 | tf_op jit(solution)/shard_map/ppermute | solution.py:285
  88.4 1.6 collective-permute-done.6
  90.0 0.0 copy-start.11
  90.0 0.0 copy-start.12
  90.0 1.8 add_convert_fusion
  91.8 0.0 copy-start.10
  91.8 0.0 copy-start.9
  91.8 5.4 %all-to-all-start.2 = ((bf16[16,16,512]{2,1,0:T(8,128)(2,1)}), bf16[16,16,512]{2,1,0:T(8,128)(2,1)S(1)}, u32[]{:S(2)}, u32[]{:S(2)}) async-start(bf16[16,16,512]{2,1,0:T(8,128)(2,1)} %add_convert_fusion), calls=%async_computation.2 | async-start | bytes 524288 | tf_op jit(solution)/shard_map/all_to_all | solution.py:313
  97.2 0.0 copy-done.11
  97.2 3.4 %collective-permute-start.3 = (bf16[1024,128]{1,0:T(8,128)(2,1)S(1)}, bf16[1024,128]{1,0:T(8,128)(2,1)S(1)}, u32[]{:S(2)}, u32[]{:S(2)}) collective-permute-start(bf16[1024,128]{1,0:T(8,128)(2,1)S(1)} %copy-done.11), channel_id=1, source_target_pairs={{0,1},{1,0},{2,3},{3,2},{4,5},{5,4},{6,7},{7,6},{8,9},{9,8},{10,11... | collective-permute-start | bytes 786440 | tf_op jit(solution)/shard_map/ppermute | solution.py:285
  100.6 0.0 copy-done.10
  100.6 4.6 %collective-permute-start.4 = (bf16[1024,128]{1,0:T(8,128)(2,1)S(1)}, bf16[1024,128]{1,0:T(8,128)(2,1)S(1)}, u32[]{:S(2)}, u32[]{:S(2)}) collective-permute-start(bf16[1024,128]{1,0:T(8,128)(2,1)S(1)} %copy-done.10), channel_id=1, source_target_pairs={{0,2},{1,3},{2,0},{3,1},{4,6},{5,7},{6,4},{7,5},{8,10},{9,11},{10,... | collective-permute-start | bytes 786440 | tf_op jit(solution)/shard_map/ppermute | solution.py:285
  105.3 0.0 copy-done.9
  105.3 2.4 %collective-permute-start.5 = (bf16[1024,128]{1,0:T(8,128)(2,1)S(1)}, bf16[1024,128]{1,0:T(8,128)(2,1)S(1)}, u32[]{:S(2)}, u32[]{:S(2)}) collective-permute-start(bf16[1024,128]{1,0:T(8,128)(2,1)S(1)} %copy-done.9), channel_id=1, source_target_pairs={{0,3},{1,2},{2,1},{3,0},{4,7},{5,6},{6,5},{7,4},{8,11},{9,10},{10,... | collective-permute-start | bytes 786440 | tf_op jit(solution)/shard_map/ppermute | solution.py:285
  107.7 0.0 copy-done.12
  107.7 11.2 %collective-permute-start.2 = (bf16[4,64,128]{2,1,0:T(8,128)(2,1)S(1)}, bf16[4,64,128]{2,1,0:T(8,128)(2,1)S(1)}, u32[]{:S(2)}, u32[]{:S(2)}) collective-permute-start(bf16[4,64,128]{2,1,0:T(8,128)(2,1)S(1)} %copy-done.12), channel_id=1, source_target_pairs={{0,16},{16,0},{1,17},{17,1},{2,18},{18,2},{3,19},{19,3},{4,20},{20... | collective-permute-start | bytes 196616 | tf_op jit(solution)/shard_map/ppermute | solution.py:285
  118.9 4.2 %collective-permute-done.2.kr1_ref = bf16[4,64,128]{2,1,0:T(8,128)(2,1)S(1)} collective-permute-done((bf16[4,64,128]{2,1,0:T(8,128)(2,1)S(1)}, bf16[4,64,128]{2,1,0:T(8,128)(2,1)S(1)}, u32[]{:S(2)}, u32[]{:S(2)}) %collective-permute-start.2) | collective-permute-done | bytes 65568 | tf_op jit(solution)/shard_map/ppermute | solution.py:285
  123.1 0.0 copy-start.8
  123.1 0.0 collective-permute-done.3.l1_ref
  123.1 0.0 copy-start.3
  123.1 0.0 collective-permute-done.4.l2_ref
  123.1 0.0 copy-start.4
  123.1 0.0 collective-permute-done.5.l3_ref
  123.1 0.0 copy-start.5
  123.1 0.0 all-to-all-done.2.dw_ref
  123.1 0.0 copy-start.2
  123.2 0.6 copy-done.8
  123.7 0.1 copy-done.3
  123.8 0.1 copy-done.4
  123.9 0.1 copy-done.5
  124.0 0.1 copy-done.2
  124.1 2.4 %combine.1 = bf16[4,592,128]{2,1,0:T(8,128)(2,1)} custom-call(bf16[4,256,128]{2,1,0:T(8,128)(2,1)} %get-tuple-element.19.dq_ref, bf16[4,64,128]{2,1,0:T(8,128)(2,1)} %get-tuple-element.20.kr0_ref, bf16[4,64,128]{2,1,0:T(8,128)(2,1)} %copy-done.8, bf16[1024,128]{1,0:T(8,128)(2,1)} %get-tuple-element.22.l0_ref, bf16[1024,128]{1,0:T(8,128)(2,1)} %copy-done.3, ...), custom_call_target="tpu_custom_call" | custom-call | tf_op jit(solution)/shard_map/combine/pallas_call | solution.py:234
  126.5 4.5 %all-to-all-start.3 = ((bf16[4,592,128]{2,1,0:T(8,128)(2,1)}), bf16[4,592,128]{2,1,0:T(8,128)(2,1)S(1)}, u32[]{:S(2)}, u32[]{:S(2)}) async-start(bf16[4,592,128]{2,1,0:T(8,128)(2,1)} %combine.1), calls=%async_computation.3 | async-start | bytes 1212416 | tf_op jit(solution)/shard_map/all_to_all | solution.py:318
  130.9 8.5 %all-to-all-done.3.msg_ref = bf16[4,592,128]{2,1,0:T(8,128)(2,1)S(1)} async-done(((bf16[4,592,128]{2,1,0:T(8,128)(2,1)}), bf16[4,592,128]{2,1,0:T(8,128)(2,1)S(1)}, u32[]{:S(2)}, u32[]{:S(2)}) %all-to-all-start.3) | async-done | bytes 606240 | tf_op jit(solution)/shard_map/all_to_all | solution.py:318
  139.5 0.8 copy-done.1
  140.3 1.9 %unpack.1 = (bf16[128,1024]{1,0:T(8,128)(2,1)}, bf16[128,256]{1,0:T(8,128)(2,1)}, bf16[2,4,128,128]{3,2,1,0:T(8,128)(2,1)}, bf16[4,768]{1,0:T(4,128)(2,1)}, bf16[4,1024]{1,0:T(4,128)(2,1)}) custom-call(s32[1]{0:T(128)} %bitcast.where_ref, bf16[4,592,128]{2,1,0:T(8,128)(2,1)} %copy-done.1), custom_call_target="tpu_custom_call" | custom-call | tf_op jit(solution)/shard_map/unpack/pallas_call | solution.py:267
  142.2 34.4 %all_to_all.25 = bf16[8,128,128]{2,1,0:T(8,128)(2,1)S(1)} all-to-all(bf16[8,128,128]{2,1,0:T(8,128)(2,1)} %bitcast.21), channel_id=1, replica_groups=mesh['zl'=8,'core'=2,'zh'=2,'y'=4,'x'=4] {'zh','x'}, dimensions={0} | all-to-all | bytes 524288 | tf_op jit(solution)/shard_map/all_to_all | solution.py:320
  176.7 0.1 copy.20
  176.8 0.7 reshape.40
  (6 shorter events, 0.1 us)
Async XLA Ops:
  7.2 27.1 %collective-permute-start.1 = (bf16[128,512]{1,0:T(8,128)(2,1)}, bf16[128,512]{1,0:T(8,128)(2,1)S(1)}, u32[]{:S(2)}, u32[]{:S(2)}) collective-permute-start(bf16[128,512]{1,0:T(8,128)(2,1)} %bitcast.24), channel_id=1, source_target_pairs={{0,16},{16,0},{1,17},{17,1},{2,18},{18,2},{3,19},{19,3},{4,20},{20... | collective-permute-start | bytes 393224 | tf_op jit(solution)/shard_map/ppermute | solution.py:285
  24.0 10.3 %copy-start.6 = (bf16[1,128,512]{2,1,0:T(8,128)(2,1)S(1)}, bf16[1,128,512]{2,1,0:T(8,128)(2,1)}, u32[]{:S(2)}) copy-start(bf16[1,128,512]{2,1,0:T(8,128)(2,1)} %param.8) | copy-start | bytes 393220
  24.0 14.8 %all-to-all-start = ((bf16[4,608,128]{2,1,0:T(8,128)(2,1)}), bf16[4,608,128]{2,1,0:T(8,128)(2,1)S(1)}, u32[]{:S(2)}, u32[]{:S(2)}) async-start(bf16[4,608,128]{2,1,0:T(8,128)(2,1)} %pack.1), calls=%async_computation | async-start | bytes 1245184 | tf_op jit(solution)/shard_map/all_to_all | solution.py:300
  28.6 47.2 %all-gather.4.cloned.1.call-start = ((), (), s32[]{:S(2)}) async-start(), calls=%async_computation.5 | async-start | bytes 1310720 | tf_op jit(solution)/shard_map/all_gather | solution.py:297
  38.9 36.9 %copy-start = (bf16[4,608,128]{2,1,0:T(8,128)(2,1)}, bf16[4,608,128]{2,1,0:T(8,128)(2,1)S(1)}, u32[]{:S(2)}) copy-start(bf16[4,608,128]{2,1,0:T(8,128)(2,1)S(1)} %all-to-all-done.msg_ref) | copy-start | bytes 1867780
  39.7 33.8 %all-to-all-start.1 = ((bf16[16,64,128]{2,1,0:T(8,128)(2,1)}), bf16[16,64,128]{2,1,0:T(8,128)(2,1)S(1)}, u32[]{:S(2)}, u32[]{:S(2)}) async-start(bf16[16,64,128]{2,1,0:T(8,128)(2,1)} %broadcast_in_dim.14), calls=%async_computation.1 | async-start | bytes 524288 | tf_op jit(solution)/shard_map/all_to_all | solution.py:305
  50.0 25.8 %collective-permute-start = (bf16[4,80,128]{2,1,0:T(8,128)(2,1)S(1)}, bf16[4,80,128]{2,1,0:T(8,128)(2,1)S(1)}, u32[]{:S(2)}, u32[]{:S(2)}) collective-permute-start(bf16[4,80,128]{2,1,0:T(8,128)(2,1)S(1)} %slice.18), channel_id=1, source_target_pairs={{0,16},{16,0},{1,17},{17,1},{2,18},{18,2},{3,19},{19,3},{4,20},{20... | collective-permute-start | bytes 245768 | tf_op jit(solution)/shard_map/ppermute | solution.py:285
  75.8 0.6 copy-start.7
  86.4 3.6 %collective-permute-start.6 = (bf16[16,16,512]{2,1,0:T(8,128)(2,1)}, bf16[16,16,512]{2,1,0:T(8,128)(2,1)S(1)}, u32[]{:S(2)}, u32[]{:S(2)}) collective-permute-start(bf16[16,16,512]{2,1,0:T(8,128)(2,1)} %get-tuple-element.27), channel_id=1, source_target_pairs={{0,32},{32,0},{1,33},{33,1},{2,34},{34,2},{3,35},{35,3},{4,36},{36... | collective-permute-start | bytes 786440 | tf_op jit(solution)/shard_map/ppermute | solution.py:285
  90.0 7.2 %copy-start.11 = (bf16[1024,128]{1,0:T(8,128)(2,1)S(1)}, bf16[1024,128]{1,0:T(8,128)(2,1)}, u32[]{:S(2)}) copy-start(bf16[1024,128]{1,0:T(8,128)(2,1)} %get-tuple-element.23) | copy-start | bytes 786436
  90.0 17.7 %copy-start.12 = (bf16[4,64,128]{2,1,0:T(8,128)(2,1)S(1)}, bf16[4,64,128]{2,1,0:T(8,128)(2,1)}, u32[]{:S(2)}) copy-start(bf16[4,64,128]{2,1,0:T(8,128)(2,1)} %get-tuple-element.21) | copy-start | bytes 196612
  91.8 8.8 %copy-start.10 = (bf16[1024,128]{1,0:T(8,128)(2,1)S(1)}, bf16[1024,128]{1,0:T(8,128)(2,1)}, u32[]{:S(2)}) copy-start(bf16[1024,128]{1,0:T(8,128)(2,1)} %get-tuple-element.24) | copy-start | bytes 786436
  91.8 13.5 %copy-start.9 = (bf16[1024,128]{1,0:T(8,128)(2,1)S(1)}, bf16[1024,128]{1,0:T(8,128)(2,1)}, u32[]{:S(2)}) copy-start(bf16[1024,128]{1,0:T(8,128)(2,1)} %get-tuple-element.25) | copy-start | bytes 786436
  91.8 31.3 %all-to-all-start.2 = ((bf16[16,16,512]{2,1,0:T(8,128)(2,1)}), bf16[16,16,512]{2,1,0:T(8,128)(2,1)S(1)}, u32[]{:S(2)}, u32[]{:S(2)}) async-start(bf16[16,16,512]{2,1,0:T(8,128)(2,1)} %add_convert_fusion), calls=%async_computation.2 | async-start | bytes 524288 | tf_op jit(solution)/shard_map/all_to_all | solution.py:313
  97.2 25.9 %collective-permute-start.3 = (bf16[1024,128]{1,0:T(8,128)(2,1)S(1)}, bf16[1024,128]{1,0:T(8,128)(2,1)S(1)}, u32[]{:S(2)}, u32[]{:S(2)}) collective-permute-start(bf16[1024,128]{1,0:T(8,128)(2,1)S(1)} %copy-done.11), channel_id=1, source_target_pairs={{0,1},{1,0},{2,3},{3,2},{4,5},{5,4},{6,7},{7,6},{8,9},{9,8},{10,11... | collective-permute-start | bytes 786440 | tf_op jit(solution)/shard_map/ppermute | solution.py:285
  100.6 22.5 %collective-permute-start.4 = (bf16[1024,128]{1,0:T(8,128)(2,1)S(1)}, bf16[1024,128]{1,0:T(8,128)(2,1)S(1)}, u32[]{:S(2)}, u32[]{:S(2)}) collective-permute-start(bf16[1024,128]{1,0:T(8,128)(2,1)S(1)} %copy-done.10), channel_id=1, source_target_pairs={{0,2},{1,3},{2,0},{3,1},{4,6},{5,7},{6,4},{7,5},{8,10},{9,11},{10,... | collective-permute-start | bytes 786440 | tf_op jit(solution)/shard_map/ppermute | solution.py:285
  105.3 17.8 %collective-permute-start.5 = (bf16[1024,128]{1,0:T(8,128)(2,1)S(1)}, bf16[1024,128]{1,0:T(8,128)(2,1)S(1)}, u32[]{:S(2)}, u32[]{:S(2)}) collective-permute-start(bf16[1024,128]{1,0:T(8,128)(2,1)S(1)} %copy-done.9), channel_id=1, source_target_pairs={{0,3},{1,2},{2,1},{3,0},{4,7},{5,6},{6,5},{7,4},{8,11},{9,10},{10,... | collective-permute-start | bytes 786440 | tf_op jit(solution)/shard_map/ppermute | solution.py:285
  107.7 15.4 %collective-permute-start.2 = (bf16[4,64,128]{2,1,0:T(8,128)(2,1)S(1)}, bf16[4,64,128]{2,1,0:T(8,128)(2,1)S(1)}, u32[]{:S(2)}, u32[]{:S(2)}) collective-permute-start(bf16[4,64,128]{2,1,0:T(8,128)(2,1)S(1)} %copy-done.12), channel_id=1, source_target_pairs={{0,16},{16,0},{1,17},{17,1},{2,18},{18,2},{3,19},{19,3},{4,20},{20... | collective-permute-start | bytes 196616 | tf_op jit(solution)/shard_map/ppermute | solution.py:285
  123.1 0.6 copy-start.8
  123.1 0.7 copy-start.3
  123.1 0.8 copy-start.4
  123.1 0.9 copy-start.5
  123.1 0.9 copy-start.2
  126.5 13.0 %all-to-all-start.3 = ((bf16[4,592,128]{2,1,0:T(8,128)(2,1)}), bf16[4,592,128]{2,1,0:T(8,128)(2,1)S(1)}, u32[]{:S(2)}, u32[]{:S(2)}) async-start(bf16[4,592,128]{2,1,0:T(8,128)(2,1)} %combine.1), calls=%async_computation.3 | async-start | bytes 1212416 | tf_op jit(solution)/shard_map/all_to_all | solution.py:318
  139.5 0.8 copy-start.1
Sparse Core Ops, SparseCore 0:
  35.1 32.6 all-gather.3

commit v3 on v2

v3 whole, which is shorter than its diff:
```python
import math

import jax
import jax.numpy as jnp
from jax import lax
from jax.experimental import pallas as pl
from jax.experimental.pallas import tpu as pltpu
from jax.sharding import Mesh, PartitionSpec as P

rope_base = 500000.0
neg_large = -1e30
log2_e = 1.4426950408889634

NY = 4
GRP = 2
TOK = 128
HALF = NY * TOK
SEQ = 2 * HALF
HD = 128
RD = 32
HALF_RD = 16
NOPE = 96
RANK = 512
ROWS = 4
ZL = 8
CORE = 2
NZ = 2 * ZL
TEN = 4
Q0, G0, L0, K0, S0, W0, MSG = 0, 256, 512, 1024, 1088, 1104, 1120
KEY_K, KEY_S, KEY = 512, 768, 784
PASS_S, PASS = 576, 592
BL0, BK0, BW0, BACK = 256, 512, 640, 672
EK0, EW0, END = 128, 384, 448
BLK = 256

f32 = jnp.float32
bf16 = jnp.bfloat16


def dot(a, b, dims=((1,), (0,))):
    return lax.dot_general(a, b, (dims, ((), ())), preferred_element_type=f32)


def pack_kernel(q_ref, g_ref, kr_ref, lat_ref, wk_ref, wv_ref, pos_ref, out_ref, key_ref):
    rope_t = kr_ref[...].astype(f32).T.astype(bf16)
    pos = pos_ref[...]
    places = jnp.concatenate(
        [(pos >> 6).astype(f32), (pos & 63).astype(f32), jnp.zeros((14, TOK), f32)], 0
    ).astype(bf16)
    for b in range(RANK // HD):
        key_ref[b * TOK:(b + 1) * TOK, :] = lat_ref[:, b * HD:(b + 1) * HD]
    key_ref[KEY_K:KEY_S, :] = rope_t
    key_ref[KEY_S:KEY, :] = places
    wk = wk_ref[...].astype(f32)
    wv = wv_ref[...].astype(f32)
    for y in range(NY):
        parts_k = []
        parts_v = []
        for g in range(GRP):
            h = y * GRP + g
            cols = slice(h * HD, (h + 1) * HD)
            out_ref[y, Q0 + g * TOK:Q0 + (g + 1) * TOK, :] = q_ref[:, cols]
            out_ref[y, G0 + g * TOK:G0 + (g + 1) * TOK, :] = g_ref[:, cols]
            parts_v.append(wv[:, cols])
            parts_k.append(
                jnp.concatenate([jnp.zeros((ROWS, RD), f32), wk[:, h * NOPE:(h + 1) * NOPE]], 1)
            )
        for b in range(RANK // HD):
            out_ref[y, L0 + b * TOK:L0 + (b + 1) * TOK, :] = lat_ref[:, b * HD:(b + 1) * HD]
        out_ref[y, K0:S0, :] = rope_t[y * GRP * RD:(y + 1) * GRP * RD, :]
        out_ref[y, S0:W0, :] = places
        out_ref[y, W0:MSG, :] = jnp.concatenate(parts_k + parts_v, 0).astype(bf16)


def pack(*parts):
    return pl.pallas_call(
        pack_kernel,
        out_shape=[
            jax.ShapeDtypeStruct((NY, MSG, HD), bf16),
            jax.ShapeDtypeStruct((KEY, HD), bf16),
        ],
        name="pack",
    )(*parts)


def spread_kernel(msg_ref, w_ref):
    tails = [msg_ref[y].astype(f32) for y in range(NY)]
    rows = [tails[y][c * ROWS:(c + 1) * ROWS] for c in range(2 * GRP) for y in range(NY)]
    block = jnp.concatenate(rows, 0).astype(bf16)
    for z in range(NZ):
        w_ref[z] = block


def spread(msg):
    return pl.pallas_call(
        spread_kernel,
        grid=(1,),
        in_specs=[pl.BlockSpec((NY, MSG - W0, HD), lambda i: (0, W0 // (MSG - W0), 0))],
        out_specs=pl.BlockSpec(memory_space=pltpu.VMEM),
        out_shape=jax.ShapeDtypeStruct((NZ, 2 * GRP * NY * ROWS, HD), bf16),
        name="spread",
    )(msg)


def relay_kernel(where_ref, key_ref, *out_refs):
    own_y = where_ref[2]
    for t, ref in enumerate(out_refs):
        rows = KEY_K + (own_y ^ t) * (GRP * RD)
        ref[0:KEY_K, :] = key_ref[0:KEY_K, :]
        ref[KEY_K:PASS_S, :] = key_ref[pl.ds(pl.multiple_of(rows, GRP * RD), GRP * RD), :]
        ref[PASS_S:PASS, :] = key_ref[KEY_S:KEY, :]


def relay(place, other):
    return pl.pallas_call(
        relay_kernel,
        in_specs=[
            pl.BlockSpec(memory_space=pltpu.SMEM),
            pl.BlockSpec(memory_space=pltpu.VMEM),
        ],
        out_shape=[jax.ShapeDtypeStruct((PASS, HD), bf16)] * NY,
        cost_estimate=pl.CostEstimate(flops=50_000_000_000, transcendentals=0, bytes_accessed=150_000_000),
        name="relay",
    )(place, other)


def main_kernel(
    where_ref, freq_ref, msg_ref, key0_ref, key1_ref, key2_ref, key3_ref, w_ref,
    dq_ref, dkr_ref, dl0_ref, dl1_ref, dl2_ref, dl3_ref, dw_own_ref, dw_other_ref,
    lat_s, w_s, k_s, kt_s, q_s, qt_s, v_s, gt_s, pos_s, rope_s, cos_s, sin_s, dkv_s, dqt_s, dw_s,
):
    core = where_ref[0]
    x = where_ref[1]
    own_y = where_ref[2]
    def take(read, lat0, rope0, pos0, tokens):
        for b in range(RANK // HD):
            lat_s[tokens, b * HD:(b + 1) * HD] = read(lat0 + b * TOK, TOK)
        rope_s[:, tokens] = read(rope0, GRP * RD).astype(f32)
        tail = read(pos0, 16).astype(f32)
        pos_s[0:1, tokens] = tail[0:1] * 64.0 + tail[1:2]

    for y in range(NY):
        take(
            lambda r, n, y=y: msg_ref[y, r:r + n, :], L0, K0, S0,
            slice(y * TOK, (y + 1) * TOK),
        )
    for t, ref in enumerate((key0_ref, key1_ref, key2_ref, key3_ref)):
        tokens = pl.ds(pl.multiple_of((NY + (own_y ^ t)) * TOK, TOK), TOK)
        take(lambda r, n, ref=ref: ref[r:r + n, :], 0, KEY_K, PASS_S, tokens)
    for z in range(NZ):
        for c in range(CORE):
            r = ((z // 2) * CORE + c) * 32 + (z % 2) * 16
            for kind in range(2 * GRP):
                w_s[r:r + 16, kind * HD:(kind + 1) * HD] = w_ref[c, z, kind * 16:(kind + 1) * 16, :]
    pos_row = pos_s[0:1, :]
    freq = freq_ref[...].astype(f32)
    heads = lax.broadcasted_iota(jnp.int32, freq.shape, 0)
    diagonal = lax.broadcasted_iota(jnp.int32, (HALF_RD, HALF_RD), 0) == lax.broadcasted_iota(
        jnp.int32, (HALF_RD, HALF_RD), 1
    )
    columns = []
    for g in range(GRP):
        row = jnp.sum(jnp.where(heads == own_y * GRP + g, freq, 0.0), 0, keepdims=True)
        columns.append(jnp.sum(jnp.where(diagonal, row, 0.0), 1, keepdims=True))
    inverse = jnp.exp(jnp.concatenate(columns, 0) * (-2.0 / HD * math.log(rope_base)))
    angles = inverse * pos_row
    cos_s[...] = jnp.cos(angles)
    sin_s[...] = jnp.sin(angles)
    pos_col = jnp.broadcast_to(pos_row, (8, SEQ)).T[:, 0:1]
    scale = HD ** -0.5
    kv = dot(lat_s[...], w_s[...])
    dkv_s[...] = jnp.zeros_like(dkv_s)

    for g in range(GRP):
        cos = cos_s[g * HALF_RD:(g + 1) * HALF_RD, :]
        sin = sin_s[g * HALF_RD:(g + 1) * HALF_RD, :]

        def rot(a, width):
            a, b = a[:HALF_RD], a[HALF_RD:RD]
            c, s = cos[:, :width], sin[:, :width]
            return jnp.concatenate([a * c - b * s, b * c + a * s], 0)

        def unrot(a, width):
            a, b = a[:HALF_RD], a[HALF_RD:RD]
            c, s = cos[:, :width], sin[:, :width]
            return jnp.concatenate([a * c + b * s, b * c - a * s], 0)

        kr = rot(rope_s[g * RD:(g + 1) * RD, :], SEQ)
        kr_pad = jnp.concatenate([kr, jnp.zeros((HD - RD, SEQ), f32)], 0)
        k = kv[:, g * HD:(g + 1) * HD] + kr_pad.T
        k_s[...] = k.astype(bf16)
        kt_s[...] = k.T.astype(bf16)
        v_s[...] = kv[:, (GRP + g) * HD:(GRP + g + 1) * HD].astype(bf16)
        for c in range(NY):
            cols = slice(c * TOK, (c + 1) * TOK)
            qt_s[:, cols] = msg_ref[c, Q0 + g * TOK:Q0 + (g + 1) * TOK, :].astype(f32).T
            gt_s[:, cols] = msg_ref[c, G0 + g * TOK:G0 + (g + 1) * TOK, :].astype(f32).T.astype(bf16)
        qt_s[0:RD, :] = rot(qt_s[0:RD, :], HALF)
        qt = qt_s[...]
        q_s[...] = qt.T.astype(bf16)

        for b in range(HALF // BLK):
            cols = slice(b * BLK, (b + 1) * BLK)
            st = dot(k_s[...], qt[:, cols].astype(bf16))
            visible = pos_col <= pos_row[:, cols]
            st = jnp.where(visible, st * (scale * log2_e), neg_large)
            top = jnp.max(st, 0, keepdims=True)
            e = jnp.exp2(st - top)
            dp = dot(v_s[...], gt_s[:, cols])
            total = jnp.sum(e, 0, keepdims=True)
            weighted = jnp.sum(e * dp, 0, keepdims=True)
            inv_total = 1.0 / total
            delta = weighted * inv_total
            probs = (e * inv_total).astype(bf16)
            ds = (scale * probs.astype(f32) * (dp - delta)).astype(bf16)
            dqt_s[:, cols] = dot(kt_s[...], ds)
            dkv_s[:, g * HD:(g + 1) * HD] += dot(ds, q_s[cols, :])
            grad = jnp.concatenate(
                [
                    msg_ref[c, G0 + g * TOK:G0 + (g + 1) * TOK, :]
                    for c in range(b * BLK // TOK, (b + 1) * BLK // TOK)
                ],
                0,
            )
            dkv_s[:, (GRP + g) * HD:(GRP + g + 1) * HD] += dot(probs, grad)

        dqt_s[0:RD, :] = unrot(dqt_s[0:RD, :], HALF)
        dq = dqt_s[...].T.astype(bf16)
        dkr = unrot(dkv_s[:, g * HD:(g + 1) * HD].T[0:RD, :], SEQ).astype(bf16)
        for c in range(NY):
            cols = slice(c * TOK, (c + 1) * TOK)
            dq_ref[c, g * TOK:(g + 1) * TOK, :] = dq[cols, :]
            for z in range(2):
                rows = slice((z * GRP + g) * RD, (z * GRP + g + 1) * RD)
                dkr_ref[c, rows, :] = dkr[:, z * HALF + c * TOK:z * HALF + (c + 1) * TOK]

    dkv = dkv_s[...].astype(bf16)
    for t, ref in enumerate((dl0_ref, dl1_ref, dl2_ref, dl3_ref)):
        rows = pl.ds(pl.multiple_of((x ^ t) * HD, HD), HD)
        ref[...] = dot(dkv, w_s[rows, :], ((1,), (1,))).astype(bf16)
    dw_s[...] = dot(lat_s[...], dkv, ((0,), (0,)))
    for z in range(ZL):
        own = pl.ds(pl.multiple_of((z * CORE + core) * 32, 32), 32)
        other = pl.ds(pl.multiple_of((z * CORE + 1 - core) * 32, 32), 32)
        dw_own_ref[z] = dw_s[own, :].astype(bf16)
        dw_other_ref[z] = dw_s[other, :].astype(bf16)


def attention(place, freq, msg, keys, w):
    smem = pl.BlockSpec(memory_space=pltpu.SMEM)
    vmem = pl.BlockSpec(memory_space=pltpu.VMEM)
    rope = jax.ShapeDtypeStruct((NY, 2 * GRP * RD, TOK), bf16)
    quarter = jax.ShapeDtypeStruct((SEQ, HD), bf16)
    weight = jax.ShapeDtypeStruct((ZL, 32, 2 * GRP * HD), bf16)
    return pl.pallas_call(
        main_kernel,
        in_specs=[smem] + [vmem] * 7,
        out_specs=[vmem] * 8,
        out_shape=[jax.ShapeDtypeStruct((NY, GRP * TOK, HD), bf16), rope]
        + [quarter] * 4
        + [weight, weight],
        scratch_shapes=[
            pltpu.VMEM((SEQ, RANK), bf16),
            pltpu.VMEM((RANK, 2 * GRP * HD), bf16),
            pltpu.VMEM((SEQ, HD), bf16),
            pltpu.VMEM((HD, SEQ), bf16),
            pltpu.VMEM((HALF, HD), bf16),
            pltpu.VMEM((HD, HALF), f32),
            pltpu.VMEM((SEQ, HD), bf16),
            pltpu.VMEM((HD, HALF), bf16),
            pltpu.VMEM((8, SEQ), f32),
            pltpu.VMEM((GRP * RD, SEQ), f32),
            pltpu.VMEM((GRP * HALF_RD, SEQ), f32),
            pltpu.VMEM((GRP * HALF_RD, SEQ), f32),
            pltpu.VMEM((SEQ, 2 * GRP * HD), f32),
            pltpu.VMEM((HD, HALF), f32),
            pltpu.VMEM((RANK, 2 * GRP * HD), f32),
        ],
        compiler_params=pltpu.CompilerParams(vmem_limit_bytes=56 * 1024 * 1024),
        name="attention_backward",
    )(place, freq, msg, *keys, w)


def combine_kernel(dq_ref, kr_ref, l0_ref, l1_ref, l2_ref, l3_ref, dw_ref, out_ref):
    dw = jnp.sum(dw_ref[...].astype(f32), 0)
    for y in range(NY):
        out_ref[y, 0:BL0, :] = dq_ref[y]
        out_ref[y, BK0:BW0, :] = kr_ref[y]
        for z in range(2):
            rows = slice((z * NY + y) * TOK, (z * NY + y + 1) * TOK)
            lat = (l0_ref[rows, :].astype(f32) + l1_ref[rows, :].astype(f32)) + (
                l2_ref[rows, :].astype(f32) + l3_ref[rows, :].astype(f32)
            )
            out_ref[y, BL0 + z * TOK:BL0 + (z + 1) * TOK, :] = lat.astype(bf16)
        for z in range(2):
            part = dw[z * 16 + y * ROWS:z * 16 + (y + 1) * ROWS, :]
            out_ref[y, BW0 + z * 16:BW0 + (z + 1) * 16, :] = jnp.concatenate(
                [part[:, c * HD:(c + 1) * HD] for c in range(2 * GRP)], 0
            ).astype(bf16)


def combine(*parts):
    return pl.pallas_call(
        combine_kernel,
        out_shape=jax.ShapeDtypeStruct((NY, BACK, HD), bf16),
        name="combine",
    )(*parts)


def halves_kernel(where_ref, msg_ref, own_ref, other_ref):
    half = where_ref[3]
    for z, ref in enumerate((own_ref, other_ref)):
        lat = sum(
            msg_ref[y, BL0 + z * TOK:BL0 + (z + 1) * TOK, :].astype(f32) for y in range(NY)
        )
        ref[0:TOK, :] = lat.astype(bf16)
        weights = pl.ds(pl.multiple_of(BW0 + (half ^ z) * 16, 16), 16)
        for y in range(NY):
            rows = slice(EK0 + y * GRP * RD, EK0 + (y + 1) * GRP * RD)
            ref[rows, :] = msg_ref[y, BK0 + z * GRP * RD:BK0 + (z + 1) * GRP * RD, :]
            ref[EW0 + y * 16:EW0 + (y + 1) * 16, :] = msg_ref[y, weights, :]


def halves(place, msg):
    part = jax.ShapeDtypeStruct((END, HD), bf16)
    return pl.pallas_call(
        halves_kernel,
        in_specs=[
            pl.BlockSpec(memory_space=pltpu.SMEM),
            pl.BlockSpec(memory_space=pltpu.VMEM),
        ],
        out_shape=[part, part],
        name="halves",
    )(place, msg)


def unpack_kernel(msg_ref, q_ref):
    for y in range(NY):
        for g in range(GRP):
            h = y * GRP + g
            q_ref[:, h * HD:(h + 1) * HD] = msg_ref[y, g * TOK:(g + 1) * TOK, :]


def unpack(msg):
    return pl.pallas_call(
        unpack_kernel,
        out_shape=jax.ShapeDtypeStruct((TOK, NY * GRP * HD), bf16),
        name="unpack",
    )(msg)


def finish_kernel(own_ref, other_ref, lat_ref, kr_ref, wk_ref, wv_ref):
    both = own_ref[...].astype(f32) + other_ref[...].astype(f32)
    lat = both[0:TOK].astype(bf16)
    for t in range(TEN):
        lat_ref[t] = lat
    kr_ref[...] = both[EK0:EW0].T.astype(bf16)
    wk = []
    wv = []
    for y in range(NY):
        tail = both[EW0 + y * 16:EW0 + (y + 1) * 16]
        for g in range(GRP):
            wk.append(tail[g * ROWS:(g + 1) * ROWS, RD:])
            wv.append(tail[(GRP + g) * ROWS:(GRP + g + 1) * ROWS])
    wk_ref[...] = jnp.concatenate(wk, 1).astype(bf16)
    wv_ref[...] = jnp.concatenate(wv, 1).astype(bf16)


def finish(own, other):
    return pl.pallas_call(
        finish_kernel,
        out_shape=[
            jax.ShapeDtypeStruct((TEN, TOK, HD), bf16),
            jax.ShapeDtypeStruct((TOK, NY * GRP * RD), bf16),
            jax.ShapeDtypeStruct((ROWS, NY * GRP * NOPE), bf16),
            jax.ShapeDtypeStruct((ROWS, NY * GRP * HD), bf16),
        ],
        name="finish",
    )(own, other)


def swap(array, axis, size, flip):
    return lax.ppermute(array, axis, [(i, i ^ flip) for i in range(size)])


def body(latent, key_rope, query, out_grad, positions, freq_index, up_key, up_value):
    place = jnp.stack([lax.axis_index(a).astype(jnp.int32) for a in ("core", "x", "y", "zh")])

    msg, own = pack(query[0], out_grad[0], key_rope[0], latent[0], up_key, up_value, positions)
    other = swap(own, "zh", 2, 1)
    msg = lax.all_to_all(msg, "y", 0, 0)
    w = lax.all_to_all(spread(msg), ("zl", "zh"), 0, 0)
    keys = relay(place, other)
    keys = [keys[0]] + [swap(keys[t], "y", NY, t) for t in range(1, NY)]
    w = lax.all_gather(w, "core", axis=0)

    dq, dkr, l0, l1, l2, l3, dw_own, dw_other = attention(place, freq_index, msg, keys, w)

    dw = dw_own.astype(f32) + swap(dw_other, "core", 2, 1).astype(f32)
    dw = lax.all_to_all(dw.astype(bf16), "zl", 0, 0)
    l1 = swap(l1, "x", TEN, 1)
    l2 = swap(l2, "x", TEN, 2)
    l3 = swap(l3, "x", TEN, 3)
    back = lax.all_to_all(combine(dq, dkr, l0, l1, l2, l3, dw), "y", 0, 0)
    own, other = halves(place, back)
    quarter, key_rope_grad, up_key_grad, up_value_grad = finish(own, swap(other, "zh", 2, 1))
    query_grad = unpack(back)
    quarters = lax.all_to_all(quarter, "x", 0, 0)
    latent_grad = quarters.transpose(1, 0, 2).reshape(1, TOK, RANK)
    return (query_grad[None], key_rope_grad[None], latent_grad, up_key_grad, up_value_grad)


def solution(mesh):
    split = Mesh(mesh.devices.reshape(ZL, CORE, 2, NY, TEN), ("zl", "core", "zh", "y", "x"))
    dp, context, tensor = ("zl", "core"), ("zh", "y"), "x"
    return jax.shard_map(
        body,
        mesh=split,
        in_specs=(
            P(dp, context, None),
            P(dp, context, tensor),
            P(dp, context, tensor),
            P(dp, context, tensor),
            P(dp, context),
            P(tensor, None),
            P(dp + context, tensor),
            P(dp + context, tensor),
        ),
        out_specs=(
            P(dp, context, tensor),
            P(dp, context, tensor),
            P(dp, context, None),
            P(dp + context, tensor),
            P(dp + context, tensor),
        ),
        check_vma=False,
    )
```

time: 185 us -> 162 us (0.88)
  the two profiles are of different devices: /device:TPU:32 before, /device:TPU:160 now
where the time goes in v3:
time: 162 us; the launch traced here: 161 us
  starting transfers between devices  72.7 us (45%)
  waiting for transfers between devices  39.1 us (24%)
  Pallas kernels  23.5 us (15%)
  blocking collectives  17.9 us (11%)
  local copies, waits for them, and re-layouts  4.7 us (3%)
  other arithmetic  2.33 us (1%)
    ppermute x9, starting transfers between devices, swap(): return lax.ppermute(array, axis, [(i, i ^ flip) for i in range(size)])  41.5 us
    ppermute x9, waiting for transfers between devices, swap(): return lax.ppermute(array, axis, [(i, i ^ flip) for i in range(size)])  27.6 us
    all_to_all x1, blocking collectives, body(): back = lax.all_to_all(combine(dq, dkr, l0, l1, l2, l3, dw), 'y', 0, 0)  15.6 us
    all_to_all x1, starting transfers between devices, body(): w = lax.all_to_all(spread(msg), ('zl', 'zh'), 0, 0)  13.4 us
    pallas_call x1, Pallas kernels, attention(): pl.pallas_call(main_kernel, in_specs=[smem] + [vmem] * 7, out_specs=[vmem...  10 us
    all_to_all x1, starting transfers between devices, body(): dw = lax.all_to_all(dw.astype(bf16), 'zl', 0, 0)  9.91 us
    all_to_all x1, waiting for transfers between devices, body(): msg = lax.all_to_all(msg, 'y', 0, 0)  5.5 us
    all_to_all x1, starting transfers between devices, body(): msg = lax.all_to_all(msg, 'y', 0, 0)  4.6 us
  transfers between devices with their start and end apart: 13, of which 9 were waited for; matrix products, arithmetic and copies ran while one was open for 0% of the time, Pallas kernels for 3%

profile of v3, /device:TPU:160, one launch (start us, length us, event | category | flops | bytes accessed | tf_op | source)
XLA Modules:
  0.0 161.1 jit_solution(1778119978495417439)
XLA Ops:
  0.6 2.4 %pack.1 = (bf16[4,1120,128]{2,1,0:T(8,128)(2,1)}, bf16[784,128]{1,0:T(8,128)(2,1)}) custom-call(bf16[128,1024]{1,0:T(8,128)(2,1)} %bitcast.16, bf16[128,1024]{1,0:T(8,128)(2,1)} %bitcast.17, bf16[128,256]{1,0:T(8,128)(2,1)} %bitcast.20, bf16[128,512]{1,0:T(8,128)(2,1)} %bitcast.19, bf16[4,768]{1,0:T(4,128)(2,1)} %wk_ref.1, bf16[4,1024]{1,0:T(4,128)(2,1)} %wv_ref.1, ...), custom_call_target="tpu_custom_call" | custom-call | tf_op jit(solution)/shard_map/pack/pallas_call | solution.py:76
  3.0 4.6 %all-to-all-start = ((bf16[4,1120,128]{2,1,0:T(8,128)(2,1)}), bf16[4,1120,128]{2,1,0:T(8,128)(2,1)S(1)}, u32[]{:S(2)}, u32[]{:S(2)}) async-start(bf16[4,1120,128]{2,1,0:T(8,128)(2,1)} %get-tuple-element.25), calls=%async_computation | async-start | bytes 2293760 | tf_op jit(solution)/shard_map/all_to_all | solution.py:391
  7.6 0.0 copy-done.12
  7.6 10.0 %collective-permute-start = (bf16[784,128]{1,0:T(8,128)(2,1)S(1)}, bf16[784,128]{1,0:T(8,128)(2,1)S(1)}, u32[]{:S(2)}, u32[]{:S(2)}) collective-permute-start(bf16[784,128]{1,0:T(8,128)(2,1)S(1)} %copy-done.12), channel_id=1, source_target_pairs={{0,16},{16,0},{1,17},{17,1},{2,18},{18,2},{3,19},{19,3},{4,20},{20... | collective-permute-start | bytes 602120 | tf_op jit(solution)/shard_map/ppermute | solution.py:383
  17.6 0.6 pad_add_fusion.where_ref
  18.3 5.5 %all-to-all-done.msg_ref = bf16[4,1120,128]{2,1,0:T(8,128)(2,1)S(1)} async-done(((bf16[4,1120,128]{2,1,0:T(8,128)(2,1)}), bf16[4,1120,128]{2,1,0:T(8,128)(2,1)S(1)}, u32[]{:S(2)}, u32[]{:S(2)}) %all-to-all-start) | async-done | bytes 1146912 | tf_op jit(solution)/shard_map/all_to_all | solution.py:391
  23.8 0.0 copy-start
  23.8 1.0 copy-done
  24.8 1.4 spread.1
  26.2 13.4 %all-to-all-start.1 = ((bf16[16,64,128]{2,1,0:T(8,128)(2,1)}), bf16[16,64,128]{2,1,0:T(8,128)(2,1)S(1)}, u32[]{:S(2)}, u32[]{:S(2)}) async-start(bf16[16,64,128]{2,1,0:T(8,128)(2,1)} %spread.1), calls=%async_computation.1 | async-start | bytes 524288 | tf_op jit(solution)/shard_map/all_to_all | solution.py:392
  39.6 0.0 collective-permute-done.key_ref
  39.6 0.0 copy-start.13
  39.6 0.7 copy-done.13
  40.3 1.8 %relay.1 = (bf16[592,128]{1,0:T(8,128)(2,1)}, bf16[592,128]{1,0:T(8,128)(2,1)}, bf16[592,128]{1,0:T(8,128)(2,1)}, bf16[592,128]{1,0:T(8,128)(2,1)}) custom-call(s32[4]{0:T(128)} %pad_add_fusion.where_ref, bf16[784,128]{1,0:T(8,128)(2,1)} %copy-done.13), custom_call_target="tpu_custom_call" | custom-call | flops 49999998976 | bytes 150000000 | tf_op jit(solution)/shard_map/relay/pallas_call | solution.py:115
  42.2 2.5 %collective-permute-start.1 = (bf16[592,128]{1,0:T(8,128)(2,1)}, bf16[592,128]{1,0:T(8,128)(2,1)S(1)}, u32[]{:S(2)}, u32[]{:S(2)}) collective-permute-start(bf16[592,128]{1,0:T(8,128)(2,1)} %get-tuple-element.28), channel_id=1, source_target_pairs={{0,4},{4,0},{8,12},{12,8},{1,5},{5,1},{9,13},{13,9},{2,6},{6,2},{1... | collective-permute-start | bytes 454664 | tf_op jit(solution)/shard_map/ppermute | solution.py:383
  44.6 4.0 %collective-permute-start.2 = (bf16[592,128]{1,0:T(8,128)(2,1)}, bf16[592,128]{1,0:T(8,128)(2,1)S(1)}, u32[]{:S(2)}, u32[]{:S(2)}) collective-permute-start(bf16[592,128]{1,0:T(8,128)(2,1)} %get-tuple-element.29), channel_id=1, source_target_pairs={{0,8},{4,12},{8,0},{12,4},{1,9},{5,13},{9,1},{13,5},{2,10},{6,14},... | collective-permute-start | bytes 454664 | tf_op jit(solution)/shard_map/ppermute | solution.py:383
  48.6 4.0 %collective-permute-start.3 = (bf16[592,128]{1,0:T(8,128)(2,1)}, bf16[592,128]{1,0:T(8,128)(2,1)S(1)}, u32[]{:S(2)}, u32[]{:S(2)}) collective-permute-start(bf16[592,128]{1,0:T(8,128)(2,1)} %get-tuple-element.30), channel_id=1, source_target_pairs={{0,12},{4,8},{8,4},{12,0},{1,13},{5,9},{9,5},{13,1},{2,14},{6,10},... | collective-permute-start | bytes 454664 | tf_op jit(solution)/shard_map/ppermute | solution.py:383
  52.6 1.9 %all-to-all-done.1 = bf16[16,64,128]{2,1,0:T(8,128)(2,1)S(1)} async-done(((bf16[16,64,128]{2,1,0:T(8,128)(2,1)}), bf16[16,64,128]{2,1,0:T(8,128)(2,1)S(1)}, u32[]{:S(2)}, u32[]{:S(2)}) %all-to-all-start.1) | async-done | bytes 262176 | tf_op jit(solution)/shard_map/all_to_all | solution.py:392
  54.5 2.3 %all-gather = bf16[32,64,128]{2,1,0:T(8,128)(2,1)} all-gather(bf16[16,64,128]{2,1,0:T(8,128)(2,1)S(1)} %all-to-all-done.1), channel_id=2, replica_groups=mesh['zl'=8,'core'=2,'zh'=2,'y'=4,'x'=4] {'core'}, dimensions={0}, use_global_device_ids=true | all-gather | bytes 786432 | tf_op jit(solution)/shard_map/all_gather | solution.py:395
  56.8 0.0 collective-permute-done.1.key1_ref
  56.8 0.0 collective-permute-done.2.key2_ref
  56.8 0.0 copy-start.6
  56.8 0.3 collective-permute-done.3.key3_ref
  57.1 0.0 copy-start.7
  57.1 0.4 copy-done.5
  57.5 0.0 copy-done.6
  57.5 0.2 copy-done.7
  57.8 10.0 %attention_backward.1 = (bf16[4,256,128]{2,1,0:T(8,128)(2,1)}, bf16[4,128,128]{2,1,0:T(8,128)(2,1)}, bf16[1024,128]{1,0:T(8,128)(2,1)}, bf16[1024,128]{1,0:T(8,1...) custom-call(s32[4]{0:T(128)} %pad_add_fusion.where_ref, ...), custom_call_target="tpu_custom_call" | custom-call | tf_op jit(solution)/shard_map/attention_backward/pallas_call | solution.py:255
  67.8 0.0 copy-start.11
  67.8 0.0 copy-start.10
  67.8 0.0 copy-start.9
  67.8 2.1 %collective-permute-start.7 = (bf16[8,32,512]{2,1,0:T(8,128)(2,1)}, bf16[8,32,512]{2,1,0:T(8,128)(2,1)S(1)}, u32[]{:S(2)}, u32[]{:S(2)}) collective-permute-start(bf16[8,32,512]{2,1,0:T(8,128)(2,1)} %get-tuple-element.38), channel_id=1, source_target_pairs={{0,32},{32,0},{1,33},{33,1},{2,34},{34,2},{3,35},{35,3},{4,36},{36... | collective-permute-start | bytes 786440 | tf_op jit(solution)/shard_map/ppermute | solution.py:383
  69.9 1.7 %collective-permute-done.7 = bf16[8,32,512]{2,1,0:T(8,128)(2,1)S(1)} collective-permute-done((bf16[8,32,512]{2,1,0:T(8,128)(2,1)}, bf16[8,32,512]{2,1,0:T(8,128)(2,1)S(1)}, u32[]{:S(2)}, u32[]{:S(2)}) %collective-permute-start.7) | collective-permute-done | bytes 262176 | tf_op jit(solution)/shard_map/ppermute | solution.py:383
  71.6 1.7 %add_convert_fusion = bf16[8,32,512]{2,1,0:T(8,128)(2,1)} fusion(bf16[8,32,512]{2,1,0:T(8,128)(2,1)S(1)} %collective-permute-done.7, bf16[8,32,512]{2,1,0:T(8,128)(2,1)} %get-tuple-element.37), kind=kLoop, calls=%fused_computation | loop fusion | flops 524288 | bytes 786432 | tf_op jit(solution)/shard_map/convert_element_type | solution.py:400
  73.3 9.9 %all-to-all-start.2 = ((bf16[8,32,512]{2,1,0:T(8,128)(2,1)}), bf16[8,32,512]{2,1,0:T(8,128)(2,1)S(1)}, u32[]{:S(2)}, u32[]{:S(2)}) async-start(bf16[8,32,512]{2,1,0:T(8,128)(2,1)} %add_convert_fusion), calls=%async_computation.2 | async-start | bytes 524288 | tf_op jit(solution)/shard_map/all_to_all | solution.py:400
  83.2 0.0 copy-done.11
  83.2 3.4 %collective-permute-start.4 = (bf16[1024,128]{1,0:T(8,128)(2,1)S(1)}, bf16[1024,128]{1,0:T(8,128)(2,1)S(1)}, u32[]{:S(2)}, u32[]{:S(2)}) collective-permute-start(bf16[1024,128]{1,0:T(8,128)(2,1)S(1)} %copy-done.11), channel_id=1, source_target_pairs={{0,1},{1,0},{2,3},{3,2},{4,5},{5,4},{6,7},{7,6},{8,9},{9,8},{10,11... | collective-permute-start | bytes 786440 | tf_op jit(solution)/shard_map/ppermute | solution.py:383
  86.6 0.0 copy-done.10
  86.6 4.6 %collective-permute-start.5 = (bf16[1024,128]{1,0:T(8,128)(2,1)S(1)}, bf16[1024,128]{1,0:T(8,128)(2,1)S(1)}, u32[]{:S(2)}, u32[]{:S(2)}) collective-permute-start(bf16[1024,128]{1,0:T(8,128)(2,1)S(1)} %copy-done.10), channel_id=1, source_target_pairs={{0,2},{1,3},{2,0},{3,1},{4,6},{5,7},{6,4},{7,5},{8,10},{9,11},{10,... | collective-permute-start | bytes 786440 | tf_op jit(solution)/shard_map/ppermute | solution.py:383
  91.3 0.0 copy-done.9
  91.3 2.4 %collective-permute-start.6 = (bf16[1024,128]{1,0:T(8,128)(2,1)S(1)}, bf16[1024,128]{1,0:T(8,128)(2,1)S(1)}, u32[]{:S(2)}, u32[]{:S(2)}) collective-permute-start(bf16[1024,128]{1,0:T(8,128)(2,1)S(1)} %copy-done.9), channel_id=1, source_target_pairs={{0,3},{1,2},{2,1},{3,0},{4,7},{5,6},{6,5},{7,4},{8,11},{9,10},{10,... | collective-permute-start | bytes 786440 | tf_op jit(solution)/shard_map/ppermute | solution.py:383
  93.7 0.7 collective-permute-done.4.l1_ref
  94.3 0.0 copy-start.2
  94.3 6.5 %collective-permute-done.5.l2_ref = bf16[1024,128]{1,0:T(8,128)(2,1)S(1)} collective-permute-done((bf16[1024,128]{1,0:T(8,128)(2,1)S(1)}, bf16[1024,128]{1,0:T(8,128)(2,1)S(1)}, u32[]{:S(2)}, u32[]{:S(2)}) %collective-permute-start.5) | collective-permute-done | bytes 262176 | tf_op jit(solution)/shard_map/ppermute | solution.py:383
  100.8 0.0 copy-start.3
  100.8 5.2 %collective-permute-done.6.l3_ref = bf16[1024,128]{1,0:T(8,128)(2,1)S(1)} collective-permute-done((bf16[1024,128]{1,0:T(8,128)(2,1)S(1)}, bf16[1024,128]{1,0:T(8,128)(2,1)S(1)}, u32[]{:S(2)}, u32[]{:S(2)}) %collective-permute-start.6) | collective-permute-done | bytes 262176 | tf_op jit(solution)/shard_map/ppermute | solution.py:383
  106.0 0.0 copy-start.4
  106.0 0.0 all-to-all-done.2.dw_ref
  106.0 0.0 copy-done.2
  106.1 0.0 copy-done.3
  106.1 0.7 copy-done.4
  106.7 0.1 copy-done.1
  106.9 2.4 %combine.1 = bf16[4,672,128]{2,1,0:T(8,128)(2,1)} custom-call(bf16[4,256,128]{2,1,0:T(8,128)(2,1)} %get-tuple-element.31.dq_ref, bf16[4,128,128]{2,1,0:T(8,128)(2,1)} %get-tuple-element.32.kr_ref, bf16[1024,128]{1,0:T(8,128)(2,1)} %get-tuple-element.33.l0_ref, bf16[1024,128]{1,0:T(8,128)(2,1)} %copy-done.2, bf16[1024,128]{1,0:T(8,128)(2,1)} %copy-done.3, ...), custom_call_target="tpu_custom_call" | custom-call | tf_op jit(solution)/shard_map/combine/pallas_call | solution.py:303
  109.3 15.6 %all_to_all.25.msg_ref = bf16[4,672,128]{2,1,0:T(8,128)(2,1)} all-to-all(bf16[4,672,128]{2,1,0:T(8,128)(2,1)} %combine.1), channel_id=1, replica_groups=mesh['zl'=8,'core'=2,'zh'=2,'y'=4,'x'=4] {'y'}, dimensions={0} | all-to-all | bytes 1376256 | tf_op jit(solution)/shard_map/all_to_all | solution.py:404
  124.9 1.8 %halves.1 = (bf16[448,128]{1,0:T(8,128)(2,1)}, bf16[448,128]{1,0:T(8,128)(2,1)}) custom-call(s32[4]{0:T(128)} %pad_add_fusion.where_ref, bf16[4,672,128]{2,1,0:T(8,128)(2,1)} %all_to_all.25.msg_ref), custom_call_target="tpu_custom_call" | custom-call | tf_op jit(solution)/shard_map/halves/pallas_call | solution.py:326
  126.7 8.6 %collective-permute-start.8 = (bf16[448,128]{1,0:T(8,128)(2,1)}, bf16[448,128]{1,0:T(8,128)(2,1)S(1)}, u32[]{:S(2)}, u32[]{:S(2)}) collective-permute-start(bf16[448,128]{1,0:T(8,128)(2,1)} %get-tuple-element.40), channel_id=1, source_target_pairs={{0,16},{16,0},{1,17},{17,1},{2,18},{18,2},{3,19},{19,3},{4,20},{20... | collective-permute-start | bytes 344072 | tf_op jit(solution)/shard_map/ppermute | solution.py:383
  135.3 13.2 %collective-permute-done.8.other_ref = bf16[448,128]{1,0:T(8,128)(2,1)S(1)} collective-permute-done((bf16[448,128]{1,0:T(8,128)(2,1)}, bf16[448,128]{1,0:T(8,128)(2,1)S(1)}, u32[]{:S(2)}, u32[]{:S(2)}) %collective-permute-start.8) | collective-permute-done | bytes 114720 | tf_op jit(solution)/shard_map/ppermute | solution.py:383
  148.6 0.6 copy-done.8
  149.2 1.7 %finish.1 = (bf16[4,128,128]{2,1,0:T(8,128)(2,1)}, bf16[128,256]{1,0:T(8,128)(2,1)}, bf16[4,768]{1,0:T(4,128)(2,1)}, bf16[4,1024]{1,0:T(4,128)(2,1)}) custom-call(bf16[448,128]{1,0:T(8,128)(2,1)} %get-tuple-element.39.own_ref, bf16[448,128]{1,0:T(8,128)(2,1)} %copy-done.8), custom_call_target="tpu_custom_call" | custom-call | tf_op jit(solution)/shard_map/finish/pallas_call | solution.py:370
  150.9 3.3 %all-to-all-start.4 = ((bf16[4,128,128]{2,1,0:T(8,128)(2,1)}), bf16[4,128,128]{2,1,0:T(8,128)(2,1)S(1)}, u32[]{:S(2)}, u32[]{:S(2)}) async-start(bf16[4,128,128]{2,1,0:T(8,128)(2,1)} %get-tuple-element.42), calls=%async_computation.4 | async-start | bytes 262144 | tf_op jit(solution)/shard_map/all_to_all | solution.py:408
  154.2 1.9 %unpack.1 = bf16[128,1024]{1,0:T(8,128)(2,1)} custom-call(bf16[4,672,128]{2,1,0:T(8,128)(2,1)} %all_to_all.25.msg_ref), custom_call_target="tpu_custom_call" | custom-call | tf_op jit(solution)/shard_map/unpack/pallas_call | solution.py:345
  156.1 4.1 %all-to-all-done.4 = bf16[4,128,128]{2,1,0:T(8,128)(2,1)S(1)} async-done(((bf16[4,128,128]{2,1,0:T(8,128)(2,1)}), bf16[4,128,128]{2,1,0:T(8,128)(2,1)S(1)}, u32[]{:S(2)}, u32[]{:S(2)}) %all-to-all-start.4) | async-done | bytes 131104 | tf_op jit(solution)/shard_map/all_to_all | solution.py:408
  160.2 0.1 copy.15
  160.3 0.8 copy.16
  (4 shorter events, 0.0 us)
Async XLA Ops:
  3.0 4.6 %copy-start.12 = (bf16[784,128]{1,0:T(8,128)(2,1)S(1)}, bf16[784,128]{1,0:T(8,128)(2,1)}, u32[]{:S(2)}) copy-start(bf16[784,128]{1,0:T(8,128)(2,1)} %get-tuple-element.26) | copy-start | bytes 602116
  3.0 20.7 %all-to-all-start = ((bf16[4,1120,128]{2,1,0:T(8,128)(2,1)}), bf16[4,1120,128]{2,1,0:T(8,128)(2,1)S(1)}, u32[]{:S(2)}, u32[]{:S(2)}) async-start(bf16[4,1120,128]{2,1,0:T(8,128)(2,1)} %get-tuple-element.25), calls=%async_computation | async-start | bytes 2293760 | tf_op jit(solution)/shard_map/all_to_all | solution.py:391
  7.6 32.0 %collective-permute-start = (bf16[784,128]{1,0:T(8,128)(2,1)S(1)}, bf16[784,128]{1,0:T(8,128)(2,1)S(1)}, u32[]{:S(2)}, u32[]{:S(2)}) collective-permute-start(bf16[784,128]{1,0:T(8,128)(2,1)S(1)} %copy-done.12), channel_id=1, source_target_pairs={{0,16},{16,0},{1,17},{17,1},{2,18},{18,2},{3,19},{19,3},{4,20},{20... | collective-permute-start | bytes 602120 | tf_op jit(solution)/shard_map/ppermute | solution.py:383
  23.8 1.0 copy-start
  26.2 28.3 %all-to-all-start.1 = ((bf16[16,64,128]{2,1,0:T(8,128)(2,1)}), bf16[16,64,128]{2,1,0:T(8,128)(2,1)S(1)}, u32[]{:S(2)}, u32[]{:S(2)}) async-start(bf16[16,64,128]{2,1,0:T(8,128)(2,1)} %spread.1), calls=%async_computation.1 | async-start | bytes 524288 | tf_op jit(solution)/shard_map/all_to_all | solution.py:392
  39.6 0.7 copy-start.13
  42.2 14.7 %collective-permute-start.1 = (bf16[592,128]{1,0:T(8,128)(2,1)}, bf16[592,128]{1,0:T(8,128)(2,1)S(1)}, u32[]{:S(2)}, u32[]{:S(2)}) collective-permute-start(bf16[592,128]{1,0:T(8,128)(2,1)} %get-tuple-element.28), channel_id=1, source_target_pairs={{0,4},{4,0},{8,12},{12,8},{1,5},{5,1},{9,13},{13,9},{2,6},{6,2},{1... | collective-permute-start | bytes 454664 | tf_op jit(solution)/shard_map/ppermute | solution.py:383
  44.6 12.2 %collective-permute-start.2 = (bf16[592,128]{1,0:T(8,128)(2,1)}, bf16[592,128]{1,0:T(8,128)(2,1)S(1)}, u32[]{:S(2)}, u32[]{:S(2)}) collective-permute-start(bf16[592,128]{1,0:T(8,128)(2,1)} %get-tuple-element.29), channel_id=1, source_target_pairs={{0,8},{4,12},{8,0},{12,4},{1,9},{5,13},{9,1},{13,5},{2,10},{6,14},... | collective-permute-start | bytes 454664 | tf_op jit(solution)/shard_map/ppermute | solution.py:383
  48.6 8.5 %collective-permute-start.3 = (bf16[592,128]{1,0:T(8,128)(2,1)}, bf16[592,128]{1,0:T(8,128)(2,1)S(1)}, u32[]{:S(2)}, u32[]{:S(2)}) collective-permute-start(bf16[592,128]{1,0:T(8,128)(2,1)} %get-tuple-element.30), channel_id=1, source_target_pairs={{0,12},{4,8},{8,4},{12,0},{1,13},{5,9},{9,5},{13,1},{2,14},{6,10},... | collective-permute-start | bytes 454664 | tf_op jit(solution)/shard_map/ppermute | solution.py:383
  56.8 0.7 copy-start.5
  56.8 0.7 copy-start.6
  57.1 0.7 copy-start.7
  67.8 15.4 %copy-start.11 = (bf16[1024,128]{1,0:T(8,128)(2,1)S(1)}, bf16[1024,128]{1,0:T(8,128)(2,1)}, u32[]{:S(2)}) copy-start(bf16[1024,128]{1,0:T(8,128)(2,1)} %get-tuple-element.34) | copy-start | bytes 786436
  67.8 18.8 %copy-start.10 = (bf16[1024,128]{1,0:T(8,128)(2,1)S(1)}, bf16[1024,128]{1,0:T(8,128)(2,1)}, u32[]{:S(2)}) copy-start(bf16[1024,128]{1,0:T(8,128)(2,1)} %get-tuple-element.35) | copy-start | bytes 786436
  67.8 23.5 %copy-start.9 = (bf16[1024,128]{1,0:T(8,128)(2,1)S(1)}, bf16[1024,128]{1,0:T(8,128)(2,1)}, u32[]{:S(2)}) copy-start(bf16[1024,128]{1,0:T(8,128)(2,1)} %get-tuple-element.36) | copy-start | bytes 786436
  67.8 3.8 %collective-permute-start.7 = (bf16[8,32,512]{2,1,0:T(8,128)(2,1)}, bf16[8,32,512]{2,1,0:T(8,128)(2,1)S(1)}, u32[]{:S(2)}, u32[]{:S(2)}) collective-permute-start(bf16[8,32,512]{2,1,0:T(8,128)(2,1)} %get-tuple-element.38), channel_id=1, source_target_pairs={{0,32},{32,0},{1,33},{33,1},{2,34},{34,2},{3,35},{35,3},{4,36},{36... | collective-permute-start | bytes 786440 | tf_op jit(solution)/shard_map/ppermute | solution.py:383
  73.3 32.7 %all-to-all-start.2 = ((bf16[8,32,512]{2,1,0:T(8,128)(2,1)}), bf16[8,32,512]{2,1,0:T(8,128)(2,1)S(1)}, u32[]{:S(2)}, u32[]{:S(2)}) async-start(bf16[8,32,512]{2,1,0:T(8,128)(2,1)} %add_convert_fusion), calls=%async_computation.2 | async-start | bytes 524288 | tf_op jit(solution)/shard_map/all_to_all | solution.py:400
  83.2 11.1 %collective-permute-start.4 = (bf16[1024,128]{1,0:T(8,128)(2,1)S(1)}, bf16[1024,128]{1,0:T(8,128)(2,1)S(1)}, u32[]{:S(2)}, u32[]{:S(2)}) collective-permute-start(bf16[1024,128]{1,0:T(8,128)(2,1)S(1)} %copy-done.11), channel_id=1, source_target_pairs={{0,1},{1,0},{2,3},{3,2},{4,5},{5,4},{6,7},{7,6},{8,9},{9,8},{10,11... | collective-permute-start | bytes 786440 | tf_op jit(solution)/shard_map/ppermute | solution.py:383
  86.6 14.2 %collective-permute-start.5 = (bf16[1024,128]{1,0:T(8,128)(2,1)S(1)}, bf16[1024,128]{1,0:T(8,128)(2,1)S(1)}, u32[]{:S(2)}, u32[]{:S(2)}) collective-permute-start(bf16[1024,128]{1,0:T(8,128)(2,1)S(1)} %copy-done.10), channel_id=1, source_target_pairs={{0,2},{1,3},{2,0},{3,1},{4,6},{5,7},{6,4},{7,5},{8,10},{9,11},{10,... | collective-permute-start | bytes 786440 | tf_op jit(solution)/shard_map/ppermute | solution.py:383
  91.3 14.8 %collective-permute-start.6 = (bf16[1024,128]{1,0:T(8,128)(2,1)S(1)}, bf16[1024,128]{1,0:T(8,128)(2,1)S(1)}, u32[]{:S(2)}, u32[]{:S(2)}) collective-permute-start(bf16[1024,128]{1,0:T(8,128)(2,1)S(1)} %copy-done.9), channel_id=1, source_target_pairs={{0,3},{1,2},{2,1},{3,0},{4,7},{5,6},{6,5},{7,4},{8,11},{9,10},{10,... | collective-permute-start | bytes 786440 | tf_op jit(solution)/shard_map/ppermute | solution.py:383
  94.3 11.7 %copy-start.2 = (bf16[1024,128]{1,0:T(8,128)(2,1)}, bf16[1024,128]{1,0:T(8,128)(2,1)S(1)}, u32[]{:S(2)}) copy-start(bf16[1024,128]{1,0:T(8,128)(2,1)S(1)} %collective-permute-done.4.l1_ref) | copy-start | bytes 786436
  100.8 5.3 %copy-start.3 = (bf16[1024,128]{1,0:T(8,128)(2,1)}, bf16[1024,128]{1,0:T(8,128)(2,1)S(1)}, u32[]{:S(2)}) copy-start(bf16[1024,128]{1,0:T(8,128)(2,1)S(1)} %collective-permute-done.5.l2_ref) | copy-start | bytes 786436
  106.0 0.7 copy-start.4
  106.0 0.8 copy-start.1
  126.7 21.9 %collective-permute-start.8 = (bf16[448,128]{1,0:T(8,128)(2,1)}, bf16[448,128]{1,0:T(8,128)(2,1)S(1)}, u32[]{:S(2)}, u32[]{:S(2)}) collective-permute-start(bf16[448,128]{1,0:T(8,128)(2,1)} %get-tuple-element.40), channel_id=1, source_target_pairs={{0,16},{16,0},{1,17},{17,1},{2,18},{18,2},{3,19},{19,3},{4,20},{20... | collective-permute-start | bytes 344072 | tf_op jit(solution)/shard_map/ppermute | solution.py:383
  148.6 0.6 copy-start.8
  150.9 9.3 %all-to-all-start.4 = ((bf16[4,128,128]{2,1,0:T(8,128)(2,1)}), bf16[4,128,128]{2,1,0:T(8,128)(2,1)S(1)}, u32[]{:S(2)}, u32[]{:S(2)}) async-start(bf16[4,128,128]{2,1,0:T(8,128)(2,1)} %get-tuple-element.42), calls=%async_computation.4 | async-start | bytes 262144 | tf_op jit(solution)/shard_map/all_to_all | solution.py:408

commit v4 on v3

--- a/solution.py
+++ b/solution.py
@@ -29,10 +29,10 @@
 Q0, G0, L0, K0, S0, W0, MSG = 0, 256, 512, 1024, 1088, 1104, 1120
 KEY_K, KEY_S, KEY = 512, 768, 784
 PASS_S, PASS = 576, 592
-BL0, BK0, BW0, BACK = 256, 512, 640, 672
-EK0, EW0, END = 128, 384, 448
+BK0, BW0, BACK = 256, 320, 336
 BLK = 256
 
+waits_for_z = pl.CostEstimate(flops=50_000_000_000, transcendentals=0, bytes_accessed=150_000_000)
 f32 = jnp.float32
 bf16 = jnp.bfloat16
 
@@ -119,18 +119,17 @@
             pl.BlockSpec(memory_space=pltpu.VMEM),
         ],
         out_shape=[jax.ShapeDtypeStruct((PASS, HD), bf16)] * NY,
-        cost_estimate=pl.CostEstimate(flops=50_000_000_000, transcendentals=0, bytes_accessed=150_000_000),
+        cost_estimate=waits_for_z,
         name="relay",
     )(place, other)
 
 
 def main_kernel(
     where_ref, freq_ref, msg_ref, key0_ref, key1_ref, key2_ref, key3_ref, w_ref,
-    dq_ref, dkr_ref, dl0_ref, dl1_ref, dl2_ref, dl3_ref, dw_own_ref, dw_other_ref,
+    lat_out_ref, dq_ref, kr_own_ref, kr_other_ref, dw_own_ref, dw_other_ref,
     lat_s, w_s, k_s, kt_s, q_s, qt_s, v_s, gt_s, pos_s, rope_s, cos_s, sin_s, dkv_s, dqt_s, dw_s,
 ):
     core = where_ref[0]
-    x = where_ref[1]
     own_y = where_ref[2]
     def take(read, lat0, rope0, pos0, tokens):
         for b in range(RANK // HD):
@@ -230,18 +229,23 @@
         for c in range(NY):
             cols = slice(c * TOK, (c + 1) * TOK)
             dq_ref[c, g * TOK:(g + 1) * TOK, :] = dq[cols, :]
-            for z in range(2):
-                rows = slice((z * GRP + g) * RD, (z * GRP + g + 1) * RD)
-                dkr_ref[c, rows, :] = dkr[:, z * HALF + c * TOK:z * HALF + (c + 1) * TOK]
+            kr_own_ref[c, g * RD:(g + 1) * RD, :] = dkr[:, cols]
+            kr_other_ref[c, g * RD:(g + 1) * RD, :] = dkr[:, HALF + c * TOK:HALF + (c + 1) * TOK]
 
     dkv = dkv_s[...].astype(bf16)
-    for t, ref in enumerate((dl0_ref, dl1_ref, dl2_ref, dl3_ref)):
-        rows = pl.ds(pl.multiple_of((x ^ t) * HD, HD), HD)
-        ref[...] = dot(dkv, w_s[rows, :], ((1,), (1,))).astype(bf16)
+    dlat = dot(dkv, w_s[...], ((1,), (1,))).astype(bf16)
+    for z in range(2):
+        for y in range(NY):
+            c = z * NY + y
+            for b in range(TEN):
+                lat_out_ref[y * TEN + b, z * TOK:(z + 1) * TOK, :] = dlat[
+                    c * TOK:(c + 1) * TOK, b * HD:(b + 1) * HD
+                ]
     dw_s[...] = dot(lat_s[...], dkv, ((0,), (0,)))
-    for z in range(ZL):
-        own = pl.ds(pl.multiple_of((z * CORE + core) * 32, 32), 32)
-        other = pl.ds(pl.multiple_of((z * CORE + 1 - core) * 32, 32), 32)
+    for z in range(NZ):
+        base = (z // 2) * CORE * 32 + (z % 2) * 16
+        own = pl.ds(pl.multiple_of(base + core * 32, 16), 16)
+        other = pl.ds(pl.multiple_of(base + (1 - core) * 32, 16), 16)
         dw_own_ref[z] = dw_s[own, :].astype(bf16)
         dw_other_ref[z] = dw_s[other, :].astype(bf16)
 
@@ -249,16 +253,18 @@
 def attention(place, freq, msg, keys, w):
     smem = pl.BlockSpec(memory_space=pltpu.SMEM)
     vmem = pl.BlockSpec(memory_space=pltpu.VMEM)
-    rope = jax.ShapeDtypeStruct((NY, 2 * GRP * RD, TOK), bf16)
-    quarter = jax.ShapeDtypeStruct((SEQ, HD), bf16)
-    weight = jax.ShapeDtypeStruct((ZL, 32, 2 * GRP * HD), bf16)
     return pl.pallas_call(
         main_kernel,
         in_specs=[smem] + [vmem] * 7,
-        out_specs=[vmem] * 8,
-        out_shape=[jax.ShapeDtypeStruct((NY, GRP * TOK, HD), bf16), rope]
-        + [quarter] * 4
-        + [weight, weight],
+        out_specs=[vmem] * 6,
+        out_shape=[
+            jax.ShapeDtypeStruct((NY * TEN, 2 * TOK, HD), bf16),
+            jax.ShapeDtypeStruct((NY, GRP * TOK, HD), bf16),
+            jax.ShapeDtypeStruct((NY, GRP * RD, TOK), bf16),
+            jax.ShapeDtypeStruct((NY, GRP * RD, TOK), bf16),
+            jax.ShapeDtypeStruct((NZ, NY * ROWS, 2 * GRP * HD), bf16),
+            jax.ShapeDtypeStruct((NZ, NY * ROWS, 2 * GRP * HD), bf16),
+        ],
         scratch_shapes=[
             pltpu.VMEM((SEQ, RANK), bf16),
             pltpu.VMEM((RANK, 2 * GRP * HD), bf16),
@@ -281,102 +287,104 @@
     )(place, freq, msg, *keys, w)
 
 
-def combine_kernel(dq_ref, kr_ref, l0_ref, l1_ref, l2_ref, l3_ref, dw_ref, out_ref):
+def fold_kernel(parts_ref, dw0_ref, dw1_ref, kr_ref, own_ref, other_ref, dw_ref):
+    both = jnp.sum(parts_ref[...].astype(f32), 0)
+    own_ref[...] = both[0:TOK]
+    other_ref[0:TOK, :] = both[TOK:].astype(bf16)
+    for y in range(NY):
+        other_ref[TOK + y * GRP * RD:TOK + (y + 1) * GRP * RD, :] = kr_ref[y]
+    dw_ref[...] = (dw0_ref[...].astype(f32) + dw1_ref[...].astype(f32)).astype(bf16)
+
+
+def fold(*parts):
+    return pl.pallas_call(
+        fold_kernel,
+        out_shape=[
+            jax.ShapeDtypeStruct((TOK, HD), f32),
+            jax.ShapeDtypeStruct((TOK + NY * GRP * RD, HD), bf16),
+            jax.ShapeDtypeStruct((NZ, NY * ROWS, 2 * GRP * HD), bf16),
+        ],
+        name="fold",
+    )(*parts)
+
+
+def merge_kernel(own_ref, kr_ref, other_ref, quarter_ref, out_ref):
+    quarter_ref[...] = (own_ref[...] + other_ref[0:TOK, :].astype(f32)).astype(bf16)
+    for y in range(NY):
+        kr = other_ref[TOK + y * GRP * RD:TOK + (y + 1) * GRP * RD, :]
+        out_ref[y] = (kr_ref[y].astype(f32) + kr.astype(f32)).astype(bf16)
+
+
+def merge(*parts):
+    return pl.pallas_call(
+        merge_kernel,
+        out_shape=[
+            jax.ShapeDtypeStruct((TOK, HD), bf16),
+            jax.ShapeDtypeStruct((NY, GRP * RD, TOK), bf16),
+        ],
+        cost_estimate=waits_for_z,
+        name="merge",
+    )(*parts)
+
+
+def combine_kernel(
+    where_ref, dq_ref, kr_ref, dw_ref, q0_ref, q1_ref, q2_ref, q3_ref, out_ref, lat_ref
+):
+    x = where_ref[1]
+    for t, ref in enumerate((q0_ref, q1_ref, q2_ref, q3_ref)):
+        lat_ref[:, pl.ds(pl.multiple_of((x ^ t) * HD, HD), HD)] = ref[...]
     dw = jnp.sum(dw_ref[...].astype(f32), 0)
     for y in range(NY):
-        out_ref[y, 0:BL0, :] = dq_ref[y]
+        out_ref[y, 0:BK0, :] = dq_ref[y]
         out_ref[y, BK0:BW0, :] = kr_ref[y]
-        for z in range(2):
-            rows = slice((z * NY + y) * TOK, (z * NY + y + 1) * TOK)
-            lat = (l0_ref[rows, :].astype(f32) + l1_ref[rows, :].astype(f32)) + (
-                l2_ref[rows, :].astype(f32) + l3_ref[rows, :].astype(f32)
-            )
-            out_ref[y, BL0 + z * TOK:BL0 + (z + 1) * TOK, :] = lat.astype(bf16)
-        for z in range(2):
-            part = dw[z * 16 + y * ROWS:z * 16 + (y + 1) * ROWS, :]
-            out_ref[y, BW0 + z * 16:BW0 + (z + 1) * 16, :] = jnp.concatenate(
-                [part[:, c * HD:(c + 1) * HD] for c in range(2 * GRP)], 0
-            ).astype(bf16)
-
-
-def combine(*parts):
+        part = dw[y * ROWS:(y + 1) * ROWS, :]
+        out_ref[y, BW0:BACK, :] = jnp.concatenate(
+            [part[:, c * HD:(c + 1) * HD] for c in range(2 * GRP)], 0
+        ).astype(bf16)
+
+
+def combine(place, *parts):
+    vmem = pl.BlockSpec(memory_space=pltpu.VMEM)
     return pl.pallas_call(
         combine_kernel,
-        out_shape=jax.ShapeDtypeStruct((NY, BACK, HD), bf16),
+        in_specs=[pl.BlockSpec(memory_space=pltpu.SMEM)] + [vmem] * (3 + TEN),
+        out_shape=[
+            jax.ShapeDtypeStruct((NY, BACK, HD), bf16),
+            jax.ShapeDtypeStruct((TOK, RANK), bf16),
+        ],
         name="combine",
-    )(*parts)
-
-
-def halves_kernel(where_ref, msg_ref, own_ref, other_ref):
-    half = where_ref[3]
-    for z, ref in enumerate((own_ref, other_ref)):
-        lat = sum(
-            msg_ref[y, BL0 + z * TOK:BL0 + (z + 1) * TOK, :].astype(f32) for y in range(NY)
-        )
-        ref[0:TOK, :] = lat.astype(bf16)
-        weights = pl.ds(pl.multiple_of(BW0 + (half ^ z) * 16, 16), 16)
-        for y in range(NY):
-            rows = slice(EK0 + y * GRP * RD, EK0 + (y + 1) * GRP * RD)
-            ref[rows, :] = msg_ref[y, BK0 + z * GRP * RD:BK0 + (z + 1) * GRP * RD, :]
-            ref[EW0 + y * 16:EW0 + (y + 1) * 16, :] = msg_ref[y, weights, :]
-
-
-def halves(place, msg):
-    part = jax.ShapeDtypeStruct((END, HD), bf16)
-    return pl.pallas_call(
-        halves_kernel,
-        in_specs=[
-            pl.BlockSpec(memory_space=pltpu.SMEM),
-            pl.BlockSpec(memory_space=pltpu.VMEM),
-        ],
-        out_shape=[part, part],
-        name="halves",
-    )(place, msg)
-
-
-def unpack_kernel(msg_ref, q_ref):
+    )(place, *parts)
+
+
+def unpack_kernel(msg_ref, q_ref, kr_ref, wk_ref, wv_ref):
+    ropes = []
+    wk = []
+    wv = []
     for y in range(NY):
         for g in range(GRP):
             h = y * GRP + g
             q_ref[:, h * HD:(h + 1) * HD] = msg_ref[y, g * TOK:(g + 1) * TOK, :]
-
-
-def unpack(msg):
-    return pl.pallas_call(
-        unpack_kernel,
-        out_shape=jax.ShapeDtypeStruct((TOK, NY * GRP * HD), bf16),
-        name="unpack",
-    )(msg)
-
-
-def finish_kernel(own_ref, other_ref, lat_ref, kr_ref, wk_ref, wv_ref):
-    both = own_ref[...].astype(f32) + other_ref[...].astype(f32)
-    lat = both[0:TOK].astype(bf16)
-    for t in range(TEN):
-        lat_ref[t] = lat
-    kr_ref[...] = both[EK0:EW0].T.astype(bf16)
-    wk = []
-    wv = []
-    for y in range(NY):
-        tail = both[EW0 + y * 16:EW0 + (y + 1) * 16]
+        ropes.append(msg_ref[y, BK0:BW0, :].astype(f32))
+        tail = msg_ref[y, BW0:BACK, :].astype(f32)
         for g in range(GRP):
             wk.append(tail[g * ROWS:(g + 1) * ROWS, RD:])
             wv.append(tail[(GRP + g) * ROWS:(GRP + g + 1) * ROWS])
+    kr_ref[...] = jnp.concatenate(ropes, 0).T.astype(bf16)
     wk_ref[...] = jnp.concatenate(wk, 1).astype(bf16)
     wv_ref[...] = jnp.concatenate(wv, 1).astype(bf16)
 
 
-def finish(own, other):
-    return pl.pallas_call(
-        finish_kernel,
-        out_shape=[
-            jax.ShapeDtypeStruct((TEN, TOK, HD), bf16),
+def unpack(msg):
+    return pl.pallas_call(
+        unpack_kernel,
+        out_shape=[
+            jax.ShapeDtypeStruct((TOK, NY * GRP * HD), bf16),
             jax.ShapeDtypeStruct((TOK, NY * GRP * RD), bf16),
             jax.ShapeDtypeStruct((ROWS, NY * GRP * NOPE), bf16),
             jax.ShapeDtypeStruct((ROWS, NY * GRP * HD), bf16),
         ],
-        name="finish",
-    )(own, other)
+        name="unpack",
+    )(msg)
 
 
 def swap(array, axis, size, flip):
@@ -394,20 +402,19 @@
     keys = [keys[0]] + [swap(keys[t], "y", NY, t) for t in range(1, NY)]
     w = lax.all_gather(w, "core", axis=0)
 
-    dq, dkr, l0, l1, l2, l3, dw_own, dw_other = attention(place, freq_index, msg, keys, w)
-
-    dw = dw_own.astype(f32) + swap(dw_other, "core", 2, 1).astype(f32)
-    dw = lax.all_to_all(dw.astype(bf16), "zl", 0, 0)
-    l1 = swap(l1, "x", TEN, 1)
-    l2 = swap(l2, "x", TEN, 2)
-    l3 = swap(l3, "x", TEN, 3)
-    back = lax.all_to_all(combine(dq, dkr, l0, l1, l2, l3, dw), "y", 0, 0)
-    own, other = halves(place, back)
-    quarter, key_rope_grad, up_key_grad, up_value_grad = finish(own, swap(other, "zh", 2, 1))
-    query_grad = unpack(back)
-    quarters = lax.all_to_all(quarter, "x", 0, 0)
-    latent_grad = quarters.transpose(1, 0, 2).reshape(1, TOK, RANK)
-    return (query_grad[None], key_rope_grad[None], latent_grad, up_key_grad, up_value_grad)
+    parts, dq, kr_own, kr_other, dw_own, dw_other = attention(place, freq_index, msg, keys, w)
+
+    dw_other = swap(dw_other, "core", 2, 1)
+    parts = lax.all_to_all(parts, ("y", "x"), 0, 0)
+    lat_own, other, dw = fold(parts, dw_own, dw_other, kr_other)
+    other = swap(other, "zh", 2, 1)
+    dw = lax.all_to_all(dw, ("zl", "zh"), 0, 0)
+    quarter, kr = merge(lat_own, kr_own, other)
+    quarters = [quarter] + [swap(quarter, "x", TEN, t) for t in range(1, TEN)]
+    back, latent_grad = combine(place, dq, kr, dw, *quarters)
+    back = lax.all_to_all(back, "y", 0, 0)
+    query_grad, key_rope_grad, up_key_grad, up_value_grad = unpack(back)
+    return (query_grad[None], key_rope_grad[None], latent_grad[None], up_key_grad, up_value_grad)
 
 
 def solution(mesh):

time: 162 us -> 152 us (0.938)
  the two profiles are of different devices: /device:TPU:160 before, /device:TPU:2 now
where the time goes in v4:
time: 152 us; the launch traced here: 151 us
  starting transfers between devices  77.4 us (51%)
  waiting for transfers between devices  30.8 us (20%)
  Pallas kernels  22.7 us (15%)
  blocking collectives  13.6 us (9%)
  local copies, waits for them, and re-layouts  4.73 us (3%)
    ppermute x9, starting transfers between devices, swap(): return lax.ppermute(array, axis, [(i, i ^ flip) for i in range(size)])  44.9 us
    all_to_all x1, starting transfers between devices, body(): w = lax.all_to_all(spread(msg), ('zl', 'zh'), 0, 0)  15 us
    all_to_all x1, waiting for transfers between devices, body(): parts = lax.all_to_all(parts, ('y', 'x'), 0, 0)  12.7 us
    ppermute x9, waiting for transfers between devices, swap(): return lax.ppermute(array, axis, [(i, i ^ flip) for i in range(size)])  11.8 us
    all_to_all x1, blocking collectives, body(): back = lax.all_to_all(back, 'y', 0, 0)  11.3 us
    pallas_call x1, Pallas kernels, attention(): pl.pallas_call(main_kernel, in_specs=[smem] + [vmem] * 7, out_specs=[vmem...  9.53 us
    all_to_all x1, starting transfers between devices, body(): dw = lax.all_to_all(dw, ('zl', 'zh'), 0, 0)  6.94 us
    all_to_all x1, waiting for transfers between devices, body(): w = lax.all_to_all(spread(msg), ('zl', 'zh'), 0, 0)  6.28 us
  transfers between devices with their start and end apart: 13, of which 5 were waited for; matrix products, arithmetic and copies ran while one was open for 0% of the time, Pallas kernels for 3%

profile of v4, /device:TPU:2, one launch (start us, length us, event | category | flops | bytes accessed | tf_op | source)
XLA Modules:
  0.0 150.7 jit_solution(10225042823713082850)
XLA Ops:
  0.6 2.4 %pack.1 = (bf16[4,1120,128]{2,1,0:T(8,128)(2,1)}, bf16[784,128]{1,0:T(8,128)(2,1)}) custom-call(bf16[128,1024]{1,0:T(8,128)(2,1)} %bitcast.13, bf16[128,1024]{1,0:T(8,128)(2,1)} %bitcast.14, bf16[128,256]{1,0:T(8,128)(2,1)} %bitcast.16, bf16[128,512]{1,0:T(8,128)(2,1)} %bitcast.15, bf16[4,768]{1,0:T(4,128)(2,1)} %wk_ref.1, bf16[4,1024]{1,0:T(4,128)(2,1)} %wv_ref.1, ...), custom_call_target="tpu_custom_call" | custom-call | tf_op jit(solution)/shard_map/pack/pallas_call | solution.py:76
  3.0 0.0 copy-start.11
  3.0 4.6 %all-to-all-start = ((bf16[4,1120,128]{2,1,0:T(8,128)(2,1)}), bf16[4,1120,128]{2,1,0:T(8,128)(2,1)S(1)}, u32[]{:S(2)}, u32[]{:S(2)}) async-start(bf16[4,1120,128]{2,1,0:T(8,128)(2,1)} %get-tuple-element.28), calls=%async_computation | async-start | bytes 2293760 | tf_op jit(solution)/shard_map/all_to_all | solution.py:399
  7.6 0.0 copy-done.11
  7.6 15.7 %collective-permute-start = (bf16[784,128]{1,0:T(8,128)(2,1)S(1)}, bf16[784,128]{1,0:T(8,128)(2,1)S(1)}, u32[]{:S(2)}, u32[]{:S(2)}) collective-permute-start(bf16[784,128]{1,0:T(8,128)(2,1)S(1)} %copy-done.11), channel_id=1, source_target_pairs={{0,16},{16,0},{1,17},{17,1},{2,18},{18,2},{3,19},{19,3},{4,20},{20... | collective-permute-start | bytes 602120 | tf_op jit(solution)/shard_map/ppermute | solution.py:391
  23.3 0.6 pad_add_fusion.where_ref
  23.9 0.0 all-to-all-done.msg_ref
  23.9 0.0 copy-start
  23.9 1.0 copy-done
  25.0 1.4 spread.1
  26.4 15.0 %all-to-all-start.1 = ((bf16[16,64,128]{2,1,0:T(8,128)(2,1)}), bf16[16,64,128]{2,1,0:T(8,128)(2,1)S(1)}, u32[]{:S(2)}, u32[]{:S(2)}) async-start(bf16[16,64,128]{2,1,0:T(8,128)(2,1)} %spread.1), calls=%async_computation.1 | async-start | bytes 524288 | tf_op jit(solution)/shard_map/all_to_all | solution.py:400
  41.4 0.0 collective-permute-done.key_ref
  41.5 0.0 copy-start.12
  41.5 0.7 copy-done.12
  42.1 1.8 %relay.1 = (bf16[592,128]{1,0:T(8,128)(2,1)}, bf16[592,128]{1,0:T(8,128)(2,1)}, bf16[592,128]{1,0:T(8,128)(2,1)}, bf16[592,128]{1,0:T(8,128)(2,1)}) custom-call(s32[4]{0:T(128)} %pad_add_fusion.where_ref, bf16[784,128]{1,0:T(8,128)(2,1)} %copy-done.12), custom_call_target="tpu_custom_call" | custom-call | flops 49999998976 | bytes 150000000 | tf_op jit(solution)/shard_map/relay/pallas_call | solution.py:115
  43.9 2.5 %collective-permute-start.1 = (bf16[592,128]{1,0:T(8,128)(2,1)}, bf16[592,128]{1,0:T(8,128)(2,1)S(1)}, u32[]{:S(2)}, u32[]{:S(2)}) collective-permute-start(bf16[592,128]{1,0:T(8,128)(2,1)} %get-tuple-element.31), channel_id=1, source_target_pairs={{0,4},{4,0},{8,12},{12,8},{1,5},{5,1},{9,13},{13,9},{2,6},{6,2},{1... | collective-permute-start | bytes 454664 | tf_op jit(solution)/shard_map/ppermute | solution.py:391
  46.4 4.0 %collective-permute-start.2 = (bf16[592,128]{1,0:T(8,128)(2,1)}, bf16[592,128]{1,0:T(8,128)(2,1)S(1)}, u32[]{:S(2)}, u32[]{:S(2)}) collective-permute-start(bf16[592,128]{1,0:T(8,128)(2,1)} %get-tuple-element.32), channel_id=1, source_target_pairs={{0,8},{4,12},{8,0},{12,4},{1,9},{5,13},{9,1},{13,5},{2,10},{6,14},... | collective-permute-start | bytes 454664 | tf_op jit(solution)/shard_map/ppermute | solution.py:391
  50.4 4.0 %collective-permute-start.3 = (bf16[592,128]{1,0:T(8,128)(2,1)}, bf16[592,128]{1,0:T(8,128)(2,1)S(1)}, u32[]{:S(2)}, u32[]{:S(2)}) collective-permute-start(bf16[592,128]{1,0:T(8,128)(2,1)} %get-tuple-element.33), channel_id=1, source_target_pairs={{0,12},{4,8},{8,4},{12,0},{1,13},{5,9},{9,5},{13,1},{2,14},{6,10},... | collective-permute-start | bytes 454664 | tf_op jit(solution)/shard_map/ppermute | solution.py:391
  54.4 6.3 %all-to-all-done.1 = bf16[16,64,128]{2,1,0:T(8,128)(2,1)S(1)} async-done(((bf16[16,64,128]{2,1,0:T(8,128)(2,1)}), bf16[16,64,128]{2,1,0:T(8,128)(2,1)S(1)}, u32[]{:S(2)}, u32[]{:S(2)}) %all-to-all-start.1) | async-done | bytes 262176 | tf_op jit(solution)/shard_map/all_to_all | solution.py:400
  60.7 2.3 %all-gather = bf16[32,64,128]{2,1,0:T(8,128)(2,1)} all-gather(bf16[16,64,128]{2,1,0:T(8,128)(2,1)S(1)} %all-to-all-done.1), channel_id=2, replica_groups=mesh['zl'=8,'core'=2,'zh'=2,'y'=4,'x'=4] {'core'}, dimensions={0}, use_global_device_ids=true | all-gather | bytes 786432 | tf_op jit(solution)/shard_map/all_gather | solution.py:403
  63.0 0.0 collective-permute-done.1.key1_ref
  63.0 0.0 copy-start.4
  63.0 0.0 collective-permute-done.2.key2_ref
  63.0 0.0 copy-start.5
  63.0 0.0 collective-permute-done.3.key3_ref
  63.0 0.0 copy-start.6
  63.0 0.6 copy-done.4
  63.6 0.0 copy-done.5
  63.7 0.1 copy-done.6
  63.7 9.5 %attention_backward.1 = (bf16[16,256,128]{2,1,0:T(8,128)(2,1)}, bf16[4,256,128]{2,1,0:T(8,128)(2,1)}, bf16[4,64,128]{2,1,0:T(8,128)(2,1)}, bf16[4,64,128]{2,1,0:...) custom-call(s32[4]{0:T(128)} %pad_add_fusion.where_ref, s32[8,16]{1,0:T(8,128)} %freq_ref.1, ...), custom_call_target="tpu_custom_call" | custom-call | tf_op jit(solution)/shard_map/attention_backward/pallas_call | solution.py:256
  73.3 0.0 copy-start.10
  73.3 5.9 %all-to-all-start.2 = ((bf16[16,256,128]{2,1,0:T(8,128)(2,1)}), bf16[16,256,128]{2,1,0:T(8,128)(2,1)S(1)}, u32[]{:S(2)}, u32[]{:S(2)}) async-start(bf16[16,256,128]{2,1,0:T(8,128)(2,1)} %get-tuple-element.35), calls=%async_computation.2 | async-start | bytes 2097152 | tf_op jit(solution)/shard_map/all_to_all | solution.py:408
  79.1 0.0 copy-done.10
  79.2 1.9 %collective-permute-start.4 = (bf16[16,16,512]{2,1,0:T(8,128)(2,1)S(1)}, bf16[16,16,512]{2,1,0:T(8,128)(2,1)S(1)}, u32[]{:S(2)}, u32[]{:S(2)}) collective-permute-start(bf16[16,16,512]{2,1,0:T(8,128)(2,1)S(1)} %copy-done.10), channel_id=1, source_target_pairs={{0,32},{32,0},{1,33},{33,1},{2,34},{34,2},{3,35},{35,3},{4,36},{36... | collective-permute-start | bytes 786440 | tf_op jit(solution)/shard_map/ppermute | solution.py:391
  81.1 1.5 collective-permute-done.4.dw1_ref
  82.6 0.0 copy-start.3
  82.6 12.7 %all-to-all-done.2.parts_ref = bf16[16,256,128]{2,1,0:T(8,128)(2,1)S(1)} async-done(((bf16[16,256,128]{2,1,0:T(8,128)(2,1)}), bf16[16,256,128]{2,1,0:T(8,128)(2,1)S(1)}, u32[]{:S(2)}, u32[]{:S(2)}) %all-to-all-start.2) | async-done | bytes 1048608 | tf_op jit(solution)/shard_map/all_to_all | solution.py:408
  95.2 0.0 copy-start.1
  95.2 0.0 copy-done.3
  95.2 1.0 copy-done.1
  96.2 2.2 %fold.1 = (f32[128,128]{1,0:T(8,128)}, bf16[384,128]{1,0:T(8,128)(2,1)}, bf16[16,16,512]{2,1,0:T(8,128)(2,1)}) custom-call(bf16[16,256,128]{2,1,0:T(8,128)(2,1)} %copy-done.1, bf16[16,16,512]{2,1,0:T(8,128)(2,1)} %get-tuple-element.36.dw0_ref, bf16[16,16,512]{2,1,0:T(8,128)(2,1)} %copy-done.3, bf16[4,64,128]{2,1,0:T(8,128)(2,1)} %get-tuple-element.38.kr_ref), custom_call_target="tpu_custom_call" | custom-call | tf_op jit(solution)/shard_map/fold/pallas_call | solution.py:300
  98.5 7.1 %collective-permute-start.5 = (bf16[384,128]{1,0:T(8,128)(2,1)}, bf16[384,128]{1,0:T(8,128)(2,1)S(1)}, u32[]{:S(2)}, u32[]{:S(2)}) collective-permute-start(bf16[384,128]{1,0:T(8,128)(2,1)} %get-tuple-element.41), channel_id=1, source_target_pairs={{0,16},{16,0},{1,17},{17,1},{2,18},{18,2},{3,19},{19,3},{4,20},{20... | collective-permute-start | bytes 294920 | tf_op jit(solution)/shard_map/ppermute | solution.py:391
  105.5 6.9 %all-to-all-start.3 = ((bf16[16,16,512]{2,1,0:T(8,128)(2,1)}), bf16[16,16,512]{2,1,0:T(8,128)(2,1)S(1)}, u32[]{:S(2)}, u32[]{:S(2)}) async-start(bf16[16,16,512]{2,1,0:T(8,128)(2,1)} %get-tuple-element.43), calls=%async_computation.3 | async-start | bytes 524288 | tf_op jit(solution)/shard_map/all_to_all | solution.py:411
  112.5 6.8 %collective-permute-done.5.other_ref = bf16[384,128]{1,0:T(8,128)(2,1)S(1)} collective-permute-done((bf16[384,128]{1,0:T(8,128)(2,1)}, bf16[384,128]{1,0:T(8,128)(2,1)S(1)}, u32[]{:S(2)}, u32[]{:S(2)}) %collective-permute-start.5) | collective-permute-done | bytes 98336 | tf_op jit(solution)/shard_map/ppermute | solution.py:391
  119.3 0.0 copy-start.13
  119.3 0.6 copy-done.13
  120.0 1.6 %merge.1 = (bf16[128,128]{1,0:T(8,128)(2,1)}, bf16[4,64,128]{2,1,0:T(8,128)(2,1)}) custom-call(f32[128,128]{1,0:T(8,128)} %get-tuple-element.39.own_ref, bf16[4,64,128]{2,1,0:T(8,128)(2,1)} %get-tuple-element.40.kr_ref, bf16[384,128]{1,0:T(8,128)(2,1)} %copy-done.13), custom_call_target="tpu_custom_call" | custom-call | flops 49999998976 | bytes 150000000 | tf_op jit(solution)/shard_map/merge/pallas_call | solution.py:319
  121.6 1.9 %collective-permute-start.8 = (bf16[128,128]{1,0:T(8,128)(2,1)}, bf16[128,128]{1,0:T(8,128)(2,1)S(1)}, u32[]{:S(2)}, u32[]{:S(2)}) collective-permute-start(bf16[128,128]{1,0:T(8,128)(2,1)} %get-tuple-element.44.q0_ref), channel_id=1, source_target_pairs={{0,3},{1,2},{2,1},{3,0},{4,7},{5,6},{6,5},{7,4},{8,11},{9,10},{10,... | collective-permute-start | bytes 98312 | tf_op jit(solution)/shard_map/ppermute | solution.py:391
  123.5 5.4 %collective-permute-start.7 = (bf16[128,128]{1,0:T(8,128)(2,1)}, bf16[128,128]{1,0:T(8,128)(2,1)S(1)}, u32[]{:S(2)}, u32[]{:S(2)}) collective-permute-start(bf16[128,128]{1,0:T(8,128)(2,1)} %get-tuple-element.44.q0_ref), channel_id=1, source_target_pairs={{0,2},{1,3},{2,0},{3,1},{4,6},{5,7},{6,4},{7,5},{8,10},{9,11},{10,... | collective-permute-start | bytes 98312 | tf_op jit(solution)/shard_map/ppermute | solution.py:391
  129.0 2.5 %collective-permute-start.6 = (bf16[128,128]{1,0:T(8,128)(2,1)}, bf16[128,128]{1,0:T(8,128)(2,1)S(1)}, u32[]{:S(2)}, u32[]{:S(2)}) collective-permute-start(bf16[128,128]{1,0:T(8,128)(2,1)} %get-tuple-element.44.q0_ref), channel_id=1, source_target_pairs={{0,1},{1,0},{2,3},{3,2},{4,5},{5,4},{6,7},{7,6},{8,9},{9,8},{10,11... | collective-permute-start | bytes 98312 | tf_op jit(solution)/shard_map/ppermute | solution.py:391
  131.4 0.0 collective-permute-done.8.q3_ref
  131.4 0.0 copy-start.7
  131.4 0.0 collective-permute-done.7.q2_ref
  131.5 0.0 copy-start.8
  131.5 3.5 %collective-permute-done.6.q1_ref = bf16[128,128]{1,0:T(8,128)(2,1)S(1)} collective-permute-done((bf16[128,128]{1,0:T(8,128)(2,1)}, bf16[128,128]{1,0:T(8,128)(2,1)S(1)}, u32[]{:S(2)}, u32[]{:S(2)}) %collective-permute-start.6) | collective-permute-done | bytes 32800 | tf_op jit(solution)/shard_map/ppermute | solution.py:391
  135.0 0.0 copy-start.9
  135.0 0.0 all-to-all-done.3.dw_ref
  135.0 0.0 copy-done.7
  135.0 0.0 copy-done.8
  135.0 0.6 copy-done.9
  135.6 0.1 copy-done.2
  135.7 1.9 %combine.1 = (bf16[4,336,128]{2,1,0:T(8,128)(2,1)}, bf16[128,512]{1,0:T(8,128)(2,1)}) custom-call(s32[4]{0:T(128)} %pad_add_fusion.where_ref, bf16[4,256,128]{2,1,0:T(8,128)(2,1)} %get-tuple-element.34.dq_ref, bf16[4,64,128]{2,1,0:T(8,128)(2,1)} %get-tuple-element.42.kr_ref, bf16[16,16,512]{2,1,0:T(8,128)(2,1)} %copy-done.2, ...), custom_call_target="tpu_custom_call" | custom-call | tf_op jit(solution)/shard_map/combine/pallas_call | solution.py:348
  137.6 11.3 %all_to_all.25.msg_ref = bf16[4,336,128]{2,1,0:T(8,128)(2,1)} all-to-all(bf16[4,336,128]{2,1,0:T(8,128)(2,1)} %get-tuple-element.45), channel_id=1, replica_groups=mesh['zl'=8,'core'=2,'zh'=2,'y'=4,'x'=4] {'y'}, dimensions={0} | all-to-all | bytes 688128 | tf_op jit(solution)/shard_map/all_to_all | solution.py:415
  148.9 1.8 %unpack.1 = (bf16[128,1024]{1,0:T(8,128)(2,1)}, bf16[128,256]{1,0:T(8,128)(2,1)}, bf16[4,768]{1,0:T(4,128)(2,1)}, bf16[4,1024]{1,0:T(4,128)(2,1)}) custom-call(bf16[4,336,128]{2,1,0:T(8,128)(2,1)} %all_to_all.25.msg_ref), custom_call_target="tpu_custom_call" | custom-call | tf_op jit(solution)/shard_map/unpack/pallas_call | solution.py:378
  (1 shorter events, 0.0 us)
Async XLA Ops:
  3.0 4.6 %copy-start.11 = (bf16[784,128]{1,0:T(8,128)(2,1)S(1)}, bf16[784,128]{1,0:T(8,128)(2,1)}, u32[]{:S(2)}) copy-start(bf16[784,128]{1,0:T(8,128)(2,1)} %get-tuple-element.29) | copy-start | bytes 602116
  3.0 20.9 %all-to-all-start = ((bf16[4,1120,128]{2,1,0:T(8,128)(2,1)}), bf16[4,1120,128]{2,1,0:T(8,128)(2,1)S(1)}, u32[]{:S(2)}, u32[]{:S(2)}) async-start(bf16[4,1120,128]{2,1,0:T(8,128)(2,1)} %get-tuple-element.28), calls=%async_computation | async-start | bytes 2293760 | tf_op jit(solution)/shard_map/all_to_all | solution.py:399
  7.6 33.8 %collective-permute-start = (bf16[784,128]{1,0:T(8,128)(2,1)S(1)}, bf16[784,128]{1,0:T(8,128)(2,1)S(1)}, u32[]{:S(2)}, u32[]{:S(2)}) collective-permute-start(bf16[784,128]{1,0:T(8,128)(2,1)S(1)} %copy-done.11), channel_id=1, source_target_pairs={{0,16},{16,0},{1,17},{17,1},{2,18},{18,2},{3,19},{19,3},{4,20},{20... | collective-permute-start | bytes 602120 | tf_op jit(solution)/shard_map/ppermute | solution.py:391
  23.9 1.0 copy-start
  26.4 34.2 %all-to-all-start.1 = ((bf16[16,64,128]{2,1,0:T(8,128)(2,1)}), bf16[16,64,128]{2,1,0:T(8,128)(2,1)S(1)}, u32[]{:S(2)}, u32[]{:S(2)}) async-start(bf16[16,64,128]{2,1,0:T(8,128)(2,1)} %spread.1), calls=%async_computation.1 | async-start | bytes 524288 | tf_op jit(solution)/shard_map/all_to_all | solution.py:400
  41.5 0.7 copy-start.12
  43.9 19.0 %collective-permute-start.1 = (bf16[592,128]{1,0:T(8,128)(2,1)}, bf16[592,128]{1,0:T(8,128)(2,1)S(1)}, u32[]{:S(2)}, u32[]{:S(2)}) collective-permute-start(bf16[592,128]{1,0:T(8,128)(2,1)} %get-tuple-element.31), channel_id=1, source_target_pairs={{0,4},{4,0},{8,12},{12,8},{1,5},{5,1},{9,13},{13,9},{2,6},{6,2},{1... | collective-permute-start | bytes 454664 | tf_op jit(solution)/shard_map/ppermute | solution.py:391
  46.4 16.6 %collective-permute-start.2 = (bf16[592,128]{1,0:T(8,128)(2,1)}, bf16[592,128]{1,0:T(8,128)(2,1)S(1)}, u32[]{:S(2)}, u32[]{:S(2)}) collective-permute-start(bf16[592,128]{1,0:T(8,128)(2,1)} %get-tuple-element.32), channel_id=1, source_target_pairs={{0,8},{4,12},{8,0},{12,4},{1,9},{5,13},{9,1},{13,5},{2,10},{6,14},... | collective-permute-start | bytes 454664 | tf_op jit(solution)/shard_map/ppermute | solution.py:391
  50.4 12.6 %collective-permute-start.3 = (bf16[592,128]{1,0:T(8,128)(2,1)}, bf16[592,128]{1,0:T(8,128)(2,1)S(1)}, u32[]{:S(2)}, u32[]{:S(2)}) collective-permute-start(bf16[592,128]{1,0:T(8,128)(2,1)} %get-tuple-element.33), channel_id=1, source_target_pairs={{0,12},{4,8},{8,4},{12,0},{1,13},{5,9},{9,5},{13,1},{2,14},{6,10},... | collective-permute-start | bytes 454664 | tf_op jit(solution)/shard_map/ppermute | solution.py:391
  63.0 0.7 copy-start.4
  63.0 0.7 copy-start.5
  63.0 0.7 copy-start.6
  73.3 5.9 %copy-start.10 = (bf16[16,16,512]{2,1,0:T(8,128)(2,1)S(1)}, bf16[16,16,512]{2,1,0:T(8,128)(2,1)}, u32[]{:S(2)}) copy-start(bf16[16,16,512]{2,1,0:T(8,128)(2,1)} %get-tuple-element.37) | copy-start | bytes 786436
  73.3 22.0 %all-to-all-start.2 = ((bf16[16,256,128]{2,1,0:T(8,128)(2,1)}), bf16[16,256,128]{2,1,0:T(8,128)(2,1)S(1)}, u32[]{:S(2)}, u32[]{:S(2)}) async-start(bf16[16,256,128]{2,1,0:T(8,128)(2,1)} %get-tuple-element.35), calls=%async_computation.2 | async-start | bytes 2097152 | tf_op jit(solution)/shard_map/all_to_all | solution.py:408
  79.2 3.4 %collective-permute-start.4 = (bf16[16,16,512]{2,1,0:T(8,128)(2,1)S(1)}, bf16[16,16,512]{2,1,0:T(8,128)(2,1)S(1)}, u32[]{:S(2)}, u32[]{:S(2)}) collective-permute-start(bf16[16,16,512]{2,1,0:T(8,128)(2,1)S(1)} %copy-done.10), channel_id=1, source_target_pairs={{0,32},{32,0},{1,33},{33,1},{2,34},{34,2},{3,35},{35,3},{4,36},{36... | collective-permute-start | bytes 786440 | tf_op jit(solution)/shard_map/ppermute | solution.py:391
  82.6 12.7 %copy-start.3 = (bf16[16,16,512]{2,1,0:T(8,128)(2,1)}, bf16[16,16,512]{2,1,0:T(8,128)(2,1)S(1)}, u32[]{:S(2)}) copy-start(bf16[16,16,512]{2,1,0:T(8,128)(2,1)S(1)} %collective-permute-done.4.dw1_ref) | copy-start | bytes 786436
  95.2 1.0 copy-start.1
  98.5 20.9 %collective-permute-start.5 = (bf16[384,128]{1,0:T(8,128)(2,1)}, bf16[384,128]{1,0:T(8,128)(2,1)S(1)}, u32[]{:S(2)}, u32[]{:S(2)}) collective-permute-start(bf16[384,128]{1,0:T(8,128)(2,1)} %get-tuple-element.41), channel_id=1, source_target_pairs={{0,16},{16,0},{1,17},{17,1},{2,18},{18,2},{3,19},{19,3},{4,20},{20... | collective-permute-start | bytes 294920 | tf_op jit(solution)/shard_map/ppermute | solution.py:391
  105.5 29.4 %all-to-all-start.3 = ((bf16[16,16,512]{2,1,0:T(8,128)(2,1)}), bf16[16,16,512]{2,1,0:T(8,128)(2,1)S(1)}, u32[]{:S(2)}, u32[]{:S(2)}) async-start(bf16[16,16,512]{2,1,0:T(8,128)(2,1)} %get-tuple-element.43), calls=%async_computation.3 | async-start | bytes 524288 | tf_op jit(solution)/shard_map/all_to_all | solution.py:411
  119.3 0.6 copy-start.13
  121.6 9.8 %collective-permute-start.8 = (bf16[128,128]{1,0:T(8,128)(2,1)}, bf16[128,128]{1,0:T(8,128)(2,1)S(1)}, u32[]{:S(2)}, u32[]{:S(2)}) collective-permute-start(bf16[128,128]{1,0:T(8,128)(2,1)} %get-tuple-element.44.q0_ref), channel_id=1, source_target_pairs={{0,3},{1,2},{2,1},{3,0},{4,7},{5,6},{6,5},{7,4},{8,11},{9,10},{10,... | collective-permute-start | bytes 98312 | tf_op jit(solution)/shard_map/ppermute | solution.py:391
  123.5 7.9 %collective-permute-start.7 = (bf16[128,128]{1,0:T(8,128)(2,1)}, bf16[128,128]{1,0:T(8,128)(2,1)S(1)}, u32[]{:S(2)}, u32[]{:S(2)}) collective-permute-start(bf16[128,128]{1,0:T(8,128)(2,1)} %get-tuple-element.44.q0_ref), channel_id=1, source_target_pairs={{0,2},{1,3},{2,0},{3,1},{4,6},{5,7},{6,4},{7,5},{8,10},{9,11},{10,... | collective-permute-start | bytes 98312 | tf_op jit(solution)/shard_map/ppermute | solution.py:391
  129.0 6.0 %collective-permute-start.6 = (bf16[128,128]{1,0:T(8,128)(2,1)}, bf16[128,128]{1,0:T(8,128)(2,1)S(1)}, u32[]{:S(2)}, u32[]{:S(2)}) collective-permute-start(bf16[128,128]{1,0:T(8,128)(2,1)} %get-tuple-element.44.q0_ref), channel_id=1, source_target_pairs={{0,1},{1,0},{2,3},{3,2},{4,5},{5,4},{6,7},{7,6},{8,9},{9,8},{10,11... | collective-permute-start | bytes 98312 | tf_op jit(solution)/shard_map/ppermute | solution.py:391
  131.4 3.5 %copy-start.7 = (bf16[128,128]{1,0:T(8,128)(2,1)}, bf16[128,128]{1,0:T(8,128)(2,1)S(1)}, u32[]{:S(2)}) copy-start(bf16[128,128]{1,0:T(8,128)(2,1)S(1)} %collective-permute-done.8.q3_ref) | copy-start | bytes 98308
  131.5 3.5 %copy-start.8 = (bf16[128,128]{1,0:T(8,128)(2,1)}, bf16[128,128]{1,0:T(8,128)(2,1)S(1)}, u32[]{:S(2)}) copy-start(bf16[128,128]{1,0:T(8,128)(2,1)S(1)} %collective-permute-done.7.q2_ref) | copy-start | bytes 98308
  135.0 0.6 copy-start.9
  135.0 0.7 copy-start.2

commit v5 on v4

--- a/solution.py
+++ b/solution.py
@@ -30,7 +30,7 @@
 KEY_K, KEY_S, KEY = 512, 768, 784
 PASS_S, PASS = 576, 592
 BK0, BW0, BACK = 256, 320, 336
-BLK = 256
+BLK = 512
 
 waits_for_z = pl.CostEstimate(flops=50_000_000_000, transcendentals=0, bytes_accessed=150_000_000)
 f32 = jnp.float32
@@ -287,12 +287,10 @@
     )(place, freq, msg, *keys, w)
 
 
-def fold_kernel(parts_ref, dw0_ref, dw1_ref, kr_ref, own_ref, other_ref, dw_ref):
+def fold_kernel(parts_ref, dw0_ref, dw1_ref, own_ref, other_ref, dw_ref):
     both = jnp.sum(parts_ref[...].astype(f32), 0)
     own_ref[...] = both[0:TOK]
-    other_ref[0:TOK, :] = both[TOK:].astype(bf16)
-    for y in range(NY):
-        other_ref[TOK + y * GRP * RD:TOK + (y + 1) * GRP * RD, :] = kr_ref[y]
+    other_ref[...] = both[TOK:].astype(bf16)
     dw_ref[...] = (dw0_ref[...].astype(f32) + dw1_ref[...].astype(f32)).astype(bf16)
 
 
@@ -301,18 +299,16 @@
         fold_kernel,
         out_shape=[
             jax.ShapeDtypeStruct((TOK, HD), f32),
-            jax.ShapeDtypeStruct((TOK + NY * GRP * RD, HD), bf16),
+            jax.ShapeDtypeStruct((TOK, HD), bf16),
             jax.ShapeDtypeStruct((NZ, NY * ROWS, 2 * GRP * HD), bf16),
         ],
         name="fold",
     )(*parts)
 
 
-def merge_kernel(own_ref, kr_ref, other_ref, quarter_ref, out_ref):
-    quarter_ref[...] = (own_ref[...] + other_ref[0:TOK, :].astype(f32)).astype(bf16)
-    for y in range(NY):
-        kr = other_ref[TOK + y * GRP * RD:TOK + (y + 1) * GRP * RD, :]
-        out_ref[y] = (kr_ref[y].astype(f32) + kr.astype(f32)).astype(bf16)
+def merge_kernel(own_ref, other_ref, kr0_ref, kr1_ref, quarter_ref, kr_ref):
+    quarter_ref[...] = (own_ref[...] + other_ref[...].astype(f32)).astype(bf16)
+    kr_ref[...] = (kr0_ref[...].astype(f32) + kr1_ref[...].astype(f32)).astype(bf16)
 
 
 def merge(*parts):
@@ -328,11 +324,14 @@
 
 
 def combine_kernel(
-    where_ref, dq_ref, kr_ref, dw_ref, q0_ref, q1_ref, q2_ref, q3_ref, out_ref, lat_ref
+    where_ref, dq_ref, kr_ref, dw_ref, q0_ref, q1_ref, pair_ref, out_ref, lat_ref
 ):
     x = where_ref[1]
-    for t, ref in enumerate((q0_ref, q1_ref, q2_ref, q3_ref)):
+    for t, ref in enumerate((q0_ref, q1_ref)):
         lat_ref[:, pl.ds(pl.multiple_of((x ^ t) * HD, HD), HD)] = ref[...]
+    for t in range(2):
+        cols = pl.ds(pl.multiple_of((x ^ 3 ^ t) * HD, HD), HD)
+        lat_ref[:, cols] = pair_ref[t * TOK:(t + 1) * TOK, :]
     dw = jnp.sum(dw_ref[...].astype(f32), 0)
     for y in range(NY):
         out_ref[y, 0:BK0, :] = dq_ref[y]
@@ -347,7 +346,7 @@
     vmem = pl.BlockSpec(memory_space=pltpu.VMEM)
     return pl.pallas_call(
         combine_kernel,
-        in_specs=[pl.BlockSpec(memory_space=pltpu.SMEM)] + [vmem] * (3 + TEN),
+        in_specs=[pl.BlockSpec(memory_space=pltpu.SMEM)] + [vmem] * 6,
         out_shape=[
             jax.ShapeDtypeStruct((NY, BACK, HD), bf16),
             jax.ShapeDtypeStruct((TOK, RANK), bf16),
@@ -406,12 +405,14 @@
 
     dw_other = swap(dw_other, "core", 2, 1)
     parts = lax.all_to_all(parts, ("y", "x"), 0, 0)
-    lat_own, other, dw = fold(parts, dw_own, dw_other, kr_other)
+    lat_own, other, dw = fold(parts, dw_own, dw_other)
     other = swap(other, "zh", 2, 1)
+    kr_other = swap(kr_other, "zh", 2, 1)
     dw = lax.all_to_all(dw, ("zl", "zh"), 0, 0)
-    quarter, kr = merge(lat_own, kr_own, other)
-    quarters = [quarter] + [swap(quarter, "x", TEN, t) for t in range(1, TEN)]
-    back, latent_grad = combine(place, dq, kr, dw, *quarters)
+    quarter, kr = merge(lat_own, other, kr_own, kr_other)
+    next_quarter = swap(quarter, "x", TEN, 1)
+    pair = swap(jnp.concatenate([quarter, next_quarter], 0), "x", TEN, 3)
+    back, latent_grad = combine(place, dq, kr, dw, quarter, next_quarter, pair)
     back = lax.all_to_all(back, "y", 0, 0)
     query_grad, key_rope_grad, up_key_grad, up_value_grad = unpack(back)
     return (query_grad[None], key_rope_grad[None], latent_grad[None], up_key_grad, up_value_grad)

time: 152 us -> 150 us (0.987)
  the two profiles are of different devices: /device:TPU:2 before, /device:TPU:32 now
where the time goes in v5:
time: 150 us; the launch traced here: 148 us
  starting transfers between devices  85.6 us (57%)
  Pallas kernels  22.2 us (15%)
  waiting for transfers between devices  20 us (13%)
  blocking collectives  13.6 us (9%)
  local copies, waits for them, and re-layouts  4.71 us (3%)
    ppermute x9, starting transfers between devices, swap(): return lax.ppermute(array, axis, [(i, i ^ flip) for i in range(size)])  52.3 us
    all_to_all x1, starting transfers between devices, body(): w = lax.all_to_all(spread(msg), ('zl', 'zh'), 0, 0)  15.2 us
    all_to_all x1, blocking collectives, body(): back = lax.all_to_all(back, 'y', 0, 0)  11.3 us
    ppermute x9, waiting for transfers between devices, swap(): return lax.ppermute(array, axis, [(i, i ^ flip) for i in range(size)])  9.19 us
    pallas_call x1, Pallas kernels, attention(): pl.pallas_call(main_kernel, in_specs=[smem] + [vmem] * 7, out_specs=[vmem...  9.09 us
    all_to_all x1, starting transfers between devices, body(): dw = lax.all_to_all(dw, ('zl', 'zh'), 0, 0)  7.45 us
    all_to_all x1, starting transfers between devices, body(): parts = lax.all_to_all(parts, ('y', 'x'), 0, 0)  6.02 us
    unnamed x30, local copies, waits for them, and re-layouts  4.71 us
  transfers between devices with their start and end apart: 13, of which 6 were waited for; matrix products, arithmetic and copies ran while one was open for 1% of the time, Pallas kernels for 5%

profile of v5, /device:TPU:32, one launch (start us, length us, event | category | flops | bytes accessed | tf_op | source)
XLA Modules:
  0.0 148.4 jit_solution(15370791995484099359)
XLA Ops:
  0.6 2.4 %pack.1 = (bf16[4,1120,128]{2,1,0:T(8,128)(2,1)}, bf16[784,128]{1,0:T(8,128)(2,1)}) custom-call(bf16[128,1024]{1,0:T(8,128)(2,1)} %bitcast.13, bf16[128,1024]{1,0:T(8,128)(2,1)} %bitcast.14, bf16[128,256]{1,0:T(8,128)(2,1)} %bitcast.16, bf16[128,512]{1,0:T(8,128)(2,1)} %bitcast.15, bf16[4,768]{1,0:T(4,128)(2,1)} %wk_ref.1, bf16[4,1024]{1,0:T(4,128)(2,1)} %wv_ref.1, ...), custom_call_target="tpu_custom_call" | custom-call | tf_op jit(solution)/shard_map/pack/pallas_call | solution.py:76
  3.0 0.0 copy-start.10
  3.0 4.6 %all-to-all-start = ((bf16[4,1120,128]{2,1,0:T(8,128)(2,1)}), bf16[4,1120,128]{2,1,0:T(8,128)(2,1)S(1)}, u32[]{:S(2)}, u32[]{:S(2)}) async-start(bf16[4,1120,128]{2,1,0:T(8,128)(2,1)} %get-tuple-element.28), calls=%async_computation | async-start | bytes 2293760 | tf_op jit(solution)/shard_map/all_to_all | solution.py:398
  7.6 0.0 copy-done.10
  7.6 14.8 %collective-permute-start = (bf16[784,128]{1,0:T(8,128)(2,1)S(1)}, bf16[784,128]{1,0:T(8,128)(2,1)S(1)}, u32[]{:S(2)}, u32[]{:S(2)}) collective-permute-start(bf16[784,128]{1,0:T(8,128)(2,1)S(1)} %copy-done.10), channel_id=1, source_target_pairs={{0,16},{16,0},{1,17},{17,1},{2,18},{18,2},{3,19},{19,3},{4,20},{20... | collective-permute-start | bytes 602120 | tf_op jit(solution)/shard_map/ppermute | solution.py:390
  22.4 0.7 pad_add_fusion.where_ref
  23.1 0.7 all-to-all-done.msg_ref
  23.8 0.0 copy-start
  23.8 1.0 copy-done
  24.8 1.4 spread.1
  26.2 15.2 %all-to-all-start.1 = ((bf16[16,64,128]{2,1,0:T(8,128)(2,1)}), bf16[16,64,128]{2,1,0:T(8,128)(2,1)S(1)}, u32[]{:S(2)}, u32[]{:S(2)}) async-start(bf16[16,64,128]{2,1,0:T(8,128)(2,1)} %spread.1), calls=%async_computation.1 | async-start | bytes 524288 | tf_op jit(solution)/shard_map/all_to_all | solution.py:399
  41.4 0.0 collective-permute-done.key_ref
  41.4 0.0 copy-start.11
  41.5 0.7 copy-done.11
  42.1 1.8 %relay.1 = (bf16[592,128]{1,0:T(8,128)(2,1)}, bf16[592,128]{1,0:T(8,128)(2,1)}, bf16[592,128]{1,0:T(8,128)(2,1)}, bf16[592,128]{1,0:T(8,128)(2,1)}) custom-call(s32[4]{0:T(128)} %pad_add_fusion.where_ref, bf16[784,128]{1,0:T(8,128)(2,1)} %copy-done.11), custom_call_target="tpu_custom_call" | custom-call | flops 49999998976 | bytes 150000000 | tf_op jit(solution)/shard_map/relay/pallas_call | solution.py:115
  43.9 2.5 %collective-permute-start.1 = (bf16[592,128]{1,0:T(8,128)(2,1)}, bf16[592,128]{1,0:T(8,128)(2,1)S(1)}, u32[]{:S(2)}, u32[]{:S(2)}) collective-permute-start(bf16[592,128]{1,0:T(8,128)(2,1)} %get-tuple-element.31), channel_id=1, source_target_pairs={{0,4},{4,0},{8,12},{12,8},{1,5},{5,1},{9,13},{13,9},{2,6},{6,2},{1... | collective-permute-start | bytes 454664 | tf_op jit(solution)/shard_map/ppermute | solution.py:390
  46.4 4.0 %collective-permute-start.2 = (bf16[592,128]{1,0:T(8,128)(2,1)}, bf16[592,128]{1,0:T(8,128)(2,1)S(1)}, u32[]{:S(2)}, u32[]{:S(2)}) collective-permute-start(bf16[592,128]{1,0:T(8,128)(2,1)} %get-tuple-element.32), channel_id=1, source_target_pairs={{0,8},{4,12},{8,0},{12,4},{1,9},{5,13},{9,1},{13,5},{2,10},{6,14},... | collective-permute-start | bytes 454664 | tf_op jit(solution)/shard_map/ppermute | solution.py:390
  50.4 4.0 %collective-permute-start.3 = (bf16[592,128]{1,0:T(8,128)(2,1)}, bf16[592,128]{1,0:T(8,128)(2,1)S(1)}, u32[]{:S(2)}, u32[]{:S(2)}) collective-permute-start(bf16[592,128]{1,0:T(8,128)(2,1)} %get-tuple-element.33), channel_id=1, source_target_pairs={{0,12},{4,8},{8,4},{12,0},{1,13},{5,9},{9,5},{13,1},{2,14},{6,10},... | collective-permute-start | bytes 454664 | tf_op jit(solution)/shard_map/ppermute | solution.py:390
  54.4 2.5 %all-to-all-done.1 = bf16[16,64,128]{2,1,0:T(8,128)(2,1)S(1)} async-done(((bf16[16,64,128]{2,1,0:T(8,128)(2,1)}), bf16[16,64,128]{2,1,0:T(8,128)(2,1)S(1)}, u32[]{:S(2)}, u32[]{:S(2)}) %all-to-all-start.1) | async-done | bytes 262176 | tf_op jit(solution)/shard_map/all_to_all | solution.py:399
  56.9 2.3 %all-gather = bf16[32,64,128]{2,1,0:T(8,128)(2,1)} all-gather(bf16[16,64,128]{2,1,0:T(8,128)(2,1)S(1)} %all-to-all-done.1), channel_id=2, replica_groups=mesh['zl'=8,'core'=2,'zh'=2,'y'=4,'x'=4] {'core'}, dimensions={0}, use_global_device_ids=true | all-gather | bytes 786432 | tf_op jit(solution)/shard_map/all_gather | solution.py:402
  59.2 0.0 collective-permute-done.1.key1_ref
  59.2 0.0 copy-start.4
  59.2 0.0 collective-permute-done.2.key2_ref
  59.2 0.0 copy-start.5
  59.2 0.0 collective-permute-done.3.key3_ref
  59.3 0.0 copy-start.6
  59.3 0.6 copy-done.4
  59.9 0.0 copy-done.5
  59.9 0.1 copy-done.6
  60.0 9.1 %attention_backward.1 = (bf16[16,256,128]{2,1,0:T(8,128)(2,1)}, bf16[4,256,128]{2,1,0:T(8,128)(2,1)}, bf16[4,64,128]{2,1,0:T(8,128)(2,1)}, bf16[4,64,128]{2,1,0:...) custom-call(s32[4]{0:T(128)} %pad_add_fusion.where_ref, s32[8,16]{1,0:T(8,128)} %freq_ref.1, ...), custom_call_target="tpu_custom_call" | custom-call | tf_op jit(solution)/shard_map/attention_backward/pallas_call | solution.py:256
  69.1 0.0 copy-start.9
  69.1 0.0 copy-start.12
  69.1 6.0 %all-to-all-start.2 = ((bf16[16,256,128]{2,1,0:T(8,128)(2,1)}), bf16[16,256,128]{2,1,0:T(8,128)(2,1)S(1)}, u32[]{:S(2)}, u32[]{:S(2)}) async-start(bf16[16,256,128]{2,1,0:T(8,128)(2,1)} %get-tuple-element.35), calls=%async_computation.2 | async-start | bytes 2097152 | tf_op jit(solution)/shard_map/all_to_all | solution.py:407
  75.1 0.0 copy-done.9
  75.1 1.9 %collective-permute-start.4 = (bf16[16,16,512]{2,1,0:T(8,128)(2,1)S(1)}, bf16[16,16,512]{2,1,0:T(8,128)(2,1)S(1)}, u32[]{:S(2)}, u32[]{:S(2)}) collective-permute-start(bf16[16,16,512]{2,1,0:T(8,128)(2,1)S(1)} %copy-done.9), channel_id=1, source_target_pairs={{0,32},{32,0},{1,33},{33,1},{2,34},{34,2},{3,35},{35,3},{4,36},{36... | collective-permute-start | bytes 786440 | tf_op jit(solution)/shard_map/ppermute | solution.py:390
  77.1 0.0 copy-done.12
  77.1 11.2 %collective-permute-start.6 = (bf16[4,64,128]{2,1,0:T(8,128)(2,1)S(1)}, bf16[4,64,128]{2,1,0:T(8,128)(2,1)S(1)}, u32[]{:S(2)}, u32[]{:S(2)}) collective-permute-start(bf16[4,64,128]{2,1,0:T(8,128)(2,1)S(1)} %copy-done.12), channel_id=1, source_target_pairs={{0,16},{16,0},{1,17},{17,1},{2,18},{18,2},{3,19},{19,3},{4,20},{20... | collective-permute-start | bytes 196616 | tf_op jit(solution)/shard_map/ppermute | solution.py:390
  88.3 0.0 collective-permute-done.4.dw1_ref
  88.3 0.0 copy-start.3
  88.3 4.6 %all-to-all-done.2.parts_ref = bf16[16,256,128]{2,1,0:T(8,128)(2,1)S(1)} async-done(((bf16[16,256,128]{2,1,0:T(8,128)(2,1)}), bf16[16,256,128]{2,1,0:T(8,128)(2,1)S(1)}, u32[]{:S(2)}, u32[]{:S(2)}) %all-to-all-start.2) | async-done | bytes 1048608 | tf_op jit(solution)/shard_map/all_to_all | solution.py:407
  92.9 0.0 copy-done.3
  92.9 1.0 copy-done.1
  93.9 2.2 %fold.1 = (f32[128,128]{1,0:T(8,128)}, bf16[128,128]{1,0:T(8,128)(2,1)}, bf16[16,16,512]{2,1,0:T(8,128)(2,1)}) custom-call(bf16[16,256,128]{2,1,0:T(8,128)(2,1)} %copy-done.1, bf16[16,16,512]{2,1,0:T(8,128)(2,1)} %get-tuple-element.36.dw0_ref, bf16[16,16,512]{2,1,0:T(8,128)(2,1)} %copy-done.3), custom_call_target="tpu_custom_call" | custom-call | tf_op jit(solution)/shard_map/fold/pallas_call | solution.py:298
  96.1 9.7 %collective-permute-start.5 = (bf16[128,128]{1,0:T(8,128)(2,1)}, bf16[128,128]{1,0:T(8,128)(2,1)S(1)}, u32[]{:S(2)}, u32[]{:S(2)}) collective-permute-start(bf16[128,128]{1,0:T(8,128)(2,1)} %get-tuple-element.39), channel_id=1, source_target_pairs={{0,16},{16,0},{1,17},{17,1},{2,18},{18,2},{3,19},{19,3},{4,20},{20... | collective-permute-start | bytes 98312 | tf_op jit(solution)/shard_map/ppermute | solution.py:390
  105.9 7.5 %all-to-all-start.3 = ((bf16[16,16,512]{2,1,0:T(8,128)(2,1)}), bf16[16,16,512]{2,1,0:T(8,128)(2,1)S(1)}, u32[]{:S(2)}, u32[]{:S(2)}) async-start(bf16[16,16,512]{2,1,0:T(8,128)(2,1)} %get-tuple-element.43), calls=%async_computation.3 | async-start | bytes 524288 | tf_op jit(solution)/shard_map/all_to_all | solution.py:411
  113.3 0.0 collective-permute-done.6.kr1_ref
  113.3 0.0 copy-start.13
  113.4 0.0 collective-permute-done.5.other_ref
  113.4 0.0 copy-start.14
  113.4 0.6 copy-done.13
  114.0 0.0 copy-done.14
  114.0 1.6 %merge.1 = (bf16[128,128]{1,0:T(8,128)(2,1)}, bf16[4,64,128]{2,1,0:T(8,128)(2,1)}) custom-call(f32[128,128]{1,0:T(8,128)} %get-tuple-element.38.own_ref, bf16[128,128]{1,0:T(8,128)(2,1)} %copy-done.14, bf16[4,64,128]{2,1,0:T(8,128)(2,1)} %get-tuple-element.40.kr0_ref, bf16[4,64,128]{2,1,0:T(8,128)(2,1)} %copy-done.13), custom_call_target="tpu_custom_call" | custom-call | flops 49999998976 | bytes 150000000 | tf_op jit(solution)/shard_map/merge/pallas_call | solution.py:315
  115.5 2.1 %collective-permute-start.7 = (bf16[128,128]{1,0:T(8,128)(2,1)}, bf16[128,128]{1,0:T(8,128)(2,1)S(1)}, u32[]{:S(2)}, u32[]{:S(2)}) collective-permute-start(bf16[128,128]{1,0:T(8,128)(2,1)} %get-tuple-element.44.q0_ref), channel_id=1, source_target_pairs={{0,1},{1,0},{2,3},{3,2},{4,5},{5,4},{6,7},{7,6},{8,9},{9,8},{10,11... | collective-permute-start | bytes 98312 | tf_op jit(solution)/shard_map/ppermute | solution.py:390
  117.7 3.9 %collective-permute-done.7.q1_ref = bf16[128,128]{1,0:T(8,128)(2,1)S(1)} collective-permute-done((bf16[128,128]{1,0:T(8,128)(2,1)}, bf16[128,128]{1,0:T(8,128)(2,1)S(1)}, u32[]{:S(2)}, u32[]{:S(2)}) %collective-permute-start.7) | collective-permute-done | bytes 32800 | tf_op jit(solution)/shard_map/ppermute | solution.py:390
  121.5 0.8 pad_maximum_fusion
  122.3 2.1 %collective-permute-start.8 = (bf16[256,128]{1,0:T(8,128)(2,1)S(1)}, bf16[256,128]{1,0:T(8,128)(2,1)S(1)}, u32[]{:S(2)}, u32[]{:S(2)}) collective-permute-start(bf16[256,128]{1,0:T(8,128)(2,1)S(1)} %pad_maximum_fusion), channel_id=1, source_target_pairs={{0,3},{1,2},{2,1},{3,0},{4,7},{5,6},{6,5},{7,4},{8,11},{9,10},{10,... | collective-permute-start | bytes 196616 | tf_op jit(solution)/shard_map/ppermute | solution.py:390
  124.4 5.3 %collective-permute-done.8.pair_ref = bf16[256,128]{1,0:T(8,128)(2,1)S(1)} collective-permute-done((bf16[256,128]{1,0:T(8,128)(2,1)S(1)}, bf16[256,128]{1,0:T(8,128)(2,1)S(1)}, u32[]{:S(2)}, u32[]{:S(2)}) %collective-permute-start.8) | collective-permute-done | bytes 65568 | tf_op jit(solution)/shard_map/ppermute | solution.py:390
  129.7 3.0 %all-to-all-done.3.dw_ref = bf16[16,16,512]{2,1,0:T(8,128)(2,1)S(1)} async-done(((bf16[16,16,512]{2,1,0:T(8,128)(2,1)}), bf16[16,16,512]{2,1,0:T(8,128)(2,1)S(1)}, u32[]{:S(2)}, u32[]{:S(2)}) %all-to-all-start.3) | async-done | bytes 262176 | tf_op jit(solution)/shard_map/all_to_all | solution.py:411
  132.7 0.0 copy-done.7
  132.7 0.0 copy-done.8
  132.7 0.7 copy-done.2
  133.4 1.9 %combine.1 = (bf16[4,336,128]{2,1,0:T(8,128)(2,1)}, bf16[128,512]{1,0:T(8,128)(2,1)}) custom-call(s32[4]{0:T(128)} %pad_add_fusion.where_ref, bf16[4,256,128]{2,1,0:T(8,128)(2,1)} %get-tuple-element.34.dq_ref, bf16[4,64,128]{2,1,0:T(8,128)(2,1)} %get-tuple-element.42.kr_ref, bf16[16,16,512]{2,1,0:T(8,128)(2,1)} %copy-done.2, ...), custom_call_target="tpu_custom_call" | custom-call | tf_op jit(solution)/shard_map/combine/pallas_call | solution.py:347
  135.3 11.3 %all_to_all.25.msg_ref = bf16[4,336,128]{2,1,0:T(8,128)(2,1)} all-to-all(bf16[4,336,128]{2,1,0:T(8,128)(2,1)} %get-tuple-element.45), channel_id=1, replica_groups=mesh['zl'=8,'core'=2,'zh'=2,'y'=4,'x'=4] {'y'}, dimensions={0} | all-to-all | bytes 688128 | tf_op jit(solution)/shard_map/all_to_all | solution.py:416
  146.6 1.8 %unpack.1 = (bf16[128,1024]{1,0:T(8,128)(2,1)}, bf16[128,256]{1,0:T(8,128)(2,1)}, bf16[4,768]{1,0:T(4,128)(2,1)}, bf16[4,1024]{1,0:T(4,128)(2,1)}) custom-call(bf16[4,336,128]{2,1,0:T(8,128)(2,1)} %all_to_all.25.msg_ref), custom_call_target="tpu_custom_call" | custom-call | tf_op jit(solution)/shard_map/unpack/pallas_call | solution.py:377
  (4 shorter events, 0.0 us)
Async XLA Ops:
  3.0 4.6 %copy-start.10 = (bf16[784,128]{1,0:T(8,128)(2,1)S(1)}, bf16[784,128]{1,0:T(8,128)(2,1)}, u32[]{:S(2)}) copy-start(bf16[784,128]{1,0:T(8,128)(2,1)} %get-tuple-element.29) | copy-start | bytes 602116
  3.0 20.7 %all-to-all-start = ((bf16[4,1120,128]{2,1,0:T(8,128)(2,1)}), bf16[4,1120,128]{2,1,0:T(8,128)(2,1)S(1)}, u32[]{:S(2)}, u32[]{:S(2)}) async-start(bf16[4,1120,128]{2,1,0:T(8,128)(2,1)} %get-tuple-element.28), calls=%async_computation | async-start | bytes 2293760 | tf_op jit(solution)/shard_map/all_to_all | solution.py:398
  7.6 33.8 %collective-permute-start = (bf16[784,128]{1,0:T(8,128)(2,1)S(1)}, bf16[784,128]{1,0:T(8,128)(2,1)S(1)}, u32[]{:S(2)}, u32[]{:S(2)}) collective-permute-start(bf16[784,128]{1,0:T(8,128)(2,1)S(1)} %copy-done.10), channel_id=1, source_target_pairs={{0,16},{16,0},{1,17},{17,1},{2,18},{18,2},{3,19},{19,3},{4,20},{20... | collective-permute-start | bytes 602120 | tf_op jit(solution)/shard_map/ppermute | solution.py:390
  23.8 1.0 copy-start
  26.2 30.7 %all-to-all-start.1 = ((bf16[16,64,128]{2,1,0:T(8,128)(2,1)}), bf16[16,64,128]{2,1,0:T(8,128)(2,1)S(1)}, u32[]{:S(2)}, u32[]{:S(2)}) async-start(bf16[16,64,128]{2,1,0:T(8,128)(2,1)} %spread.1), calls=%async_computation.1 | async-start | bytes 524288 | tf_op jit(solution)/shard_map/all_to_all | solution.py:399
  41.4 0.7 copy-start.11
  43.9 15.3 %collective-permute-start.1 = (bf16[592,128]{1,0:T(8,128)(2,1)}, bf16[592,128]{1,0:T(8,128)(2,1)S(1)}, u32[]{:S(2)}, u32[]{:S(2)}) collective-permute-start(bf16[592,128]{1,0:T(8,128)(2,1)} %get-tuple-element.31), channel_id=1, source_target_pairs={{0,4},{4,0},{8,12},{12,8},{1,5},{5,1},{9,13},{13,9},{2,6},{6,2},{1... | collective-permute-start | bytes 454664 | tf_op jit(solution)/shard_map/ppermute | solution.py:390
  46.4 12.8 %collective-permute-start.2 = (bf16[592,128]{1,0:T(8,128)(2,1)}, bf16[592,128]{1,0:T(8,128)(2,1)S(1)}, u32[]{:S(2)}, u32[]{:S(2)}) collective-permute-start(bf16[592,128]{1,0:T(8,128)(2,1)} %get-tuple-element.32), channel_id=1, source_target_pairs={{0,8},{4,12},{8,0},{12,4},{1,9},{5,13},{9,1},{13,5},{2,10},{6,14},... | collective-permute-start | bytes 454664 | tf_op jit(solution)/shard_map/ppermute | solution.py:390
  50.4 8.9 %collective-permute-start.3 = (bf16[592,128]{1,0:T(8,128)(2,1)}, bf16[592,128]{1,0:T(8,128)(2,1)S(1)}, u32[]{:S(2)}, u32[]{:S(2)}) collective-permute-start(bf16[592,128]{1,0:T(8,128)(2,1)} %get-tuple-element.33), channel_id=1, source_target_pairs={{0,12},{4,8},{8,4},{12,0},{1,13},{5,9},{9,5},{13,1},{2,14},{6,10},... | collective-permute-start | bytes 454664 | tf_op jit(solution)/shard_map/ppermute | solution.py:390
  59.2 0.7 copy-start.4
  59.2 0.7 copy-start.5
  59.3 0.7 copy-start.6
  69.1 6.0 %copy-start.9 = (bf16[16,16,512]{2,1,0:T(8,128)(2,1)S(1)}, bf16[16,16,512]{2,1,0:T(8,128)(2,1)}, u32[]{:S(2)}) copy-start(bf16[16,16,512]{2,1,0:T(8,128)(2,1)} %get-tuple-element.37) | copy-start | bytes 786436
  69.1 8.0 %copy-start.12 = (bf16[4,64,128]{2,1,0:T(8,128)(2,1)S(1)}, bf16[4,64,128]{2,1,0:T(8,128)(2,1)}, u32[]{:S(2)}) copy-start(bf16[4,64,128]{2,1,0:T(8,128)(2,1)} %get-tuple-element.41) | copy-start | bytes 196612
  69.1 23.8 %all-to-all-start.2 = ((bf16[16,256,128]{2,1,0:T(8,128)(2,1)}), bf16[16,256,128]{2,1,0:T(8,128)(2,1)S(1)}, u32[]{:S(2)}, u32[]{:S(2)}) async-start(bf16[16,256,128]{2,1,0:T(8,128)(2,1)} %get-tuple-element.35), calls=%async_computation.2 | async-start | bytes 2097152 | tf_op jit(solution)/shard_map/all_to_all | solution.py:407
  75.1 13.2 %collective-permute-start.4 = (bf16[16,16,512]{2,1,0:T(8,128)(2,1)S(1)}, bf16[16,16,512]{2,1,0:T(8,128)(2,1)S(1)}, u32[]{:S(2)}, u32[]{:S(2)}) collective-permute-start(bf16[16,16,512]{2,1,0:T(8,128)(2,1)S(1)} %copy-done.9), channel_id=1, source_target_pairs={{0,32},{32,0},{1,33},{33,1},{2,34},{34,2},{3,35},{35,3},{4,36},{36... | collective-permute-start | bytes 786440 | tf_op jit(solution)/shard_map/ppermute | solution.py:390
  77.1 36.3 %collective-permute-start.6 = (bf16[4,64,128]{2,1,0:T(8,128)(2,1)S(1)}, bf16[4,64,128]{2,1,0:T(8,128)(2,1)S(1)}, u32[]{:S(2)}, u32[]{:S(2)}) collective-permute-start(bf16[4,64,128]{2,1,0:T(8,128)(2,1)S(1)} %copy-done.12), channel_id=1, source_target_pairs={{0,16},{16,0},{1,17},{17,1},{2,18},{18,2},{3,19},{19,3},{4,20},{20... | collective-permute-start | bytes 196616 | tf_op jit(solution)/shard_map/ppermute | solution.py:390
  88.3 4.6 %copy-start.3 = (bf16[16,16,512]{2,1,0:T(8,128)(2,1)}, bf16[16,16,512]{2,1,0:T(8,128)(2,1)S(1)}, u32[]{:S(2)}) copy-start(bf16[16,16,512]{2,1,0:T(8,128)(2,1)S(1)} %collective-permute-done.4.dw1_ref) | copy-start | bytes 786436
  92.9 1.0 copy-start.1
  96.1 17.2 %collective-permute-start.5 = (bf16[128,128]{1,0:T(8,128)(2,1)}, bf16[128,128]{1,0:T(8,128)(2,1)S(1)}, u32[]{:S(2)}, u32[]{:S(2)}) collective-permute-start(bf16[128,128]{1,0:T(8,128)(2,1)} %get-tuple-element.39), channel_id=1, source_target_pairs={{0,16},{16,0},{1,17},{17,1},{2,18},{18,2},{3,19},{19,3},{4,20},{20... | collective-permute-start | bytes 98312 | tf_op jit(solution)/shard_map/ppermute | solution.py:390
  105.9 26.8 %all-to-all-start.3 = ((bf16[16,16,512]{2,1,0:T(8,128)(2,1)}), bf16[16,16,512]{2,1,0:T(8,128)(2,1)S(1)}, u32[]{:S(2)}, u32[]{:S(2)}) async-start(bf16[16,16,512]{2,1,0:T(8,128)(2,1)} %get-tuple-element.43), calls=%async_computation.3 | async-start | bytes 524288 | tf_op jit(solution)/shard_map/all_to_all | solution.py:411
  113.3 0.6 copy-start.13
  113.4 0.6 copy-start.14
  115.5 6.0 %collective-permute-start.7 = (bf16[128,128]{1,0:T(8,128)(2,1)}, bf16[128,128]{1,0:T(8,128)(2,1)S(1)}, u32[]{:S(2)}, u32[]{:S(2)}) collective-permute-start(bf16[128,128]{1,0:T(8,128)(2,1)} %get-tuple-element.44.q0_ref), channel_id=1, source_target_pairs={{0,1},{1,0},{2,3},{3,2},{4,5},{5,4},{6,7},{7,6},{8,9},{9,8},{10,11... | collective-permute-start | bytes 98312 | tf_op jit(solution)/shard_map/ppermute | solution.py:390
  121.5 11.2 %copy-start.7 = (bf16[128,128]{1,0:T(8,128)(2,1)}, bf16[128,128]{1,0:T(8,128)(2,1)S(1)}, u32[]{:S(2)}) copy-start(bf16[128,128]{1,0:T(8,128)(2,1)S(1)} %collective-permute-done.7.q1_ref) | copy-start | bytes 98308
  122.3 7.4 %collective-permute-start.8 = (bf16[256,128]{1,0:T(8,128)(2,1)S(1)}, bf16[256,128]{1,0:T(8,128)(2,1)S(1)}, u32[]{:S(2)}, u32[]{:S(2)}) collective-permute-start(bf16[256,128]{1,0:T(8,128)(2,1)S(1)} %pad_maximum_fusion), channel_id=1, source_target_pairs={{0,3},{1,2},{2,1},{3,0},{4,7},{5,6},{6,5},{7,4},{8,11},{9,10},{10,... | collective-permute-start | bytes 196616 | tf_op jit(solution)/shard_map/ppermute | solution.py:390
  129.7 3.1 %copy-start.8 = (bf16[256,128]{1,0:T(8,128)(2,1)}, bf16[256,128]{1,0:T(8,128)(2,1)S(1)}, u32[]{:S(2)}) copy-start(bf16[256,128]{1,0:T(8,128)(2,1)S(1)} %collective-permute-done.8.pair_ref) | copy-start | bytes 196612
  132.7 0.7 copy-start.2

commit v6 on v5

--- a/solution.py
+++ b/solution.py
@@ -81,25 +81,6 @@
         ],
         name="pack",
     )(*parts)
-
-
-def spread_kernel(msg_ref, w_ref):
-    tails = [msg_ref[y].astype(f32) for y in range(NY)]
-    rows = [tails[y][c * ROWS:(c + 1) * ROWS] for c in range(2 * GRP) for y in range(NY)]
-    block = jnp.concatenate(rows, 0).astype(bf16)
-    for z in range(NZ):
-        w_ref[z] = block
-
-
-def spread(msg):
-    return pl.pallas_call(
-        spread_kernel,
-        grid=(1,),
-        in_specs=[pl.BlockSpec((NY, MSG - W0, HD), lambda i: (0, W0 // (MSG - W0), 0))],
-        out_specs=pl.BlockSpec(memory_space=pltpu.VMEM),
-        out_shape=jax.ShapeDtypeStruct((NZ, 2 * GRP * NY * ROWS, HD), bf16),
-        name="spread",
-    )(msg)
 
 
 def relay_kernel(where_ref, key_ref, *out_refs):
@@ -287,23 +268,27 @@
     )(place, freq, msg, *keys, w)
 
 
-def fold_kernel(parts_ref, dw0_ref, dw1_ref, own_ref, other_ref, dw_ref):
+def fold_kernel(parts_ref, dw_ref, own_ref, other_ref, passed_ref):
     both = jnp.sum(parts_ref[...].astype(f32), 0)
     own_ref[...] = both[0:TOK]
     other_ref[...] = both[TOK:].astype(bf16)
-    dw_ref[...] = (dw0_ref[...].astype(f32) + dw1_ref[...].astype(f32)).astype(bf16)
-
-
-def fold(*parts):
+
+
+def fold(parts, dw):
+    vmem = pl.BlockSpec(memory_space=pltpu.VMEM)
+    whole = pl.BlockSpec(memory_space=pl.ANY)
     return pl.pallas_call(
         fold_kernel,
+        in_specs=[vmem, whole],
+        out_specs=[vmem, vmem, whole],
         out_shape=[
             jax.ShapeDtypeStruct((TOK, HD), f32),
             jax.ShapeDtypeStruct((TOK, HD), bf16),
-            jax.ShapeDtypeStruct((NZ, NY * ROWS, 2 * GRP * HD), bf16),
-        ],
+            jax.ShapeDtypeStruct(dw.shape, bf16),
+        ],
+        input_output_aliases={1: 2},
         name="fold",
-    )(*parts)
+    )(parts, dw)
 
 
 def merge_kernel(own_ref, other_ref, kr0_ref, kr1_ref, quarter_ref, kr_ref):
@@ -396,16 +381,18 @@
     msg, own = pack(query[0], out_grad[0], key_rope[0], latent[0], up_key, up_value, positions)
     other = swap(own, "zh", 2, 1)
     msg = lax.all_to_all(msg, "y", 0, 0)
-    w = lax.all_to_all(spread(msg), ("zl", "zh"), 0, 0)
+    w = msg[:, W0:MSG, :].reshape(NY, 2 * GRP, ROWS, HD).transpose(1, 0, 2, 3)
+    w = w.reshape(1, 2 * GRP * NY * ROWS, HD)
+    w = lax.all_to_all(jnp.broadcast_to(w, (NZ,) + w.shape[1:]), ("zl", "zh"), 0, 0)
     keys = relay(place, other)
     keys = [keys[0]] + [swap(keys[t], "y", NY, t) for t in range(1, NY)]
     w = lax.all_gather(w, "core", axis=0)
 
     parts, dq, kr_own, kr_other, dw_own, dw_other = attention(place, freq_index, msg, keys, w)
 
-    dw_other = swap(dw_other, "core", 2, 1)
+    dw = (dw_own.astype(f32) + swap(dw_other, "core", 2, 1).astype(f32)).astype(bf16)
     parts = lax.all_to_all(parts, ("y", "x"), 0, 0)
-    lat_own, other, dw = fold(parts, dw_own, dw_other)
+    lat_own, other, dw = fold(parts, dw)
     other = swap(other, "zh", 2, 1)
     kr_other = swap(kr_other, "zh", 2, 1)
     dw = lax.all_to_all(dw, ("zl", "zh"), 0, 0)

time: 150 us -> 148 us (0.987)
  Pallas kernels: 22.2 us -> 20.5 us
    ppermute x9, waiting for transfers between devices: 9.19 us -> 11.9 us  [swap(): return lax.ppermute(array, axis, [(i, i ^ flip) for i in range(size)])]
    all_to_all x1, starting transfers between devices: 7.45 us -> 4.89 us  [body(): dw = lax.all_to_all(dw, ('zl', 'zh'), 0, 0)]
    pallas_call x2 -> x1, Pallas kernels: 3.68 us -> 1.97 us  [fold(): pl.pallas_call(fold_kernel, in_specs=[vmem, whole], out_specs=[vmem, vmem...]
  transfers between devices with their start and end apart: 13 -> 13, of which waited for: 6 -> 8; matrix products, arithmetic and copies ran while one was open for 1% -> 2% of each run, Pallas kernels for 5% -> 4%
where the time goes in v6:
time: 148 us; the launch traced here: 147 us
  starting transfers between devices  84.6 us (57%)
  waiting for transfers between devices  20.7 us (14%)
  Pallas kernels  20.5 us (14%)
  blocking collectives  13.6 us (9%)
  local copies, waits for them, and re-layouts  4.48 us (3%)
  other arithmetic  2.23 us (2%)
    ppermute x9, starting transfers between devices, swap(): return lax.ppermute(array, axis, [(i, i ^ flip) for i in range(size)])  52.7 us
    all_to_all x1, starting transfers between devices, body(): lax.all_to_all(jnp.broadcast_to(w, (NZ,) + w.shape[1:]), ('zl', 'zh'), 0, 0)  15.2 us
    ppermute x9, waiting for transfers between devices, swap(): return lax.ppermute(array, axis, [(i, i ^ flip) for i in range(size)])  11.9 us
    all_to_all x1, blocking collectives, body(): back = lax.all_to_all(back, 'y', 0, 0)  11.3 us
    pallas_call x1, Pallas kernels, attention(): pl.pallas_call(main_kernel, in_specs=[smem] + [vmem] * 7, out_specs=[vmem...  9.1 us
    all_to_all x1, starting transfers between devices, body(): parts = lax.all_to_all(parts, ('y', 'x'), 0, 0)  7.2 us
    all_to_all x1, starting transfers between devices, body(): dw = lax.all_to_all(dw, ('zl', 'zh'), 0, 0)  4.89 us
    all_to_all x1, starting transfers between devices, body(): msg = lax.all_to_all(msg, 'y', 0, 0)  4.6 us
  transfers between devices with their start and end apart: 13, of which 8 were waited for; matrix products, arithmetic and copies ran while one was open for 2% of the time, Pallas kernels for 4%

profile of v6, /device:TPU:32, one launch (start us, length us, event | category | flops | bytes accessed | tf_op | source)
XLA Modules:
  0.0 147.0 jit_solution(15249289300780441154)
XLA Ops:
  0.6 2.4 %pack.1 = (bf16[4,1120,128]{2,1,0:T(8,128)(2,1)}, bf16[784,128]{1,0:T(8,128)(2,1)}) custom-call(bf16[128,1024]{1,0:T(8,128)(2,1)} %bitcast.17, bf16[128,1024]{1,0:T(8,128)(2,1)} %bitcast.18, bf16[128,256]{1,0:T(8,128)(2,1)} %bitcast.20, bf16[128,512]{1,0:T(8,128)(2,1)} %bitcast.19, bf16[4,768]{1,0:T(4,128)(2,1)} %wk_ref.1, bf16[4,1024]{1,0:T(4,128)(2,1)} %wv_ref.1, ...), custom_call_target="tpu_custom_call" | custom-call | tf_op jit(solution)/shard_map/pack/pallas_call | solution.py:76
  3.0 0.0 copy-start.10
  3.0 4.6 %all-to-all-start = ((bf16[4,1120,128]{2,1,0:T(8,128)(2,1)}), bf16[4,1120,128]{2,1,0:T(8,128)(2,1)S(1)}, u32[]{:S(2)}, u32[]{:S(2)}) async-start(bf16[4,1120,128]{2,1,0:T(8,128)(2,1)} %get-tuple-element.28), calls=%async_computation | async-start | bytes 2293760 | tf_op jit(solution)/shard_map/all_to_all | solution.py:383
  7.6 0.0 copy-done.10
  7.6 14.8 %collective-permute-start = (bf16[784,128]{1,0:T(8,128)(2,1)S(1)}, bf16[784,128]{1,0:T(8,128)(2,1)S(1)}, u32[]{:S(2)}, u32[]{:S(2)}) collective-permute-start(bf16[784,128]{1,0:T(8,128)(2,1)S(1)} %copy-done.10), channel_id=1, source_target_pairs={{0,16},{16,0},{1,17},{17,1},{2,18},{18,2},{3,19},{19,3},{4,20},{20... | collective-permute-start | bytes 602120 | tf_op jit(solution)/shard_map/ppermute | solution.py:375
  22.4 0.7 pad_add_fusion.where_ref
  23.1 0.7 all-to-all-done.msg_ref
  23.8 0.0 copy-start
  23.8 0.8 broadcast_in_dim.17
  24.6 15.2 %all-to-all-start.1 = ((bf16[16,64,128]{2,1,0:T(8,128)(2,1)}), bf16[16,64,128]{2,1,0:T(8,128)(2,1)S(1)}, u32[]{:S(2)}, u32[]{:S(2)}) async-start(bf16[16,64,128]{2,1,0:T(8,128)(2,1)} %broadcast_in_dim.17), calls=%async_computation.1 | async-start | bytes 524288 | tf_op jit(solution)/shard_map/all_to_all | solution.py:386
  39.8 0.0 collective-permute-done.key_ref
  39.8 0.0 copy-start.11
  39.9 0.7 copy-done.11
  40.5 1.8 %relay.1 = (bf16[592,128]{1,0:T(8,128)(2,1)}, bf16[592,128]{1,0:T(8,128)(2,1)}, bf16[592,128]{1,0:T(8,128)(2,1)}, bf16[592,128]{1,0:T(8,128)(2,1)}) custom-call(s32[4]{0:T(128)} %pad_add_fusion.where_ref, bf16[784,128]{1,0:T(8,128)(2,1)} %copy-done.11), custom_call_target="tpu_custom_call" | custom-call | flops 49999998976 | bytes 150000000 | tf_op jit(solution)/shard_map/relay/pallas_call | solution.py:96
  42.3 0.0 copy-done
  42.3 3.0 %collective-permute-start.1 = (bf16[592,128]{1,0:T(8,128)(2,1)}, bf16[592,128]{1,0:T(8,128)(2,1)S(1)}, u32[]{:S(2)}, u32[]{:S(2)}) collective-permute-start(bf16[592,128]{1,0:T(8,128)(2,1)} %get-tuple-element.31), channel_id=1, source_target_pairs={{0,4},{4,0},{8,12},{12,8},{1,5},{5,1},{9,13},{13,9},{2,6},{6,2},{1... | collective-permute-start | bytes 454664 | tf_op jit(solution)/shard_map/ppermute | solution.py:375
  45.3 5.6 %collective-permute-start.2 = (bf16[592,128]{1,0:T(8,128)(2,1)}, bf16[592,128]{1,0:T(8,128)(2,1)S(1)}, u32[]{:S(2)}, u32[]{:S(2)}) collective-permute-start(bf16[592,128]{1,0:T(8,128)(2,1)} %get-tuple-element.32), channel_id=1, source_target_pairs={{0,8},{4,12},{8,0},{12,4},{1,9},{5,13},{9,1},{13,5},{2,10},{6,14},... | collective-permute-start | bytes 454664 | tf_op jit(solution)/shard_map/ppermute | solution.py:375
  50.9 2.5 %collective-permute-start.3 = (bf16[592,128]{1,0:T(8,128)(2,1)}, bf16[592,128]{1,0:T(8,128)(2,1)S(1)}, u32[]{:S(2)}, u32[]{:S(2)}) collective-permute-start(bf16[592,128]{1,0:T(8,128)(2,1)} %get-tuple-element.33), channel_id=1, source_target_pairs={{0,12},{4,8},{8,4},{12,0},{1,13},{5,9},{9,5},{13,1},{2,14},{6,10},... | collective-permute-start | bytes 454664 | tf_op jit(solution)/shard_map/ppermute | solution.py:375
  53.4 2.3 %all-to-all-done.1 = bf16[16,64,128]{2,1,0:T(8,128)(2,1)S(1)} async-done(((bf16[16,64,128]{2,1,0:T(8,128)(2,1)}), bf16[16,64,128]{2,1,0:T(8,128)(2,1)S(1)}, u32[]{:S(2)}, u32[]{:S(2)}) %all-to-all-start.1) | async-done | bytes 262176 | tf_op jit(solution)/shard_map/all_to_all | solution.py:386
  55.7 2.3 %all-gather = bf16[32,64,128]{2,1,0:T(8,128)(2,1)} all-gather(bf16[16,64,128]{2,1,0:T(8,128)(2,1)S(1)} %all-to-all-done.1), channel_id=2, replica_groups=mesh['zl'=8,'core'=2,'zh'=2,'y'=4,'x'=4] {'core'}, dimensions={0}, use_global_device_ids=true | all-gather | bytes 786432 | tf_op jit(solution)/shard_map/all_gather | solution.py:389
  58.0 0.0 collective-permute-done.1.key1_ref
  58.0 0.0 copy-start.4
  58.0 0.0 collective-permute-done.2.key2_ref
  58.0 0.0 copy-start.5
  58.0 1.4 collective-permute-done.3.key3_ref
  59.4 0.0 copy-start.6
  59.4 0.0 copy-done.4
  59.4 0.0 copy-done.5
  59.4 0.7 copy-done.6
  60.1 9.1 %attention_backward.1 = (bf16[16,256,128]{2,1,0:T(8,128)(2,1)}, bf16[4,256,128]{2,1,0:T(8,128)(2,1)}, bf16[4,64,128]{2,1,0:T(8,128)(2,1)}, bf16[4,64,128]{2,1,0:...) custom-call(s32[4]{0:T(128)} %pad_add_fusion.where_ref, s32[8,16]{1,0:T(8,128)} %freq_ref.1, ...), custom_call_target="tpu_custom_call" | custom-call | tf_op jit(solution)/shard_map/attention_backward/pallas_call | solution.py:237
  69.2 0.0 copy-start.9
  69.2 0.0 copy-start.12
  69.2 0.0 copy-start.3
  69.2 7.2 %all-to-all-start.2 = ((bf16[16,256,128]{2,1,0:T(8,128)(2,1)}), bf16[16,256,128]{2,1,0:T(8,128)(2,1)S(1)}, u32[]{:S(2)}, u32[]{:S(2)}) async-start(bf16[16,256,128]{2,1,0:T(8,128)(2,1)} %get-tuple-element.35), calls=%async_computation.2 | async-start | bytes 2097152 | tf_op jit(solution)/shard_map/all_to_all | solution.py:394
  76.4 0.0 copy-done.9
  76.4 1.9 %collective-permute-start.4 = (bf16[16,16,512]{2,1,0:T(8,128)(2,1)S(1)}, bf16[16,16,512]{2,1,0:T(8,128)(2,1)S(1)}, u32[]{:S(2)}, u32[]{:S(2)}) collective-permute-start(bf16[16,16,512]{2,1,0:T(8,128)(2,1)S(1)} %copy-done.9), channel_id=1, source_target_pairs={{0,32},{32,0},{1,33},{33,1},{2,34},{34,2},{3,35},{35,3},{4,36},{36... | collective-permute-start | bytes 786440 | tf_op jit(solution)/shard_map/ppermute | solution.py:375
  78.3 0.0 copy-done.12
  78.4 11.3 %collective-permute-start.6 = (bf16[4,64,128]{2,1,0:T(8,128)(2,1)S(1)}, bf16[4,64,128]{2,1,0:T(8,128)(2,1)S(1)}, u32[]{:S(2)}, u32[]{:S(2)}) collective-permute-start(bf16[4,64,128]{2,1,0:T(8,128)(2,1)S(1)} %copy-done.12), channel_id=1, source_target_pairs={{0,16},{16,0},{1,17},{17,1},{2,18},{18,2},{3,19},{19,3},{4,20},{20... | collective-permute-start | bytes 196616 | tf_op jit(solution)/shard_map/ppermute | solution.py:375
  89.6 0.0 collective-permute-done.4
  89.6 0.0 copy-done.3
  89.7 0.8 add_convert_fusion.dw_ref
  90.5 3.8 %all-to-all-done.2.parts_ref = bf16[16,256,128]{2,1,0:T(8,128)(2,1)S(1)} async-done(((bf16[16,256,128]{2,1,0:T(8,128)(2,1)}), bf16[16,256,128]{2,1,0:T(8,128)(2,1)S(1)}, u32[]{:S(2)}, u32[]{:S(2)}) %all-to-all-start.2) | async-done | bytes 1048608 | tf_op jit(solution)/shard_map/all_to_all | solution.py:394
  94.2 1.0 copy-done.1
  95.2 2.0 %fold.1 = (f32[128,128]{1,0:T(8,128)}, bf16[128,128]{1,0:T(8,128)(2,1)}, bf16[16,16,512]{2,1,0:T(8,128)(2,1)}) custom-call(bf16[16,256,128]{2,1,0:T(8,128)(2,1)} %copy-done.1, bf16[16,16,512]{2,1,0:T(8,128)(2,1)} %add_convert_fusion.dw_ref), custom_call_target="tpu_custom_call", output_to_operand_aliasing={{2}: (1, {})} | custom-call | tf_op jit(solution)/shard_map/fold/pallas_call | solution.py:280
  97.2 9.9 %collective-permute-start.5 = (bf16[128,128]{1,0:T(8,128)(2,1)}, bf16[128,128]{1,0:T(8,128)(2,1)S(1)}, u32[]{:S(2)}, u32[]{:S(2)}) collective-permute-start(bf16[128,128]{1,0:T(8,128)(2,1)} %get-tuple-element.39), channel_id=1, source_target_pairs={{0,16},{16,0},{1,17},{17,1},{2,18},{18,2},{3,19},{19,3},{4,20},{20... | collective-permute-start | bytes 98312 | tf_op jit(solution)/shard_map/ppermute | solution.py:375
  107.0 4.9 %all-to-all-start.3 = ((bf16[16,16,512]{2,1,0:T(8,128)(2,1)}), bf16[16,16,512]{2,1,0:T(8,128)(2,1)S(1)}, u32[]{:S(2)}, u32[]{:S(2)}) async-start(bf16[16,16,512]{2,1,0:T(8,128)(2,1)} %get-tuple-element.43), calls=%async_computation.3 | async-start | bytes 524288 | tf_op jit(solution)/shard_map/all_to_all | solution.py:398
  111.9 0.0 collective-permute-done.6.kr1_ref
  111.9 0.0 copy-start.13
  112.0 0.9 collective-permute-done.5.other_ref
  112.9 0.0 copy-done.13
  112.9 0.6 copy-done.14
  113.5 1.6 %merge.1 = (bf16[128,128]{1,0:T(8,128)(2,1)}, bf16[4,64,128]{2,1,0:T(8,128)(2,1)}) custom-call(f32[128,128]{1,0:T(8,128)} %get-tuple-element.38.own_ref, bf16[128,128]{1,0:T(8,128)(2,1)} %copy-done.14, bf16[4,64,128]{2,1,0:T(8,128)(2,1)} %get-tuple-element.40.kr0_ref, bf16[4,64,128]{2,1,0:T(8,128)(2,1)} %copy-done.13), custom_call_target="tpu_custom_call" | custom-call | flops 49999998976 | bytes 150000000 | tf_op jit(solution)/shard_map/merge/pallas_call | solution.py:300
  115.1 1.9 %collective-permute-start.7 = (bf16[128,128]{1,0:T(8,128)(2,1)}, bf16[128,128]{1,0:T(8,128)(2,1)S(1)}, u32[]{:S(2)}, u32[]{:S(2)}) collective-permute-start(bf16[128,128]{1,0:T(8,128)(2,1)} %get-tuple-element.44.q0_ref), channel_id=1, source_target_pairs={{0,1},{1,0},{2,3},{3,2},{4,5},{5,4},{6,7},{7,6},{8,9},{9,8},{10,11... | collective-permute-start | bytes 98312 | tf_op jit(solution)/shard_map/ppermute | solution.py:375
  117.0 4.1 %collective-permute-done.7.q1_ref = bf16[128,128]{1,0:T(8,128)(2,1)S(1)} collective-permute-done((bf16[128,128]{1,0:T(8,128)(2,1)}, bf16[128,128]{1,0:T(8,128)(2,1)S(1)}, u32[]{:S(2)}, u32[]{:S(2)}) %collective-permute-start.7) | collective-permute-done | bytes 32800 | tf_op jit(solution)/shard_map/ppermute | solution.py:375
  121.1 0.8 pad_maximum_fusion
  121.8 1.9 %collective-permute-start.8 = (bf16[256,128]{1,0:T(8,128)(2,1)S(1)}, bf16[256,128]{1,0:T(8,128)(2,1)S(1)}, u32[]{:S(2)}, u32[]{:S(2)}) collective-permute-start(bf16[256,128]{1,0:T(8,128)(2,1)S(1)} %pad_maximum_fusion), channel_id=1, source_target_pairs={{0,3},{1,2},{2,1},{3,0},{4,7},{5,6},{6,5},{7,4},{8,11},{9,10},{10,... | collective-permute-start | bytes 196616 | tf_op jit(solution)/shard_map/ppermute | solution.py:375
  123.8 5.4 %collective-permute-done.8.pair_ref = bf16[256,128]{1,0:T(8,128)(2,1)S(1)} collective-permute-done((bf16[256,128]{1,0:T(8,128)(2,1)S(1)}, bf16[256,128]{1,0:T(8,128)(2,1)S(1)}, u32[]{:S(2)}, u32[]{:S(2)}) %collective-permute-start.8) | collective-permute-done | bytes 65568 | tf_op jit(solution)/shard_map/ppermute | solution.py:375
  129.2 2.1 %all-to-all-done.3.dw_ref = bf16[16,16,512]{2,1,0:T(8,128)(2,1)S(1)} async-done(((bf16[16,16,512]{2,1,0:T(8,128)(2,1)}), bf16[16,16,512]{2,1,0:T(8,128)(2,1)S(1)}, u32[]{:S(2)}, u32[]{:S(2)}) %all-to-all-start.3) | async-done | bytes 262176 | tf_op jit(solution)/shard_map/all_to_all | solution.py:398
  131.3 0.0 copy-done.7
  131.3 0.0 copy-done.8
  131.4 0.7 copy-done.2
  132.0 1.9 %combine.1 = (bf16[4,336,128]{2,1,0:T(8,128)(2,1)}, bf16[128,512]{1,0:T(8,128)(2,1)}) custom-call(s32[4]{0:T(128)} %pad_add_fusion.where_ref, bf16[4,256,128]{2,1,0:T(8,128)(2,1)} %get-tuple-element.34.dq_ref, bf16[4,64,128]{2,1,0:T(8,128)(2,1)} %get-tuple-element.42.kr_ref, bf16[16,16,512]{2,1,0:T(8,128)(2,1)} %copy-done.2, ...), custom_call_target="tpu_custom_call" | custom-call | tf_op jit(solution)/shard_map/combine/pallas_call | solution.py:332
  134.0 11.3 %all_to_all.25.msg_ref = bf16[4,336,128]{2,1,0:T(8,128)(2,1)} all-to-all(bf16[4,336,128]{2,1,0:T(8,128)(2,1)} %get-tuple-element.45), channel_id=1, replica_groups=mesh['zl'=8,'core'=2,'zh'=2,'y'=4,'x'=4] {'y'}, dimensions={0} | all-to-all | bytes 688128 | tf_op jit(solution)/shard_map/all_to_all | solution.py:403
  145.2 1.8 %unpack.1 = (bf16[128,1024]{1,0:T(8,128)(2,1)}, bf16[128,256]{1,0:T(8,128)(2,1)}, bf16[4,768]{1,0:T(4,128)(2,1)}, bf16[4,1024]{1,0:T(4,128)(2,1)}) custom-call(bf16[4,336,128]{2,1,0:T(8,128)(2,1)} %all_to_all.25.msg_ref), custom_call_target="tpu_custom_call" | custom-call | tf_op jit(solution)/shard_map/unpack/pallas_call | solution.py:362
  (7 shorter events, 0.0 us)
Async XLA Ops:
  3.0 4.6 %copy-start.10 = (bf16[784,128]{1,0:T(8,128)(2,1)S(1)}, bf16[784,128]{1,0:T(8,128)(2,1)}, u32[]{:S(2)}) copy-start(bf16[784,128]{1,0:T(8,128)(2,1)} %get-tuple-element.29) | copy-start | bytes 602116
  3.0 20.7 %all-to-all-start = ((bf16[4,1120,128]{2,1,0:T(8,128)(2,1)}), bf16[4,1120,128]{2,1,0:T(8,128)(2,1)S(1)}, u32[]{:S(2)}, u32[]{:S(2)}) async-start(bf16[4,1120,128]{2,1,0:T(8,128)(2,1)} %get-tuple-element.28), calls=%async_computation | async-start | bytes 2293760 | tf_op jit(solution)/shard_map/all_to_all | solution.py:383
  7.6 32.2 %collective-permute-start = (bf16[784,128]{1,0:T(8,128)(2,1)S(1)}, bf16[784,128]{1,0:T(8,128)(2,1)S(1)}, u32[]{:S(2)}, u32[]{:S(2)}) collective-permute-start(bf16[784,128]{1,0:T(8,128)(2,1)S(1)} %copy-done.10), channel_id=1, source_target_pairs={{0,16},{16,0},{1,17},{17,1},{2,18},{18,2},{3,19},{19,3},{4,20},{20... | collective-permute-start | bytes 602120 | tf_op jit(solution)/shard_map/ppermute | solution.py:375
  23.8 18.6 %copy-start = (bf16[4,1120,128]{2,1,0:T(8,128)(2,1)}, bf16[4,1120,128]{2,1,0:T(8,128)(2,1)S(1)}, u32[]{:S(2)}) copy-start(bf16[4,1120,128]{2,1,0:T(8,128)(2,1)S(1)} %all-to-all-done.msg_ref) | copy-start | bytes 3440644
  24.6 31.1 %all-to-all-start.1 = ((bf16[16,64,128]{2,1,0:T(8,128)(2,1)}), bf16[16,64,128]{2,1,0:T(8,128)(2,1)S(1)}, u32[]{:S(2)}, u32[]{:S(2)}) async-start(bf16[16,64,128]{2,1,0:T(8,128)(2,1)} %broadcast_in_dim.17), calls=%async_computation.1 | async-start | bytes 524288 | tf_op jit(solution)/shard_map/all_to_all | solution.py:386
  39.8 0.7 copy-start.11
  42.3 15.6 %collective-permute-start.1 = (bf16[592,128]{1,0:T(8,128)(2,1)}, bf16[592,128]{1,0:T(8,128)(2,1)S(1)}, u32[]{:S(2)}, u32[]{:S(2)}) collective-permute-start(bf16[592,128]{1,0:T(8,128)(2,1)} %get-tuple-element.31), channel_id=1, source_target_pairs={{0,4},{4,0},{8,12},{12,8},{1,5},{5,1},{9,13},{13,9},{2,6},{6,2},{1... | collective-permute-start | bytes 454664 | tf_op jit(solution)/shard_map/ppermute | solution.py:375
  45.3 12.7 %collective-permute-start.2 = (bf16[592,128]{1,0:T(8,128)(2,1)}, bf16[592,128]{1,0:T(8,128)(2,1)S(1)}, u32[]{:S(2)}, u32[]{:S(2)}) collective-permute-start(bf16[592,128]{1,0:T(8,128)(2,1)} %get-tuple-element.32), channel_id=1, source_target_pairs={{0,8},{4,12},{8,0},{12,4},{1,9},{5,13},{9,1},{13,5},{2,10},{6,14},... | collective-permute-start | bytes 454664 | tf_op jit(solution)/shard_map/ppermute | solution.py:375
  50.9 8.5 %collective-permute-start.3 = (bf16[592,128]{1,0:T(8,128)(2,1)}, bf16[592,128]{1,0:T(8,128)(2,1)S(1)}, u32[]{:S(2)}, u32[]{:S(2)}) collective-permute-start(bf16[592,128]{1,0:T(8,128)(2,1)} %get-tuple-element.33), channel_id=1, source_target_pairs={{0,12},{4,8},{8,4},{12,0},{1,13},{5,9},{9,5},{13,1},{2,14},{6,10},... | collective-permute-start | bytes 454664 | tf_op jit(solution)/shard_map/ppermute | solution.py:375
  58.0 1.4 copy-start.4
  58.0 1.4 copy-start.5
  59.4 0.7 copy-start.6
  69.2 7.2 %copy-start.9 = (bf16[16,16,512]{2,1,0:T(8,128)(2,1)S(1)}, bf16[16,16,512]{2,1,0:T(8,128)(2,1)}, u32[]{:S(2)}) copy-start(bf16[16,16,512]{2,1,0:T(8,128)(2,1)} %get-tuple-element.37) | copy-start | bytes 786436
  69.2 9.2 %copy-start.12 = (bf16[4,64,128]{2,1,0:T(8,128)(2,1)S(1)}, bf16[4,64,128]{2,1,0:T(8,128)(2,1)}, u32[]{:S(2)}) copy-start(bf16[4,64,128]{2,1,0:T(8,128)(2,1)} %get-tuple-element.41) | copy-start | bytes 196612
  69.2 20.4 %copy-start.3 = (bf16[16,16,512]{2,1,0:T(8,128)(2,1)S(1)}, bf16[16,16,512]{2,1,0:T(8,128)(2,1)}, u32[]{:S(2)}) copy-start(bf16[16,16,512]{2,1,0:T(8,128)(2,1)} %get-tuple-element.36) | copy-start | bytes 786436
  69.2 25.0 %all-to-all-start.2 = ((bf16[16,256,128]{2,1,0:T(8,128)(2,1)}), bf16[16,256,128]{2,1,0:T(8,128)(2,1)S(1)}, u32[]{:S(2)}, u32[]{:S(2)}) async-start(bf16[16,256,128]{2,1,0:T(8,128)(2,1)} %get-tuple-element.35), calls=%async_computation.2 | async-start | bytes 2097152 | tf_op jit(solution)/shard_map/all_to_all | solution.py:394
  76.4 13.2 %collective-permute-start.4 = (bf16[16,16,512]{2,1,0:T(8,128)(2,1)S(1)}, bf16[16,16,512]{2,1,0:T(8,128)(2,1)S(1)}, u32[]{:S(2)}, u32[]{:S(2)}) collective-permute-start(bf16[16,16,512]{2,1,0:T(8,128)(2,1)S(1)} %copy-done.9), channel_id=1, source_target_pairs={{0,32},{32,0},{1,33},{33,1},{2,34},{34,2},{3,35},{35,3},{4,36},{36... | collective-permute-start | bytes 786440 | tf_op jit(solution)/shard_map/ppermute | solution.py:375
  78.4 33.6 %collective-permute-start.6 = (bf16[4,64,128]{2,1,0:T(8,128)(2,1)S(1)}, bf16[4,64,128]{2,1,0:T(8,128)(2,1)S(1)}, u32[]{:S(2)}, u32[]{:S(2)}) collective-permute-start(bf16[4,64,128]{2,1,0:T(8,128)(2,1)S(1)} %copy-done.12), channel_id=1, source_target_pairs={{0,16},{16,0},{1,17},{17,1},{2,18},{18,2},{3,19},{19,3},{4,20},{20... | collective-permute-start | bytes 196616 | tf_op jit(solution)/shard_map/ppermute | solution.py:375
  94.2 1.0 copy-start.1
  97.2 15.7 %collective-permute-start.5 = (bf16[128,128]{1,0:T(8,128)(2,1)}, bf16[128,128]{1,0:T(8,128)(2,1)S(1)}, u32[]{:S(2)}, u32[]{:S(2)}) collective-permute-start(bf16[128,128]{1,0:T(8,128)(2,1)} %get-tuple-element.39), channel_id=1, source_target_pairs={{0,16},{16,0},{1,17},{17,1},{2,18},{18,2},{3,19},{19,3},{4,20},{20... | collective-permute-start | bytes 98312 | tf_op jit(solution)/shard_map/ppermute | solution.py:375
  107.0 24.3 %all-to-all-start.3 = ((bf16[16,16,512]{2,1,0:T(8,128)(2,1)}), bf16[16,16,512]{2,1,0:T(8,128)(2,1)S(1)}, u32[]{:S(2)}, u32[]{:S(2)}) async-start(bf16[16,16,512]{2,1,0:T(8,128)(2,1)} %get-tuple-element.43), calls=%async_computation.3 | async-start | bytes 524288 | tf_op jit(solution)/shard_map/all_to_all | solution.py:398
  111.9 0.9 copy-start.13
  112.9 0.6 copy-start.14
  115.1 6.0 %collective-permute-start.7 = (bf16[128,128]{1,0:T(8,128)(2,1)}, bf16[128,128]{1,0:T(8,128)(2,1)S(1)}, u32[]{:S(2)}, u32[]{:S(2)}) collective-permute-start(bf16[128,128]{1,0:T(8,128)(2,1)} %get-tuple-element.44.q0_ref), channel_id=1, source_target_pairs={{0,1},{1,0},{2,3},{3,2},{4,5},{5,4},{6,7},{7,6},{8,9},{9,8},{10,11... | collective-permute-start | bytes 98312 | tf_op jit(solution)/shard_map/ppermute | solution.py:375
  121.1 10.3 %copy-start.7 = (bf16[128,128]{1,0:T(8,128)(2,1)}, bf16[128,128]{1,0:T(8,128)(2,1)S(1)}, u32[]{:S(2)}) copy-start(bf16[128,128]{1,0:T(8,128)(2,1)S(1)} %collective-permute-done.7.q1_ref) | copy-start | bytes 98308
  121.8 7.4 %collective-permute-start.8 = (bf16[256,128]{1,0:T(8,128)(2,1)S(1)}, bf16[256,128]{1,0:T(8,128)(2,1)S(1)}, u32[]{:S(2)}, u32[]{:S(2)}) collective-permute-start(bf16[256,128]{1,0:T(8,128)(2,1)S(1)} %pad_maximum_fusion), channel_id=1, source_target_pairs={{0,3},{1,2},{2,1},{3,0},{4,7},{5,6},{6,5},{7,4},{8,11},{9,10},{10,... | collective-permute-start | bytes 196616 | tf_op jit(solution)/shard_map/ppermute | solution.py:375
  129.2 2.2 %copy-start.8 = (bf16[256,128]{1,0:T(8,128)(2,1)}, bf16[256,128]{1,0:T(8,128)(2,1)S(1)}, u32[]{:S(2)}) copy-start(bf16[256,128]{1,0:T(8,128)(2,1)S(1)} %collective-permute-done.8.pair_ref) | copy-start | bytes 196612
  131.3 0.7 copy-start.2

commit v7 on v6

--- a/solution.py
+++ b/solution.py
@@ -224,7 +224,7 @@
                 ]
     dw_s[...] = dot(lat_s[...], dkv, ((0,), (0,)))
     for z in range(NZ):
-        base = (z // 2) * CORE * 32 + (z % 2) * 16
+        base = (z % ZL) * CORE * 32 + (z // ZL) * 16
         own = pl.ds(pl.multiple_of(base + core * 32, 16), 16)
         other = pl.ds(pl.multiple_of(base + (1 - core) * 32, 16), 16)
         dw_own_ref[z] = dw_s[own, :].astype(bf16)
@@ -395,7 +395,7 @@
     lat_own, other, dw = fold(parts, dw)
     other = swap(other, "zh", 2, 1)
     kr_other = swap(kr_other, "zh", 2, 1)
-    dw = lax.all_to_all(dw, ("zl", "zh"), 0, 0)
+    dw = lax.all_to_all(dw, ("zh", "zl"), 0, 0)
     quarter, kr = merge(lat_own, other, kr_own, kr_other)
     next_quarter = swap(quarter, "x", TEN, 1)
     pair = swap(jnp.concatenate([quarter, next_quarter], 0), "x", TEN, 3)

time: 148 us -> 146 us (0.986)
  waiting for transfers between devices: 20.7 us -> 19.1 us
    all_to_all x1, waiting for transfers between devices: 2.14 us -> 0.53 us  [body(): dw = lax.all_to_all(dw, ('zh', 'zl'), 0, 0)]
where the time goes in v7:
time: 146 us; the launch traced here: 145 us
  starting transfers between devices  84.6 us (58%)
  Pallas kernels  20.5 us (14%)
  waiting for transfers between devices  19.1 us (13%)
  blocking collectives  13.6 us (9%)
  local copies, waits for them, and re-layouts  4.48 us (3%)
  other arithmetic  2.23 us (2%)
    ppermute x9, starting transfers between devices, swap(): return lax.ppermute(array, axis, [(i, i ^ flip) for i in range(size)])  52.7 us
    all_to_all x1, starting transfers between devices, body(): lax.all_to_all(jnp.broadcast_to(w, (NZ,) + w.shape[1:]), ('zl', 'zh'), 0, 0)  15.2 us
    ppermute x9, waiting for transfers between devices, swap(): return lax.ppermute(array, axis, [(i, i ^ flip) for i in range(size)])  11.9 us
    all_to_all x1, blocking collectives, body(): back = lax.all_to_all(back, 'y', 0, 0)  11.3 us
    pallas_call x1, Pallas kernels, attention(): pl.pallas_call(main_kernel, in_specs=[smem] + [vmem] * 7, out_specs=[vmem...  9.1 us
    all_to_all x1, starting transfers between devices, body(): parts = lax.all_to_all(parts, ('y', 'x'), 0, 0)  7.2 us
    all_to_all x1, starting transfers between devices, body(): dw = lax.all_to_all(dw, ('zh', 'zl'), 0, 0)  4.89 us
    all_to_all x1, starting transfers between devices, body(): msg = lax.all_to_all(msg, 'y', 0, 0)  4.6 us
  transfers between devices with their start and end apart: 13, of which 8 were waited for; matrix products, arithmetic and copies ran while one was open for 2% of the time, Pallas kernels for 4%

profile of v7, /device:TPU:32, one launch (start us, length us, event | category | flops | bytes accessed | tf_op | source)
XLA Modules:
  0.0 145.4 jit_solution(14164038384312707806)
XLA Ops:
  0.6 2.4 %pack.1 = (bf16[4,1120,128]{2,1,0:T(8,128)(2,1)}, bf16[784,128]{1,0:T(8,128)(2,1)}) custom-call(bf16[128,1024]{1,0:T(8,128)(2,1)} %bitcast.17, bf16[128,1024]{1,0:T(8,128)(2,1)} %bitcast.18, bf16[128,256]{1,0:T(8,128)(2,1)} %bitcast.20, bf16[128,512]{1,0:T(8,128)(2,1)} %bitcast.19, bf16[4,768]{1,0:T(4,128)(2,1)} %wk_ref.1, bf16[4,1024]{1,0:T(4,128)(2,1)} %wv_ref.1, ...), custom_call_target="tpu_custom_call" | custom-call | tf_op jit(solution)/shard_map/pack/pallas_call | solution.py:76
  3.0 0.0 copy-start.10
  3.0 4.6 %all-to-all-start = ((bf16[4,1120,128]{2,1,0:T(8,128)(2,1)}), bf16[4,1120,128]{2,1,0:T(8,128)(2,1)S(1)}, u32[]{:S(2)}, u32[]{:S(2)}) async-start(bf16[4,1120,128]{2,1,0:T(8,128)(2,1)} %get-tuple-element.28), calls=%async_computation | async-start | bytes 2293760 | tf_op jit(solution)/shard_map/all_to_all | solution.py:383
  7.6 0.0 copy-done.10
  7.6 14.8 %collective-permute-start = (bf16[784,128]{1,0:T(8,128)(2,1)S(1)}, bf16[784,128]{1,0:T(8,128)(2,1)S(1)}, u32[]{:S(2)}, u32[]{:S(2)}) collective-permute-start(bf16[784,128]{1,0:T(8,128)(2,1)S(1)} %copy-done.10), channel_id=1, source_target_pairs={{0,16},{16,0},{1,17},{17,1},{2,18},{18,2},{3,19},{19,3},{4,20},{20... | collective-permute-start | bytes 602120 | tf_op jit(solution)/shard_map/ppermute | solution.py:375
  22.4 0.7 pad_add_fusion.where_ref
  23.1 0.7 all-to-all-done.msg_ref
  23.8 0.0 copy-start
  23.8 0.8 broadcast_in_dim.17
  24.6 15.2 %all-to-all-start.1 = ((bf16[16,64,128]{2,1,0:T(8,128)(2,1)}), bf16[16,64,128]{2,1,0:T(8,128)(2,1)S(1)}, u32[]{:S(2)}, u32[]{:S(2)}) async-start(bf16[16,64,128]{2,1,0:T(8,128)(2,1)} %broadcast_in_dim.17), calls=%async_computation.1 | async-start | bytes 524288 | tf_op jit(solution)/shard_map/all_to_all | solution.py:386
  39.8 0.0 collective-permute-done.key_ref
  39.8 0.0 copy-start.11
  39.9 0.7 copy-done.11
  40.5 1.8 %relay.1 = (bf16[592,128]{1,0:T(8,128)(2,1)}, bf16[592,128]{1,0:T(8,128)(2,1)}, bf16[592,128]{1,0:T(8,128)(2,1)}, bf16[592,128]{1,0:T(8,128)(2,1)}) custom-call(s32[4]{0:T(128)} %pad_add_fusion.where_ref, bf16[784,128]{1,0:T(8,128)(2,1)} %copy-done.11), custom_call_target="tpu_custom_call" | custom-call | flops 49999998976 | bytes 150000000 | tf_op jit(solution)/shard_map/relay/pallas_call | solution.py:96
  42.3 0.0 copy-done
  42.3 3.0 %collective-permute-start.1 = (bf16[592,128]{1,0:T(8,128)(2,1)}, bf16[592,128]{1,0:T(8,128)(2,1)S(1)}, u32[]{:S(2)}, u32[]{:S(2)}) collective-permute-start(bf16[592,128]{1,0:T(8,128)(2,1)} %get-tuple-element.31), channel_id=1, source_target_pairs={{0,4},{4,0},{8,12},{12,8},{1,5},{5,1},{9,13},{13,9},{2,6},{6,2},{1... | collective-permute-start | bytes 454664 | tf_op jit(solution)/shard_map/ppermute | solution.py:375
  45.3 5.6 %collective-permute-start.2 = (bf16[592,128]{1,0:T(8,128)(2,1)}, bf16[592,128]{1,0:T(8,128)(2,1)S(1)}, u32[]{:S(2)}, u32[]{:S(2)}) collective-permute-start(bf16[592,128]{1,0:T(8,128)(2,1)} %get-tuple-element.32), channel_id=1, source_target_pairs={{0,8},{4,12},{8,0},{12,4},{1,9},{5,13},{9,1},{13,5},{2,10},{6,14},... | collective-permute-start | bytes 454664 | tf_op jit(solution)/shard_map/ppermute | solution.py:375
  50.9 2.5 %collective-permute-start.3 = (bf16[592,128]{1,0:T(8,128)(2,1)}, bf16[592,128]{1,0:T(8,128)(2,1)S(1)}, u32[]{:S(2)}, u32[]{:S(2)}) collective-permute-start(bf16[592,128]{1,0:T(8,128)(2,1)} %get-tuple-element.33), channel_id=1, source_target_pairs={{0,12},{4,8},{8,4},{12,0},{1,13},{5,9},{9,5},{13,1},{2,14},{6,10},... | collective-permute-start | bytes 454664 | tf_op jit(solution)/shard_map/ppermute | solution.py:375
  53.4 2.3 %all-to-all-done.1 = bf16[16,64,128]{2,1,0:T(8,128)(2,1)S(1)} async-done(((bf16[16,64,128]{2,1,0:T(8,128)(2,1)}), bf16[16,64,128]{2,1,0:T(8,128)(2,1)S(1)}, u32[]{:S(2)}, u32[]{:S(2)}) %all-to-all-start.1) | async-done | bytes 262176 | tf_op jit(solution)/shard_map/all_to_all | solution.py:386
  55.7 2.3 %all-gather = bf16[32,64,128]{2,1,0:T(8,128)(2,1)} all-gather(bf16[16,64,128]{2,1,0:T(8,128)(2,1)S(1)} %all-to-all-done.1), channel_id=2, replica_groups=mesh['zl'=8,'core'=2,'zh'=2,'y'=4,'x'=4] {'core'}, dimensions={0}, use_global_device_ids=true | all-gather | bytes 786432 | tf_op jit(solution)/shard_map/all_gather | solution.py:389
  58.0 0.0 collective-permute-done.1.key1_ref
  58.0 0.0 copy-start.4
  58.0 0.0 collective-permute-done.2.key2_ref
  58.0 0.0 copy-start.5
  58.0 1.4 collective-permute-done.3.key3_ref
  59.4 0.0 copy-start.6
  59.4 0.0 copy-done.4
  59.4 0.0 copy-done.5
  59.4 0.7 copy-done.6
  60.1 9.1 %attention_backward.1 = (bf16[16,256,128]{2,1,0:T(8,128)(2,1)}, bf16[4,256,128]{2,1,0:T(8,128)(2,1)}, bf16[4,64,128]{2,1,0:T(8,128)(2,1)}, bf16[4,64,128]{2,1,0:...) custom-call(s32[4]{0:T(128)} %pad_add_fusion.where_ref, s32[8,16]{1,0:T(8,128)} %freq_ref.1, ...), custom_call_target="tpu_custom_call" | custom-call | tf_op jit(solution)/shard_map/attention_backward/pallas_call | solution.py:237
  69.2 0.0 copy-start.9
  69.2 0.0 copy-start.12
  69.2 0.0 copy-start.3
  69.2 7.2 %all-to-all-start.2 = ((bf16[16,256,128]{2,1,0:T(8,128)(2,1)}), bf16[16,256,128]{2,1,0:T(8,128)(2,1)S(1)}, u32[]{:S(2)}, u32[]{:S(2)}) async-start(bf16[16,256,128]{2,1,0:T(8,128)(2,1)} %get-tuple-element.35), calls=%async_computation.2 | async-start | bytes 2097152 | tf_op jit(solution)/shard_map/all_to_all | solution.py:394
  76.4 0.0 copy-done.9
  76.4 1.9 %collective-permute-start.4 = (bf16[16,16,512]{2,1,0:T(8,128)(2,1)S(1)}, bf16[16,16,512]{2,1,0:T(8,128)(2,1)S(1)}, u32[]{:S(2)}, u32[]{:S(2)}) collective-permute-start(bf16[16,16,512]{2,1,0:T(8,128)(2,1)S(1)} %copy-done.9), channel_id=1, source_target_pairs={{0,32},{32,0},{1,33},{33,1},{2,34},{34,2},{3,35},{35,3},{4,36},{36... | collective-permute-start | bytes 786440 | tf_op jit(solution)/shard_map/ppermute | solution.py:375
  78.3 0.0 copy-done.12
  78.4 11.3 %collective-permute-start.6 = (bf16[4,64,128]{2,1,0:T(8,128)(2,1)S(1)}, bf16[4,64,128]{2,1,0:T(8,128)(2,1)S(1)}, u32[]{:S(2)}, u32[]{:S(2)}) collective-permute-start(bf16[4,64,128]{2,1,0:T(8,128)(2,1)S(1)} %copy-done.12), channel_id=1, source_target_pairs={{0,16},{16,0},{1,17},{17,1},{2,18},{18,2},{3,19},{19,3},{4,20},{20... | collective-permute-start | bytes 196616 | tf_op jit(solution)/shard_map/ppermute | solution.py:375
  89.6 0.0 collective-permute-done.4
  89.6 0.0 copy-done.3
  89.7 0.8 add_convert_fusion.dw_ref
  90.5 3.8 %all-to-all-done.2.parts_ref = bf16[16,256,128]{2,1,0:T(8,128)(2,1)S(1)} async-done(((bf16[16,256,128]{2,1,0:T(8,128)(2,1)}), bf16[16,256,128]{2,1,0:T(8,128)(2,1)S(1)}, u32[]{:S(2)}, u32[]{:S(2)}) %all-to-all-start.2) | async-done | bytes 1048608 | tf_op jit(solution)/shard_map/all_to_all | solution.py:394
  94.2 1.0 copy-done.1
  95.2 2.0 %fold.1 = (f32[128,128]{1,0:T(8,128)}, bf16[128,128]{1,0:T(8,128)(2,1)}, bf16[16,16,512]{2,1,0:T(8,128)(2,1)}) custom-call(bf16[16,256,128]{2,1,0:T(8,128)(2,1)} %copy-done.1, bf16[16,16,512]{2,1,0:T(8,128)(2,1)} %add_convert_fusion.dw_ref), custom_call_target="tpu_custom_call", output_to_operand_aliasing={{2}: (1, {})} | custom-call | tf_op jit(solution)/shard_map/fold/pallas_call | solution.py:280
  97.2 9.9 %collective-permute-start.5 = (bf16[128,128]{1,0:T(8,128)(2,1)}, bf16[128,128]{1,0:T(8,128)(2,1)S(1)}, u32[]{:S(2)}, u32[]{:S(2)}) collective-permute-start(bf16[128,128]{1,0:T(8,128)(2,1)} %get-tuple-element.39), channel_id=1, source_target_pairs={{0,16},{16,0},{1,17},{17,1},{2,18},{18,2},{3,19},{19,3},{4,20},{20... | collective-permute-start | bytes 98312 | tf_op jit(solution)/shard_map/ppermute | solution.py:375
  107.0 4.9 %all-to-all-start.3 = ((bf16[16,16,512]{2,1,0:T(8,128)(2,1)}), bf16[16,16,512]{2,1,0:T(8,128)(2,1)S(1)}, u32[]{:S(2)}, u32[]{:S(2)}) async-start(bf16[16,16,512]{2,1,0:T(8,128)(2,1)} %get-tuple-element.43), calls=%async_computation.3 | async-start | bytes 524288 | tf_op jit(solution)/shard_map/all_to_all | solution.py:398
  111.9 0.0 collective-permute-done.6.kr1_ref
  111.9 0.0 copy-start.13
  112.0 0.9 collective-permute-done.5.other_ref
  112.9 0.0 copy-done.13
  112.9 0.6 copy-done.14
  113.5 1.6 %merge.1 = (bf16[128,128]{1,0:T(8,128)(2,1)}, bf16[4,64,128]{2,1,0:T(8,128)(2,1)}) custom-call(f32[128,128]{1,0:T(8,128)} %get-tuple-element.38.own_ref, bf16[128,128]{1,0:T(8,128)(2,1)} %copy-done.14, bf16[4,64,128]{2,1,0:T(8,128)(2,1)} %get-tuple-element.40.kr0_ref, bf16[4,64,128]{2,1,0:T(8,128)(2,1)} %copy-done.13), custom_call_target="tpu_custom_call" | custom-call | flops 49999998976 | bytes 150000000 | tf_op jit(solution)/shard_map/merge/pallas_call | solution.py:300
  115.1 1.9 %collective-permute-start.7 = (bf16[128,128]{1,0:T(8,128)(2,1)}, bf16[128,128]{1,0:T(8,128)(2,1)S(1)}, u32[]{:S(2)}, u32[]{:S(2)}) collective-permute-start(bf16[128,128]{1,0:T(8,128)(2,1)} %get-tuple-element.44.q0_ref), channel_id=1, source_target_pairs={{0,1},{1,0},{2,3},{3,2},{4,5},{5,4},{6,7},{7,6},{8,9},{9,8},{10,11... | collective-permute-start | bytes 98312 | tf_op jit(solution)/shard_map/ppermute | solution.py:375
  117.0 4.1 %collective-permute-done.7.q1_ref = bf16[128,128]{1,0:T(8,128)(2,1)S(1)} collective-permute-done((bf16[128,128]{1,0:T(8,128)(2,1)}, bf16[128,128]{1,0:T(8,128)(2,1)S(1)}, u32[]{:S(2)}, u32[]{:S(2)}) %collective-permute-start.7) | collective-permute-done | bytes 32800 | tf_op jit(solution)/shard_map/ppermute | solution.py:375
  121.1 0.8 pad_maximum_fusion
  121.8 1.9 %collective-permute-start.8 = (bf16[256,128]{1,0:T(8,128)(2,1)S(1)}, bf16[256,128]{1,0:T(8,128)(2,1)S(1)}, u32[]{:S(2)}, u32[]{:S(2)}) collective-permute-start(bf16[256,128]{1,0:T(8,128)(2,1)S(1)} %pad_maximum_fusion), channel_id=1, source_target_pairs={{0,3},{1,2},{2,1},{3,0},{4,7},{5,6},{6,5},{7,4},{8,11},{9,10},{10,... | collective-permute-start | bytes 196616 | tf_op jit(solution)/shard_map/ppermute | solution.py:375
  123.8 5.4 %collective-permute-done.8.pair_ref = bf16[256,128]{1,0:T(8,128)(2,1)S(1)} collective-permute-done((bf16[256,128]{1,0:T(8,128)(2,1)S(1)}, bf16[256,128]{1,0:T(8,128)(2,1)S(1)}, u32[]{:S(2)}, u32[]{:S(2)}) %collective-permute-start.8) | collective-permute-done | bytes 65568 | tf_op jit(solution)/shard_map/ppermute | solution.py:375
  129.2 0.5 all-to-all-done.3.dw_ref
  129.7 0.0 copy-done.7
  129.7 0.1 copy-done.8
  129.8 0.6 copy-done.2
  130.4 1.9 %combine.1 = (bf16[4,336,128]{2,1,0:T(8,128)(2,1)}, bf16[128,512]{1,0:T(8,128)(2,1)}) custom-call(s32[4]{0:T(128)} %pad_add_fusion.where_ref, bf16[4,256,128]{2,1,0:T(8,128)(2,1)} %get-tuple-element.34.dq_ref, bf16[4,64,128]{2,1,0:T(8,128)(2,1)} %get-tuple-element.42.kr_ref, bf16[16,16,512]{2,1,0:T(8,128)(2,1)} %copy-done.2, ...), custom_call_target="tpu_custom_call" | custom-call | tf_op jit(solution)/shard_map/combine/pallas_call | solution.py:332
  132.3 11.3 %all_to_all.25.msg_ref = bf16[4,336,128]{2,1,0:T(8,128)(2,1)} all-to-all(bf16[4,336,128]{2,1,0:T(8,128)(2,1)} %get-tuple-element.45), channel_id=1, replica_groups=mesh['zl'=8,'core'=2,'zh'=2,'y'=4,'x'=4] {'y'}, dimensions={0} | all-to-all | bytes 688128 | tf_op jit(solution)/shard_map/all_to_all | solution.py:403
  143.6 1.8 %unpack.1 = (bf16[128,1024]{1,0:T(8,128)(2,1)}, bf16[128,256]{1,0:T(8,128)(2,1)}, bf16[4,768]{1,0:T(4,128)(2,1)}, bf16[4,1024]{1,0:T(4,128)(2,1)}) custom-call(bf16[4,336,128]{2,1,0:T(8,128)(2,1)} %all_to_all.25.msg_ref), custom_call_target="tpu_custom_call" | custom-call | tf_op jit(solution)/shard_map/unpack/pallas_call | solution.py:362
  (7 shorter events, 0.0 us)
Async XLA Ops:
  3.0 4.6 %copy-start.10 = (bf16[784,128]{1,0:T(8,128)(2,1)S(1)}, bf16[784,128]{1,0:T(8,128)(2,1)}, u32[]{:S(2)}) copy-start(bf16[784,128]{1,0:T(8,128)(2,1)} %get-tuple-element.29) | copy-start | bytes 602116
  3.0 20.7 %all-to-all-start = ((bf16[4,1120,128]{2,1,0:T(8,128)(2,1)}), bf16[4,1120,128]{2,1,0:T(8,128)(2,1)S(1)}, u32[]{:S(2)}, u32[]{:S(2)}) async-start(bf16[4,1120,128]{2,1,0:T(8,128)(2,1)} %get-tuple-element.28), calls=%async_computation | async-start | bytes 2293760 | tf_op jit(solution)/shard_map/all_to_all | solution.py:383
  7.6 32.2 %collective-permute-start = (bf16[784,128]{1,0:T(8,128)(2,1)S(1)}, bf16[784,128]{1,0:T(8,128)(2,1)S(1)}, u32[]{:S(2)}, u32[]{:S(2)}) collective-permute-start(bf16[784,128]{1,0:T(8,128)(2,1)S(1)} %copy-done.10), channel_id=1, source_target_pairs={{0,16},{16,0},{1,17},{17,1},{2,18},{18,2},{3,19},{19,3},{4,20},{20... | collective-permute-start | bytes 602120 | tf_op jit(solution)/shard_map/ppermute | solution.py:375
  23.8 18.6 %copy-start = (bf16[4,1120,128]{2,1,0:T(8,128)(2,1)}, bf16[4,1120,128]{2,1,0:T(8,128)(2,1)S(1)}, u32[]{:S(2)}) copy-start(bf16[4,1120,128]{2,1,0:T(8,128)(2,1)S(1)} %all-to-all-done.msg_ref) | copy-start | bytes 3440644
  24.6 31.1 %all-to-all-start.1 = ((bf16[16,64,128]{2,1,0:T(8,128)(2,1)}), bf16[16,64,128]{2,1,0:T(8,128)(2,1)S(1)}, u32[]{:S(2)}, u32[]{:S(2)}) async-start(bf16[16,64,128]{2,1,0:T(8,128)(2,1)} %broadcast_in_dim.17), calls=%async_computation.1 | async-start | bytes 524288 | tf_op jit(solution)/shard_map/all_to_all | solution.py:386
  39.8 0.7 copy-start.11
  42.3 15.6 %collective-permute-start.1 = (bf16[592,128]{1,0:T(8,128)(2,1)}, bf16[592,128]{1,0:T(8,128)(2,1)S(1)}, u32[]{:S(2)}, u32[]{:S(2)}) collective-permute-start(bf16[592,128]{1,0:T(8,128)(2,1)} %get-tuple-element.31), channel_id=1, source_target_pairs={{0,4},{4,0},{8,12},{12,8},{1,5},{5,1},{9,13},{13,9},{2,6},{6,2},{1... | collective-permute-start | bytes 454664 | tf_op jit(solution)/shard_map/ppermute | solution.py:375
  45.3 12.7 %collective-permute-start.2 = (bf16[592,128]{1,0:T(8,128)(2,1)}, bf16[592,128]{1,0:T(8,128)(2,1)S(1)}, u32[]{:S(2)}, u32[]{:S(2)}) collective-permute-start(bf16[592,128]{1,0:T(8,128)(2,1)} %get-tuple-element.32), channel_id=1, source_target_pairs={{0,8},{4,12},{8,0},{12,4},{1,9},{5,13},{9,1},{13,5},{2,10},{6,14},... | collective-permute-start | bytes 454664 | tf_op jit(solution)/shard_map/ppermute | solution.py:375
  50.9 8.5 %collective-permute-start.3 = (bf16[592,128]{1,0:T(8,128)(2,1)}, bf16[592,128]{1,0:T(8,128)(2,1)S(1)}, u32[]{:S(2)}, u32[]{:S(2)}) collective-permute-start(bf16[592,128]{1,0:T(8,128)(2,1)} %get-tuple-element.33), channel_id=1, source_target_pairs={{0,12},{4,8},{8,4},{12,0},{1,13},{5,9},{9,5},{13,1},{2,14},{6,10},... | collective-permute-start | bytes 454664 | tf_op jit(solution)/shard_map/ppermute | solution.py:375
  58.0 1.4 copy-start.4
  58.0 1.4 copy-start.5
  59.4 0.7 copy-start.6
  69.2 7.2 %copy-start.9 = (bf16[16,16,512]{2,1,0:T(8,128)(2,1)S(1)}, bf16[16,16,512]{2,1,0:T(8,128)(2,1)}, u32[]{:S(2)}) copy-start(bf16[16,16,512]{2,1,0:T(8,128)(2,1)} %get-tuple-element.37) | copy-start | bytes 786436
  69.2 9.2 %copy-start.12 = (bf16[4,64,128]{2,1,0:T(8,128)(2,1)S(1)}, bf16[4,64,128]{2,1,0:T(8,128)(2,1)}, u32[]{:S(2)}) copy-start(bf16[4,64,128]{2,1,0:T(8,128)(2,1)} %get-tuple-element.41) | copy-start | bytes 196612
  69.2 20.4 %copy-start.3 = (bf16[16,16,512]{2,1,0:T(8,128)(2,1)S(1)}, bf16[16,16,512]{2,1,0:T(8,128)(2,1)}, u32[]{:S(2)}) copy-start(bf16[16,16,512]{2,1,0:T(8,128)(2,1)} %get-tuple-element.36) | copy-start | bytes 786436
  69.2 25.0 %all-to-all-start.2 = ((bf16[16,256,128]{2,1,0:T(8,128)(2,1)}), bf16[16,256,128]{2,1,0:T(8,128)(2,1)S(1)}, u32[]{:S(2)}, u32[]{:S(2)}) async-start(bf16[16,256,128]{2,1,0:T(8,128)(2,1)} %get-tuple-element.35), calls=%async_computation.2 | async-start | bytes 2097152 | tf_op jit(solution)/shard_map/all_to_all | solution.py:394
  76.4 13.2 %collective-permute-start.4 = (bf16[16,16,512]{2,1,0:T(8,128)(2,1)S(1)}, bf16[16,16,512]{2,1,0:T(8,128)(2,1)S(1)}, u32[]{:S(2)}, u32[]{:S(2)}) collective-permute-start(bf16[16,16,512]{2,1,0:T(8,128)(2,1)S(1)} %copy-done.9), channel_id=1, source_target_pairs={{0,32},{32,0},{1,33},{33,1},{2,34},{34,2},{3,35},{35,3},{4,36},{36... | collective-permute-start | bytes 786440 | tf_op jit(solution)/shard_map/ppermute | solution.py:375
  78.4 33.6 %collective-permute-start.6 = (bf16[4,64,128]{2,1,0:T(8,128)(2,1)S(1)}, bf16[4,64,128]{2,1,0:T(8,128)(2,1)S(1)}, u32[]{:S(2)}, u32[]{:S(2)}) collective-permute-start(bf16[4,64,128]{2,1,0:T(8,128)(2,1)S(1)} %copy-done.12), channel_id=1, source_target_pairs={{0,16},{16,0},{1,17},{17,1},{2,18},{18,2},{3,19},{19,3},{4,20},{20... | collective-permute-start | bytes 196616 | tf_op jit(solution)/shard_map/ppermute | solution.py:375
  94.2 1.0 copy-start.1
  97.2 15.7 %collective-permute-start.5 = (bf16[128,128]{1,0:T(8,128)(2,1)}, bf16[128,128]{1,0:T(8,128)(2,1)S(1)}, u32[]{:S(2)}, u32[]{:S(2)}) collective-permute-start(bf16[128,128]{1,0:T(8,128)(2,1)} %get-tuple-element.39), channel_id=1, source_target_pairs={{0,16},{16,0},{1,17},{17,1},{2,18},{18,2},{3,19},{19,3},{4,20},{20... | collective-permute-start | bytes 98312 | tf_op jit(solution)/shard_map/ppermute | solution.py:375
  107.0 22.7 %all-to-all-start.3 = ((bf16[16,16,512]{2,1,0:T(8,128)(2,1)}), bf16[16,16,512]{2,1,0:T(8,128)(2,1)S(1)}, u32[]{:S(2)}, u32[]{:S(2)}) async-start(bf16[16,16,512]{2,1,0:T(8,128)(2,1)} %get-tuple-element.43), calls=%async_computation.3 | async-start | bytes 524288 | tf_op jit(solution)/shard_map/all_to_all | solution.py:398
  111.9 0.9 copy-start.13
  112.9 0.6 copy-start.14
  115.1 6.0 %collective-permute-start.7 = (bf16[128,128]{1,0:T(8,128)(2,1)}, bf16[128,128]{1,0:T(8,128)(2,1)S(1)}, u32[]{:S(2)}, u32[]{:S(2)}) collective-permute-start(bf16[128,128]{1,0:T(8,128)(2,1)} %get-tuple-element.44.q0_ref), channel_id=1, source_target_pairs={{0,1},{1,0},{2,3},{3,2},{4,5},{5,4},{6,7},{7,6},{8,9},{9,8},{10,11... | collective-permute-start | bytes 98312 | tf_op jit(solution)/shard_map/ppermute | solution.py:375
  121.1 8.7 %copy-start.7 = (bf16[128,128]{1,0:T(8,128)(2,1)}, bf16[128,128]{1,0:T(8,128)(2,1)S(1)}, u32[]{:S(2)}) copy-start(bf16[128,128]{1,0:T(8,128)(2,1)S(1)} %collective-permute-done.7.q1_ref) | copy-start | bytes 98308
  121.8 7.4 %collective-permute-start.8 = (bf16[256,128]{1,0:T(8,128)(2,1)S(1)}, bf16[256,128]{1,0:T(8,128)(2,1)S(1)}, u32[]{:S(2)}, u32[]{:S(2)}) collective-permute-start(bf16[256,128]{1,0:T(8,128)(2,1)S(1)} %pad_maximum_fusion), channel_id=1, source_target_pairs={{0,3},{1,2},{2,1},{3,0},{4,7},{5,6},{6,5},{7,4},{8,11},{9,10},{10,... | collective-permute-start | bytes 196616 | tf_op jit(solution)/shard_map/ppermute | solution.py:375
  129.2 0.6 copy-start.8
  129.7 0.7 copy-start.2
